TPU v7x, 512 devices: a whole 4x4x16 slice. The times are simulated.
512 devices in a mesh: replica: 32 (over x, z_hi, core), fsdp: 16 (over z_lo, y).
Axes of the slice: x: 4, y: 4, z: 16 (z_hi: 4, z_lo: 4; z = z_hi * 4 + z_lo), core: 2. Of those that a mesh axis runs over, the one named last changes fastest.
Arguments:
- hidden: bfloat16 [32, 2048, 4608], P('replica', 'fsdp'), may hold values from -6 to 6
- queries: bfloat16 [32, 2048, 2048], P('replica', 'fsdp'), may hold values from -48 to 48
- values: bfloat16 [32, 2048, 1024], P('replica', 'fsdp'), may hold values from -6 to 6
- codes: bfloat16 [32, 4608, 1024], P('replica', 'fsdp'), may hold values from -6 to 6
- exponents: int32 [32, 4608, 8], P('replica', 'fsdp'), may hold values from -2 to 1
- base: bfloat16 [4608, 1024], P('fsdp'), may hold values from -1.5 to 1.5
- momentum: bfloat16 [4608, 1024], P('fsdp'), may hold values from -1.5 to 1.5
Outputs:
- blended: bfloat16 [32, 4608, 1024], P('replica', 'fsdp')
- attended: bfloat16 [32, 2048, 2048], P('replica', 'fsdp')
All inputs are finite; a program needn't handle non-finite values.
Results may differ from a plain program's by a relative error of at most 0.035.
Values may be sent and summed in bfloat16 or wider, within the bound.
No kernel may reach another device: no remote copies, remote signals or barrier semaphores. Data moves between devices by JAX's collectives and lax.ppermute only.
A program may use at most 64 MiB of HBM per device.

v0:
```python
import math

import jax
import jax.numpy as jnp
from jax import lax
from jax.sharding import PartitionSpec as P

D = 4608
HD = 128
QH = 16
KVH = 8
BLOCK = 128


momentum_rate = 0.9
outer_rate = 0.7
blend_share = 0.25
logit_cap = 50.0
query_scalar = 12.0


def dequantize(code_block, exponent_block):
    row_count = code_block.shape[0]
    col_count = code_block.shape[1]
    factor = jnp.exp2(exponent_block.astype(jnp.float32))
    grouped = code_block.astype(jnp.float32).reshape(row_count, col_count // BLOCK, BLOCK)
    return (grouped * factor[:, :, None]).reshape(row_count, col_count)


def outer_update(mean_delta, base_part, moment_part):
    moment_new = momentum_rate * moment_part.astype(jnp.float32) + mean_delta
    return (
        base_part.astype(jnp.float32) - outer_rate * (mean_delta + momentum_rate * moment_new)
    ).astype(jnp.bfloat16)


def widen_heads(block):
    row_count = block.shape[0]
    group_size = QH // KVH
    spread = jnp.broadcast_to(
        block.reshape(row_count, KVH, 1, HD), (row_count, KVH, group_size, HD)
    )
    return spread.reshape(row_count, QH * HD)


def attend_local(query_all, key_all, value_all):
    row_count = query_all.shape[0]
    local_heads = query_all.shape[1] // HD
    query_heads = query_all.reshape(row_count, local_heads, HD)
    key_heads = key_all.reshape(row_count, local_heads, HD)
    value_heads = value_all.reshape(row_count, local_heads, HD)
    stride_rows = min(512, row_count)
    position = jnp.arange(row_count)

    def block_rows(block_index):
        offset = block_index * stride_rows
        query_block = lax.dynamic_slice_in_dim(query_heads, offset, stride_rows, 0)
        scores = (
            jnp.einsum("qhd,khd->hqk", query_block, key_heads, preferred_element_type=jnp.float32)
            / query_scalar
        )
        capped = logit_cap * jnp.tanh(scores / logit_cap)
        rows_at = offset + jnp.arange(stride_rows)
        allowed = position[None, :] <= rows_at[:, None]
        weights = jnp.where(allowed[None], jnp.exp(capped), jnp.zeros_like(capped))
        totals = jnp.sum(weights, axis=2)
        mixed = jnp.einsum(
            "hqk,khd->qhd",
            weights.astype(jnp.bfloat16),
            value_heads,
            preferred_element_type=jnp.float32,
        )
        return (mixed / jnp.transpose(totals)[:, :, None]).astype(jnp.bfloat16)

    mixed_all = lax.map(block_rows, jnp.arange(row_count // stride_rows))
    return mixed_all.reshape(row_count, local_heads * HD)


def on_device(hidden, queries, values, codes, exponents, base, momentum):
    delta = dequantize(codes[0], exponents[0])
    replicas = lax.axis_size("replica")
    delta_total = lax.psum(delta.astype(jnp.bfloat16), "replica").astype(jnp.float32)
    outer_params = outer_update(delta_total / replicas, base, momentum)
    local_params = base.astype(jnp.float32) - delta
    mixed_params = (
        blend_share * local_params + (1.0 - blend_share) * outer_params.astype(jnp.float32)
    ).astype(jnp.bfloat16)
    rows_in = hidden[0]
    projected = jnp.dot(
        rows_in,
        lax.all_gather(mixed_params, "fsdp", axis=0, tiled=True),
        preferred_element_type=jnp.float32,
    )
    key_rows = (projected / math.sqrt(D)).astype(jnp.bfloat16)
    query_all, key_all, value_all = (
        lax.all_to_all(queries[0], "fsdp", split_axis=1, concat_axis=0, tiled=True),
        lax.all_to_all(widen_heads(key_rows), "fsdp", split_axis=1, concat_axis=0, tiled=True),
        lax.all_to_all(widen_heads(values[0]), "fsdp", split_axis=1, concat_axis=0, tiled=True),
    )
    mixed_heads = attend_local(query_all, key_all, value_all)
    attended = lax.all_to_all(mixed_heads, "fsdp", split_axis=0, concat_axis=1, tiled=True)
    return (mixed_params[None], attended[None])


def solution(mesh):
    placed = (
        P("replica", "fsdp", None),
        P("replica", "fsdp", None),
        P("replica", "fsdp", None),
        P("replica", "fsdp", None),
        P("replica", "fsdp", None),
        P("fsdp", None),
        P("fsdp", None),
    )
    return jax.shard_map(
        on_device,
        mesh=mesh,
        in_specs=placed,
        out_specs=(P("replica", "fsdp", None), P("replica", "fsdp", None)),
        check_vma=False,
    )
```

profile of v0, /device:TPU:1, one launch (start us, length us, event | category | flops | bytes accessed | tf_op | source)
XLA Modules:
  0.0 537.3 jit_solution(10162061577213985707)
XLA Ops:
  8.6 1.1 fusion.30
  9.8 339.5 %all-reduce.2.cloned.1.call-done = bf16[288,1024]{1,0:T(8,128)(2,1)} async-done(((bf16[288,1024]{1,0:T(8,128)(2,1)}), bf16[288,1024]{1,0:T(8,128)(2,1)}) %all-reduce.2.cloned.1.call-update) | async-done | bytes 589840 | tf_op jit(solution)/shard_map/psum | solution.py:82
  349.3 2.8 fusion.27
  352.2 1.0 copy.37
  353.2 0.9 broadcast_in_dim.39
  354.2 4.5 all-to-all-start.2
  358.6 1.0 copy.30
  359.6 10.6 %all-to-all-done.2 = bf16[128,16,128]{2,0,1:T(8,128)(2,1)S(1)} async-done(((bf16[128,16,128]{2,0,1:T(8,128)(2,1)}), bf16[128,16,128]{2,0,1:T(8,128)(2,1)S(1)}, u32[]{:S(2)}, u32[]{:S(2)}) %all-to-all-start.2) | async-done | bytes 524320 | tf_op jit(solution)/shard_map/all_to_all | solution.py:98
  370.2 18.9 %all-to-all-start = ((bf16[128,16,128]{0,2,1:T(8,128)(2,1)}), bf16[128,16,128]{0,2,1:T(8,128)(2,1)S(1)}, u32[]{:S(2)}, u32[]{:S(2)}) async-start(bf16[128,16,128]{0,2,1:T(8,128)(2,1)} %bitcast.3), calls=%async_computation | async-start | bytes 1048576 | tf_op jit(solution)/shard_map/all_to_all | solution.py:96
  389.2 85.3 %all-gather.2.cloned.1.call-done = bf16[4608,1024]{1,0:T(8,128)(2,1)} async-done(((bf16[288,1024]{1,0:T(8,128)(2,1)}), bf16[4608,1024]{1,0:T(8,128)(2,1)}) %all-gather.2.cloned.1.call-update) | async-done | bytes 9437200 | tf_op jit(solution)/shard_map/all_gather | solution.py:91
  474.5 6.3 %fusion.24 = bf16[1024,128]{1,0:T(8,128)(2,1)S(1)} fusion(bf16[4608,1024]{1,0:T(8,128)(2,1)} %all-gather.2.cloned.1.call-done, bf16[1,128,4608]{2,1,0:T(8,128)(2,1)S(1)} %copy-done), kind=kOutput, calls=%fused_computation.19 | convolution fusion | flops 1208221696 | bytes 10878976 | tf_op jit(solution)/shard_map/dot_general | solution.py:89
  481.9 4.4 all-to-all-start.1
  486.6 10.8 %all-to-all-done.1 = bf16[128,16,128]{2,0,1:T(8,128)(2,1)S(1)} async-done(((bf16[128,16,128]{2,0,1:T(8,128)(2,1)}), bf16[128,16,128]{2,0,1:T(8,128)(2,1)S(1)}, u32[]{:S(2)}, u32[]{:S(2)}) %all-to-all-start.1) | async-done | bytes 524320 | tf_op jit(solution)/shard_map/all_to_all | solution.py:97
  497.4 17.1 %while.13 = (s32[]{:T(128)}, bf16[4,512,1,128]{3,1,2,0:T(8,128)(2,1)}, s32[4]{0:T(128)S(1)}, bf16[2048,1,128]{2,0,1:T(8,128)(2,1)S(1)}, bf16[2048,1,128]{2,0,1:T...) while((s32[]{:T(128)}, ...), condition=%wide.region_3.4_spmd.clone, body=%wide.region_1.3_spmd.clone.sunk | while | flops 543293440 | bytes 5513895 | solution.py:75
  498.7 1.6 fusion.40
  500.3 1.4 fusion.41
  502.9 1.6 fusion.40
  504.6 1.4 fusion.41
  507.2 1.6 fusion.40
  508.9 1.4 fusion.41
  511.5 1.6 fusion.40
  513.1 1.4 fusion.41
  514.5 14.6 %all_to_all.64 = bf16[16,128,128]{2,1,0:T(8,128)(2,1)S(1)} all-to-all(bf16[16,128,128]{2,1,0:T(8,128)(2,1)} %bitcast.15), channel_id=1, replica_groups=mesh['replica'=32,'fsdp'=16] {'fsdp'}, dimensions={0} | all-to-all | bytes 1048576 | tf_op jit(solution)/shard_map/all_to_all | solution.py:101
  529.4 1.0 copy.35
  (31 shorter events, 5.6 us)
Async XLA Ops:
  7.2 467.3 %copy-start = (bf16[1,128,4608]{2,1,0:T(8,128)(2,1)S(1)}, bf16[1,128,4608]{2,1,0:T(8,128)(2,1)}, u32[]{:S(2)}) copy-start(bf16[1,128,4608]{2,1,0:T(8,128)(2,1)} %param.9) | copy-start | bytes 3538948
  7.2 1.4 copy-start.1
  7.2 342.1 %all-reduce.2.cloned.1.call-start = ((), (), s32[]{:S(2)}) async-start(), calls=%async_computation.4 | async-start | bytes 1179648 | tf_op jit(solution)/shard_map/psum | solution.py:82
  8.6 340.7 %copy-start.2 = (bf16[288,1024]{1,0:T(8,128)(2,1)S(1)}, bf16[288,1024]{1,0:T(8,128)(2,1)}, u32[]{:S(2)}) copy-start(bf16[288,1024]{1,0:T(8,128)(2,1)} %param.14) | copy-start | bytes 1769476
  9.7 464.7 %all-gather.2.cloned.1.call-start = ((), (), s32[]{:S(2)}) async-start(), calls=%async_computation.5 | async-start | bytes 10027008 | tf_op jit(solution)/shard_map/all_gather | solution.py:91
  353.2 5.4 %copy-start.3 = (bf16[1,128,2048]{2,1,0:T(8,128)(2,1)S(1)}, bf16[1,128,2048]{2,1,0:T(8,128)(2,1)}, u32[]{:S(2)}) copy-start(bf16[1,128,2048]{2,1,0:T(8,128)(2,1)} %param.10) | copy-start | bytes 1572868
  354.2 16.1 %all-to-all-start.2 = ((bf16[128,16,128]{2,0,1:T(8,128)(2,1)}), bf16[128,16,128]{2,0,1:T(8,128)(2,1)S(1)}, u32[]{:S(2)}, u32[]{:S(2)}) async-start(bf16[128,16,128]{2,0,1:T(8,128)(2,1)} %bitcast.12), calls=%async_computation.2 | async-start | bytes 1048576 | tf_op jit(solution)/shard_map/all_to_all | solution.py:98
  370.2 110.7 %all-to-all-start = ((bf16[128,16,128]{0,2,1:T(8,128)(2,1)}), bf16[128,16,128]{0,2,1:T(8,128)(2,1)S(1)}, u32[]{:S(2)}, u32[]{:S(2)}) async-start(bf16[128,16,128]{0,2,1:T(8,128)(2,1)} %bitcast.3), calls=%async_computation | async-start | bytes 1048576 | tf_op jit(solution)/shard_map/all_to_all | solution.py:96
  481.9 15.5 %all-to-all-start.1 = ((bf16[128,16,128]{2,0,1:T(8,128)(2,1)}), bf16[128,16,128]{2,0,1:T(8,128)(2,1)S(1)}, u32[]{:S(2)}, u32[]{:S(2)}) async-start(bf16[128,16,128]{2,0,1:T(8,128)(2,1)} %bitcast.9), calls=%async_computation.1 | async-start | bytes 1048576 | tf_op jit(solution)/shard_map/all_to_all | solution.py:97
Sparse Core Ops, SparseCore 0:
  11.5 337.7 all-reduce.1
  352.3 122.1 all-gather.1
where the time goes:
time: 547 us; the launch traced here: 537 us
  waiting for transfers between devices  446 us (82%)
  starting transfers between devices  27.8 us (5%)
  matrix products  18.4 us (3%)
  blocking collectives  14.6 us (3%)
  between operations  14.2 us (3%)
  local copies, waits for them, and re-layouts  8.55 us (2%)
    psum x1, waiting for transfers between devices, on_device(): lax.psum(delta.astype(jnp.bfloat16), 'replica').astype(jnp.float32)  340 us
    all_gather x1, waiting for transfers between devices, on_device(): lax.all_gather(mixed_params, 'fsdp', axis=0, tiled=True)  85.3 us
    all_to_all x1, starting transfers between devices, on_device(): lax.all_to_all(queries[0], 'fsdp', split_axis=1, concat_axis=0, tiled=True)  18.9 us
    all_to_all x1, blocking collectives, on_device(): lax.all_to_all(mixed_heads, 'fsdp', split_axis=0, concat_axis=1, tiled=True)  14.6 us
  transfers between devices with their start and end apart: 5, of which 4 were waited for; matrix products, arithmetic and copies ran while one was open for 2% of the time, Pallas kernels for 0%

commit v1 on v0

v1 whole, which is shorter than its diff:
```python
import math

import jax
import jax.numpy as jnp
from jax import lax
from jax.experimental import pallas as pl
from jax.experimental.pallas import tpu as pltpu
from jax.sharding import Mesh
from jax.sharding import PartitionSpec as P

D = 4608
HD = 128
QH = 16
KVH = 8
BLOCK = 128
KC = 1024
VMEM = pl.BlockSpec(memory_space=pltpu.VMEM)
SMEM = pl.BlockSpec(memory_space=pltpu.SMEM)

momentum_rate = 0.9
outer_rate = 0.7
blend_share = 0.25
logit_cap = 50.0
query_scalar = 12.0

NX, NZH, NC, NZL, NY = 4, 4, 2, 4, 4


def params(mib=40):
    return pltpu.CompilerParams(vmem_limit_bytes=mib << 20)


def prep_kernel(codes_ref, exps_ref, base_ref, delta_ref, part_ref):
    factor = jnp.exp2(exps_ref[...].astype(jnp.float32))
    for j in range(KC // BLOCK):
        cols = slice(j * BLOCK, (j + 1) * BLOCK)
        delta = codes_ref[:, cols].astype(jnp.float32) * factor[:, j : j + 1]
        delta_ref[j] = delta.astype(jnp.bfloat16)
        part_ref[:, cols] = (base_ref[:, cols].astype(jnp.float32) - delta).astype(jnp.bfloat16)


def prep(codes, exps, base):
    rows = codes.shape[0]
    return pl.pallas_call(
        prep_kernel,
        out_shape=(
            jax.ShapeDtypeStruct((KC // BLOCK, rows, BLOCK), jnp.bfloat16),
            jax.ShapeDtypeStruct((rows, KC), jnp.bfloat16),
        ),
        in_specs=[VMEM] * 3,
        out_specs=(VMEM, VMEM),
        compiler_params=params(),
        name="prep",
    )(codes, exps, base)


def local_kernel(h0_ref, h1_ref, h2_ref, h3_ref, part_ref, hidden_ref, out_ref):
    for s, ref in enumerate((h0_ref, h1_ref, h2_ref, h3_ref)):
        hidden_ref[s * 128 : (s + 1) * 128, :] = ref[...]
    for n in range(KC // 256):
        cols = slice(n * 256, (n + 1) * 256)
        out_ref[:, cols] = blend_share * jnp.dot(
            hidden_ref[...], part_ref[:, cols], preferred_element_type=jnp.float32
        )


def local_product(hidden, part):
    return pl.pallas_call(
        local_kernel,
        out_shape=(
            jax.ShapeDtypeStruct((512, part.shape[0]), jnp.bfloat16),
            jax.ShapeDtypeStruct((512, KC), jnp.float32),
        ),
        in_specs=[VMEM] * 5,
        out_specs=(VMEM, VMEM),
        compiler_params=params(),
        name="local_product",
    )(*hidden, part)


def project_kernel(place_ref, hidden_ref, local_ref, same_ref, other_ref, out_ref, own_ref, weight):
    rows = own_ref.shape[0]
    c, z, y = place_ref[0], place_ref[1], place_ref[2]
    for x in range(NX):
        for near, ref in enumerate((same_ref, other_ref)):
            at = (x * NC + lax.rem(c + near, NC)) * BLOCK
            cols = pl.ds(pl.multiple_of(at, BLOCK), BLOCK)
            own_ref[:, cols] = ref[x * NY + y]
            for ys in range(NY):
                weight[ys * rows : (ys + 1) * rows, cols] = ref[x * NY + ys]
    for n in range(NZL):
        cols = slice(n * 256, (n + 1) * 256)
        outer = jnp.dot(hidden_ref[...], weight[:, cols], preferred_element_type=jnp.float32)
        total = (local_ref[:, cols] + (1.0 - blend_share) * outer).astype(jnp.bfloat16)
        for s in range(NZL):
            at = pl.multiple_of(lax.rem(z - s + NZL, NZL) * 128, 128)
            out_ref[n, pl.ds(at, 128), :] = total[s * 128 : (s + 1) * 128]


def project(place, hidden, local, same, other):
    rows = same.shape[1]
    return pl.pallas_call(
        project_kernel,
        out_shape=(
            jax.ShapeDtypeStruct((NZL, 512, KC // NZL), jnp.bfloat16),
            jax.ShapeDtypeStruct((rows, KC), jnp.bfloat16),
        ),
        in_specs=[SMEM] + [VMEM] * 4,
        out_specs=(VMEM, VMEM),
        scratch_shapes=[pltpu.VMEM((NY * rows, KC), jnp.bfloat16)],
        compiler_params=params(),
        name="project",
    )(place, hidden, local, same, other)


def attend_kernel(place_ref, q_ref, keys, values, out_ref):
    z, y = place_ref[1], place_ref[2]
    row = lax.broadcasted_iota(jnp.int32, (256, 128), 0) % 128
    col = lax.broadcasted_iota(jnp.int32, (256, 128), 1)
    seen = col - row
    for zq in range(NZL):
        at = lax.rem(z - zq + NZL, NZL)
        q = jnp.concatenate([q_ref[at, :, :HD], q_ref[at, :, HD:]], axis=0)
        acc = jnp.zeros((256, HD), jnp.float32)
        total = jnp.zeros((256, 128), jnp.float32)
        for zk in range(zq + 1):
            rows = slice(zk * 128, (zk + 1) * 128)
            value_rows = pl.ds(pl.multiple_of(lax.rem(z - zk + NZL, NZL) * 128, 128), 128)
            for s in range(NY):
                scores = lax.dot_general(
                    q,
                    keys[s, rows, :],
                    (((1,), (1,)), ((), ())),
                    preferred_element_type=jnp.float32,
                )
                p = jnp.exp(logit_cap * jnp.tanh(scores * (1.0 / (query_scalar * logit_cap))))
                if zk == zq:
                    p = jnp.where(seen <= (y - s) * 128, p, 0.0)
                total += p
                acc += jnp.dot(
                    p.astype(jnp.bfloat16),
                    values[s, value_rows, :],
                    preferred_element_type=jnp.float32,
                )
        out = (acc / jnp.sum(total, axis=1, keepdims=True)).astype(jnp.bfloat16)
        out_ref[zq, :, :HD] = out[:128]
        out_ref[zq, :, HD:] = out[128:]


def attend(place, q, keys, values):
    kv_spec = pl.BlockSpec((NY, 512, HD), lambda h: (0, 0, h))
    q_spec = pl.BlockSpec((NZL, 128, 2 * HD), lambda h: (0, 0, h))
    return pl.pallas_call(
        attend_kernel,
        grid=(2,),
        out_shape=jax.ShapeDtypeStruct((NZL, 128, 4 * HD), jnp.bfloat16),
        in_specs=[SMEM, q_spec] + [kv_spec] * 2,
        out_specs=q_spec,
        compiler_params=params(),
        name="attend",
    )(place, q, keys, values)


def swap(array, axis, pairs):
    return lax.ppermute(array, axis, pairs + [(b, a) for a, b in pairs])


def add(a, b):
    return a.astype(jnp.float32) + b.astype(jnp.float32)


def deal(arrays, axis):
    at = lax.axis_index(axis)
    pieces = []
    for step in range(4):
        to = lax.rem(at + step, 4)
        cut = []
        for array in arrays:
            width = array.shape[1] // 4
            cut.append(lax.dynamic_slice_in_dim(array, to * width, width, 1))
        piece = jnp.concatenate(cut, axis=1)
        if step:
            piece = lax.ppermute(piece, axis, [(i, (i + step) % 4) for i in range(4)])
        pieces.append(piece)
    return pieces


def gather(array, axis, size):
    return lax.all_to_all(jnp.broadcast_to(array, (size,) + array.shape), axis, 0, 0, tiled=True)


def exchange(array, axis):
    return lax.all_to_all(array, axis, 0, 0, tiled=True)


def on_device(hidden, queries, values, codes, exponents, base, momentum):
    x, c, z, y = (lax.axis_index(name) for name in ("x", "c", "zl", "y"))
    place = jnp.stack([c, z, y]).astype(jnp.int32)
    rows = codes.shape[1]

    delta, part = prep(codes[0], exponents[0], base)
    part_all = lax.all_gather(part, "y", axis=0, tiled=True)

    sent = exchange(delta, ("x", "c"))
    hidden_in, _ = lax.optimization_barrier((hidden[0], part))
    hidden_deal = deal([hidden_in], "zl")
    eighth = jnp.sum(sent.astype(jnp.float32), axis=0).astype(jnp.bfloat16)
    pair = add(eighth, swap(eighth, "zh", [(0, 1), (2, 3)])).astype(jnp.bfloat16)
    pair, *hidden_deal = lax.optimization_barrier((pair, *hidden_deal))
    mean = add(pair, swap(pair, "zh", [(1, 2), (3, 0)])) / (NX * NZH * NC)
    at = (x * NC + c) * BLOCK
    base_here = lax.dynamic_slice_in_dim(base, at, BLOCK, 1).astype(jnp.float32)
    moment_here = lax.dynamic_slice_in_dim(momentum, at, BLOCK, 1).astype(jnp.float32)
    moment_new = momentum_rate * moment_here + mean
    outer = (base_here - outer_rate * (mean + momentum_rate * moment_new)).astype(jnp.bfloat16)

    queries_in, values_in, outer = lax.optimization_barrier((queries[0], values[0], outer))
    both = jnp.stack(deal([queries_in, values_in], "zl"))

    same = gather(outer, ("x", "y"), NX * NY)
    other = lax.ppermute(same, "c", [(0, 1), (1, 0)])
    hidden_here, local = local_product(hidden_deal, part_all)
    other, both = lax.optimization_barrier((other, both))
    sums, own = project(place, hidden_here, local, same, other)

    value_all = lax.all_gather(both[:, :, 512:].reshape(512, KC // NZL), "y", axis=0)
    sums = exchange(sums, "zl")
    keys = (jnp.sum(sums.astype(jnp.float32), axis=0) / math.sqrt(D)).astype(jnp.bfloat16)
    mixed = attend(place, both, gather(keys, "y", NY), value_all)
    attended = jnp.transpose(exchange(mixed, "zl"), (1, 0, 2))

    whole = jnp.transpose(delta, (1, 0, 2)).reshape(rows, KC).astype(jnp.float32)
    blended = blend_share * (base.astype(jnp.float32) - whole) + (
        1.0 - blend_share
    ) * own.astype(jnp.float32)
    return blended.astype(jnp.bfloat16)[None], attended.reshape(1, 128, QH * HD)


def solution(mesh):
    split = Mesh(
        mesh.devices.reshape(NX, NZH, NC, NZL, NY),
        ("x", "zh", "c", "zl", "y"),
    )
    replica, fsdp = ("x", "zh", "c"), ("zl", "y")
    stacked = P(replica, fsdp, None)
    return jax.shard_map(
        on_device,
        mesh=split,
        in_specs=(stacked,) * 5 + (P(fsdp, None),) * 2,
        out_specs=(stacked, stacked),
        check_vma=False,
    )
```

time: 547 us -> 220 us (0.40); the launches traced: 537 us -> 219 us
  waiting for transfers between devices: 446 us -> 89.2 us
  starting transfers between devices: 27.8 us -> 67.7 us
  matrix products: 18.4 us -> 0 us
  Pallas kernels: 0 us -> 11.3 us
  blocking collectives: 14.6 us -> 21 us
    psum x1 -> x0, waiting for transfers between devices: 340 us -> none  [on_device(): lax.psum(delta.astype(jnp.bfloat16), 'replica').astype(jnp.float32)]
    all_gather x1 -> x2, waiting for transfers between devices: 85.3 us -> 0.04 us  [the longest x1 0.02 us: on_device(): part_all = lax.all_gather(part, 'y', axis=0, tiled=True)]
    ppermute x0 -> x9, starting transfers between devices: none -> 40.7 us  [the longest x6 24.8 us: deal(): piece = lax.ppermute(piece, axis, [(i, (i + step) % 4) for i in range(4)])]
    all_to_all x3 -> x4, waiting for transfers between devices: 21.4 us -> 58.9 us  [the longest x3 45.2 us: exchange(): return lax.all_to_all(array, axis, 0, 0, tiled=True)]
    ppermute x0 -> x9, waiting for transfers between devices: none -> 29.6 us  [the longest x6 27 us: deal(): piece = lax.ppermute(piece, axis, [(i, (i + step) % 4) for i in range(4)])]
    dot_general x9 -> x0, matrix products: 18.4 us -> none  [the longest x4 6.58 us: block_rows(): jnp.einsum('qhd,khd->hqk', query_block, key_heads, preferred_element_type...]
    pallas_call x0 -> x4, Pallas kernels: none -> 11.3 us  [the longest x1 5.22 us: attend(): pl.pallas_call(attend_kernel, grid=(2,), out_shape=jax.ShapeDtypeStruct((...]
    all_to_all x1, blocking collectives: 14.6 us -> 21 us  [gather(): lax.all_to_all(jnp.broadcast_to(array, (size,) + array.shape), axis, 0, 0...]
  transfers between devices with their start and end apart: 5 -> 15, of which waited for: 4 -> 9; matrix products, arithmetic and copies ran while one was open for 2% -> 3% of each run, Pallas kernels for 0% -> 0%
where the time goes in v1:
time: 220 us; the launch traced here: 219 us
  waiting for transfers between devices  89.2 us (41%)
  starting transfers between devices  67.7 us (31%)
  blocking collectives  21 us (10%)
  between operations  14.5 us (7%)
  Pallas kernels  11.3 us (5%)
  local copies, waits for them, and re-layouts  11.2 us (5%)
  other arithmetic  3.66 us (2%)
    all_to_all x3, waiting for transfers between devices, exchange(): return lax.all_to_all(array, axis, 0, 0, tiled=True)  45.2 us
    ppermute x6, waiting for transfers between devices, deal(): piece = lax.ppermute(piece, axis, [(i, (i + step) % 4) for i in range(4)])  27 us
    ppermute x6, starting transfers between devices, deal(): piece = lax.ppermute(piece, axis, [(i, (i + step) % 4) for i in range(4)])  24.8 us
    all_to_all x3, starting transfers between devices, exchange(): return lax.all_to_all(array, axis, 0, 0, tiled=True)  23.4 us
    all_to_all x1, blocking collectives, gather(): lax.all_to_all(jnp.broadcast_to(array, (size,) + array.shape), axis, 0, 0...  21 us
    all_to_all x1, waiting for transfers between devices, gather(): lax.all_to_all(jnp.broadcast_to(array, (size,) + array.shape), axis, 0, 0...  13.7 us
    ppermute x2, starting transfers between devices, swap(): return lax.ppermute(array, axis, pairs + [(b, a) for a, b in pairs])  10.9 us
    unnamed x24, local copies, waits for them, and re-layouts  8.8 us
  transfers between devices with their start and end apart: 15, of which 9 were waited for; matrix products, arithmetic and copies ran while one was open for 3% of the time, Pallas kernels for 0%

profile of v1, /device:TPU:1, one launch (start us, length us, event | category | flops | bytes accessed | tf_op | source)
XLA Modules:
  0.0 218.5 jit_solution(18301739968382450582)
XLA Ops:
  11.5 10.4 %all-to-all-start = ((bf16[8,288,128]{2,1,0:T(8,128)(2,1)}), bf16[8,288,128]{2,1,0:T(8,128)(2,1)S(1)}, u32[]{:S(2)}, u32[]{:S(2)}) async-start(bf16[8,288,128]{2,1,0:T(8,128)(2,1)} %get-tuple-element.19), calls=%async_computation | async-start | bytes 1179648 | tf_op jit(solution)/shard_map/all_to_all | solution.py:193
  22.7 9.4 %all-to-all-done = bf16[8,288,128]{2,1,0:T(8,128)(2,1)S(1)} async-done(((bf16[8,288,128]{2,1,0:T(8,128)(2,1)}), bf16[8,288,128]{2,1,0:T(8,128)(2,1)S(1)}, u32[]{:S(2)}, u32[]{:S(2)}) %all-to-all-start) | async-done | bytes 589856 | tf_op jit(solution)/shard_map/all_to_all | solution.py:193
  32.3 4.4 %collective-permute-start = (bf16[288,128]{1,0:T(8,128)(2,1)S(1)}, bf16[288,128]{1,0:T(8,128)(2,1)S(1)}, u32[]{:S(2)}, u32[]{:S(2)}) collective-permute-start(bf16[288,128]{1,0:T(8,128)(2,1)S(1)} %reduce_sum.21), channel_id=1, source_target_pairs={{0,32},{64,96},{32,0},{96,64},{1,33},{65,97},{33,1},{97,65},{2,34}... | collective-permute-start | bytes 221192 | tf_op jit(solution)/shard_map/ppermute | solution.py:165
  36.8 6.3 %collective-permute-start.3 = (bf16[128,1152]{1,0:T(8,128)(2,1)S(1)}, bf16[128,1152]{1,0:T(8,128)(2,1)S(1)}, u32[]{:S(2)}, u32[]{:S(2)}) collective-permute-start(bf16[128,1152]{1,0:T(8,128)(2,1)S(1)} %get-tuple-element.40), channel_id=1, source_target_pairs={{0,12},{4,0},{8,4},{12,8},{1,13},{5,1},{9,5},{13,9},{2,14},{6,2},{... | collective-permute-start | bytes 884744 | tf_op jit(solution)/shard_map/ppermute | solution.py:183
  43.1 1.9 collective-permute-start.2
  45.0 2.2 %collective-permute-start.1 = (bf16[128,1152]{1,0:T(8,128)(2,1)S(1)}, bf16[128,1152]{1,0:T(8,128)(2,1)S(1)}, u32[]{:S(2)}, u32[]{:S(2)}) collective-permute-start(bf16[128,1152]{1,0:T(8,128)(2,1)S(1)} %get-tuple-element.42), channel_id=1, source_target_pairs={{0,4},{4,8},{8,12},{12,0},{1,5},{5,9},{9,13},{13,1},{2,6},{6,10},{... | collective-permute-start | bytes 884744 | tf_op jit(solution)/shard_map/ppermute | solution.py:183
  48.3 20.5 %collective-permute-done.2.h2_ref = bf16[128,1152]{1,0:T(8,128)(2,1)S(1)} collective-permute-done((bf16[128,1152]{1,0:T(8,128)(2,1)S(1)}, bf16[128,1152]{1,0:T(8,128)(2,1)S(1)}, u32[]{:S(2)}, u32[]{:S(2)}) %collective-permute-start.2) | collective-permute-done | bytes 294944 | tf_op jit(solution)/shard_map/ppermute | solution.py:183
  68.7 6.5 %collective-permute-start.4 = (bf16[288,128]{1,0:T(8,128)(2,1)S(1)}, bf16[288,128]{1,0:T(8,128)(2,1)S(1)}, u32[]{:S(2)}, u32[]{:S(2)}) collective-permute-start(bf16[288,128]{1,0:T(8,128)(2,1)S(1)} %add_convert_fusion), channel_id=1, source_target_pairs={{32,64},{96,0},{64,32},{0,96},{33,65},{97,1},{65,33},{1,97},{34,66... | collective-permute-start | bytes 221192 | tf_op jit(solution)/shard_map/ppermute | solution.py:165
  75.3 2.6 %collective-permute-done.4 = bf16[288,128]{1,0:T(8,128)(2,1)S(1)} collective-permute-done((bf16[288,128]{1,0:T(8,128)(2,1)S(1)}, bf16[288,128]{1,0:T(8,128)(2,1)S(1)}, u32[]{:S(2)}, u32[]{:S(2)}) %collective-permute-start.4) | collective-permute-done | bytes 73760 | tf_op jit(solution)/shard_map/ppermute | solution.py:165
  79.1 21.0 %all_to_all.25.same_ref = bf16[16,288,128]{2,1,0:T(8,128)(2,1)S(1)} all-to-all(bf16[16,288,128]{2,1,0:T(8,128)(2,1)S(1)} %broadcast_in_dim.9), channel_id=1, replica_groups=mesh['x'=4,'zh'=4,'c'=2,'zl'=4,'y'=4] {'x','y'}, dimensions={0} | all-to-all | bytes 2359296 | tf_op jit(solution)/shard_map/all_to_all | solution.py:189
  100.1 5.0 %collective-permute-start.5 = (bf16[16,288,128]{2,1,0:T(8,128)(2,1)S(1)}, bf16[16,288,128]{2,1,0:T(8,128)(2,1)}, u32[]{:S(2)}, u32[]{:S(2)}) collective-permute-start(bf16[16,288,128]{2,1,0:T(8,128)(2,1)S(1)} %all_to_all.25.same_ref), channel_id=1, source_target_pairs={{0,16},{16,0},{1,17},{17,1},{2,18},{18,2},{3,19},{19,3},{4,20},{20... | collective-permute-start | bytes 3538952 | tf_op jit(solution)/shard_map/ppermute | solution.py:221
  105.3 5.2 %collective-permute-start.6 = (bf16[128,768]{1,0:T(8,128)(2,1)S(1)}, bf16[128,768]{1,0:T(8,128)(2,1)S(1)}, u32[]{:S(2)}, u32[]{:S(2)}) collective-permute-start(bf16[128,768]{1,0:T(8,128)(2,1)S(1)} %pad_maximum_fusion.1), channel_id=1, source_target_pairs={{0,4},{4,8},{8,12},{12,0},{1,5},{5,9},{9,13},{13,1},{2,6},{6,10},{... | collective-permute-start | bytes 589832 | tf_op jit(solution)/shard_map/ppermute | solution.py:183
  110.6 4.9 %collective-permute-start.7 = (bf16[128,768]{1,0:T(8,128)(2,1)S(1)}, bf16[128,768]{1,0:T(8,128)(2,1)S(1)}, u32[]{:S(2)}, u32[]{:S(2)}) collective-permute-start(bf16[128,768]{1,0:T(8,128)(2,1)S(1)} %pad_maximum_fusion.2), channel_id=1, source_target_pairs={{0,8},{4,12},{8,0},{12,4},{1,9},{5,13},{9,1},{13,5},{2,10},{6,14},... | collective-permute-start | bytes 589832 | tf_op jit(solution)/shard_map/ppermute | solution.py:183
  115.5 4.3 %collective-permute-start.8 = (bf16[128,768]{1,0:T(8,128)(2,1)S(1)}, bf16[128,768]{1,0:T(8,128)(2,1)S(1)}, u32[]{:S(2)}, u32[]{:S(2)}) collective-permute-start(bf16[128,768]{1,0:T(8,128)(2,1)S(1)} %pad_maximum_fusion.3), channel_id=1, source_target_pairs={{0,12},{4,0},{8,4},{12,8},{1,13},{5,1},{9,5},{13,9},{2,14},{6,2},{... | collective-permute-start | bytes 589832 | tf_op jit(solution)/shard_map/ppermute | solution.py:183
  119.9 5.1 %collective-permute-done.7 = bf16[128,768]{1,0:T(8,128)(2,1)S(1)} collective-permute-done((bf16[128,768]{1,0:T(8,128)(2,1)S(1)}, bf16[128,768]{1,0:T(8,128)(2,1)S(1)}, u32[]{:S(2)}, u32[]{:S(2)}) %collective-permute-start.7) | collective-permute-done | bytes 196640 | tf_op jit(solution)/shard_map/ppermute | solution.py:183
  129.7 3.2 %project.1 = (bf16[4,512,256]{2,1,0:T(8,128)(2,1)S(1)}, bf16[288,1024]{1,0:T(8,128)(2,1)S(1)}) custom-call(s32[3]{0:T(128)S(1)} %pad_add_fusion.place_ref, bf16[512,1152]{1,0:T(8,128)(2,1)S(1)} %get-tuple-element.26.hidden_ref, f32[512,1024]{1,0:T(8,128)S(1)} %get-tuple-element.27.local_ref, bf16[16,288,128]{2,1,0:T(8,128)(2,1)S(1)} %all_to_all.25.same_ref, ...), custom_call_target="tpu_custom_call" | custom-call | tf_op jit(solution)/shard_map/project/pallas_call | solution.py:102
  133.9 9.5 %all-to-all-start.2 = ((bf16[4,512,256]{2,1,0:T(8,128)(2,1)}), bf16[4,512,256]{2,1,0:T(8,128)(2,1)S(1)}, u32[]{:S(2)}, u32[]{:S(2)}) async-start(bf16[4,512,256]{2,1,0:T(8,128)(2,1)} %copy-done.4), calls=%async_computation.2 | async-start | bytes 2097152 | tf_op jit(solution)/shard_map/all_to_all | solution.py:193
  144.1 24.6 %all-to-all-done.2 = bf16[4,512,256]{2,1,0:T(8,128)(2,1)S(1)} async-done(((bf16[4,512,256]{2,1,0:T(8,128)(2,1)}), bf16[4,512,256]{2,1,0:T(8,128)(2,1)S(1)}, u32[]{:S(2)}, u32[]{:S(2)}) %all-to-all-start.2) | async-done | bytes 1048608 | tf_op jit(solution)/shard_map/all_to_all | solution.py:193
  169.9 3.5 %all-to-all-start.3 = ((bf16[4,512,256]{2,1,0:T(8,128)(2,1)}), bf16[4,512,256]{2,1,0:T(8,128)(2,1)S(1)}, u32[]{:S(2)}, u32[]{:S(2)}) async-start(bf16[4,512,256]{2,1,0:T(8,128)(2,1)} %broadcast_in_dim.11), calls=%async_computation.3 | async-start | bytes 2097152 | tf_op jit(solution)/shard_map/all_to_all | solution.py:189
  173.4 13.7 %all-to-all-done.3.keys = bf16[4,512,256]{2,1,0:T(8,128)(2,1)S(1)} async-done(((bf16[4,512,256]{2,1,0:T(8,128)(2,1)}), bf16[4,512,256]{2,1,0:T(8,128)(2,1)S(1)}, u32[]{:S(2)}, u32[]{:S(2)}) %all-to-all-start.3) | async-done | bytes 1048608 | tf_op jit(solution)/shard_map/all_to_all | solution.py:189
  188.4 5.2 %attend.1 = bf16[4,128,512]{2,1,0:T(8,128)(2,1)} custom-call(s32[3]{0:T(128)S(1)} %pad_add_fusion.place_ref, bf16[4,128,768]{2,1,0:T(8,128)(2,1)S(1)} %pad_maximum_fusion.q_ref, bf16[4,512,256]{2,1,0:T(8,128)(2,1)S(1)} %all-to-all-done.3.keys, bf16[4,512,256]{2,1,0:T(8,128)(2,1)S(1)} %copy-done.3), custom_call_target="tpu_custom_call" | custom-call | tf_op jit(solution)/shard_map/attend/pallas_call | solution.py:153
  193.6 3.5 %all-to-all-start.4 = ((bf16[4,128,512]{2,1,0:T(8,128)(2,1)}), bf16[4,128,512]{2,1,0:T(8,128)(2,1)S(1)}, u32[]{:S(2)}, u32[]{:S(2)}) async-start(bf16[4,128,512]{2,1,0:T(8,128)(2,1)} %attend.1), calls=%async_computation.4 | async-start | bytes 1048576 | tf_op jit(solution)/shard_map/all_to_all | solution.py:193
  197.1 2.2 fusion.3
  199.2 11.1 %all-to-all-done.4 = bf16[4,128,512]{2,1,0:T(8,128)(2,1)S(1)} async-done(((bf16[4,128,512]{2,1,0:T(8,128)(2,1)}), bf16[4,128,512]{2,1,0:T(8,128)(2,1)S(1)}, u32[]{:S(2)}, u32[]{:S(2)}) %all-to-all-start.4) | async-done | bytes 524320 | tf_op jit(solution)/shard_map/all_to_all | solution.py:193
  (56 shorter events, 17.8 us)
Async XLA Ops:
  8.0 1.1 copy-start
  9.1 1.1 copy-start.5
  11.5 25.2 %copy-start.8 = (bf16[1,128,4608]{2,1,0:T(8,128)(2,1)S(1)}, bf16[1,128,4608]{2,1,0:T(8,128)(2,1)}, u32[]{:S(2)}) copy-start(bf16[1,128,4608]{2,1,0:T(8,128)(2,1)} %param.7) | copy-start | bytes 3538948
  11.5 20.7 %all-to-all-start = ((bf16[8,288,128]{2,1,0:T(8,128)(2,1)}), bf16[8,288,128]{2,1,0:T(8,128)(2,1)S(1)}, u32[]{:S(2)}, u32[]{:S(2)}) async-start(bf16[8,288,128]{2,1,0:T(8,128)(2,1)} %get-tuple-element.19), calls=%async_computation | async-start | bytes 1179648 | tf_op jit(solution)/shard_map/all_to_all | solution.py:193
  22.0 103.6 %all-gather.3.cloned.1.call-start = ((), (), s32[]{:S(2)}) async-start(), calls=%async_computation.5 | async-start | bytes 2949120 | tf_op jit(solution)/shard_map/all_gather | solution.py:202
  32.3 45.6 %copy-start.1 = (bf16[288,1024]{1,0:T(8,128)(2,1)S(1)}, bf16[288,1024]{1,0:T(8,128)(2,1)}, u32[]{:S(2)}) copy-start(bf16[288,1024]{1,0:T(8,128)(2,1)} %base_ref.1) | copy-start | bytes 1769476
  32.3 14.9 %collective-permute-start = (bf16[288,128]{1,0:T(8,128)(2,1)S(1)}, bf16[288,128]{1,0:T(8,128)(2,1)S(1)}, u32[]{:S(2)}, u32[]{:S(2)}) collective-permute-start(bf16[288,128]{1,0:T(8,128)(2,1)S(1)} %reduce_sum.21), channel_id=1, source_target_pairs={{0,32},{64,96},{32,0},{96,64},{1,33},{65,97},{33,1},{97,65},{2,34}... | collective-permute-start | bytes 221192 | tf_op jit(solution)/shard_map/ppermute | solution.py:165
  36.8 11.4 %collective-permute-start.3 = (bf16[128,1152]{1,0:T(8,128)(2,1)S(1)}, bf16[128,1152]{1,0:T(8,128)(2,1)S(1)}, u32[]{:S(2)}, u32[]{:S(2)}) collective-permute-start(bf16[128,1152]{1,0:T(8,128)(2,1)S(1)} %get-tuple-element.40), channel_id=1, source_target_pairs={{0,12},{4,0},{8,4},{12,8},{1,13},{5,1},{9,5},{13,9},{2,14},{6,2},{... | collective-permute-start | bytes 884744 | tf_op jit(solution)/shard_map/ppermute | solution.py:183
  43.1 25.6 %collective-permute-start.2 = (bf16[128,1152]{1,0:T(8,128)(2,1)S(1)}, bf16[128,1152]{1,0:T(8,128)(2,1)S(1)}, u32[]{:S(2)}, u32[]{:S(2)}) collective-permute-start(bf16[128,1152]{1,0:T(8,128)(2,1)S(1)} %get-tuple-element.41), channel_id=1, source_target_pairs={{0,8},{4,12},{8,0},{12,4},{1,9},{5,13},{9,1},{13,5},{2,10},{6,14},... | collective-permute-start | bytes 884744 | tf_op jit(solution)/shard_map/ppermute | solution.py:183
  45.0 23.7 %collective-permute-start.1 = (bf16[128,1152]{1,0:T(8,128)(2,1)S(1)}, bf16[128,1152]{1,0:T(8,128)(2,1)S(1)}, u32[]{:S(2)}, u32[]{:S(2)}) collective-permute-start(bf16[128,1152]{1,0:T(8,128)(2,1)S(1)} %get-tuple-element.42), channel_id=1, source_target_pairs={{0,4},{4,8},{8,12},{12,0},{1,5},{5,9},{9,13},{13,1},{2,6},{6,10},{... | collective-permute-start | bytes 884744 | tf_op jit(solution)/shard_map/ppermute | solution.py:183
  68.7 10.2 %copy-start.6 = (bf16[128,1152]{1,0:T(8,128)(2,1)}, bf16[128,1152]{1,0:T(8,128)(2,1)S(1)}, u32[]{:S(2)}) copy-start(bf16[128,1152]{1,0:T(8,128)(2,1)S(1)} %collective-permute-done.1.h1_ref) | copy-start | bytes 884740
  68.7 9.2 %collective-permute-start.4 = (bf16[288,128]{1,0:T(8,128)(2,1)S(1)}, bf16[288,128]{1,0:T(8,128)(2,1)S(1)}, u32[]{:S(2)}, u32[]{:S(2)}) collective-permute-start(bf16[288,128]{1,0:T(8,128)(2,1)S(1)} %add_convert_fusion), channel_id=1, source_target_pairs={{32,64},{96,0},{64,32},{0,96},{33,65},{97,1},{65,33},{1,97},{34,66... | collective-permute-start | bytes 221192 | tf_op jit(solution)/shard_map/ppermute | solution.py:165
  79.1 26.1 %copy-start.10 = (bf16[1,128,1024]{2,1,0:T(8,128)(2,1)S(1)}, bf16[1,128,1024]{2,1,0:T(8,128)(2,1)}, u32[]{:S(2)}) copy-start(bf16[1,128,1024]{2,1,0:T(8,128)(2,1)} %param.9) | copy-start | bytes 786436
  79.1 26.2 %copy-start.9 = (bf16[1,128,2048]{2,1,0:T(8,128)(2,1)S(1)}, bf16[1,128,2048]{2,1,0:T(8,128)(2,1)}, u32[]{:S(2)}) copy-start(bf16[1,128,2048]{2,1,0:T(8,128)(2,1)} %param.8) | copy-start | bytes 1572868
  100.1 25.4 %collective-permute-start.5 = (bf16[16,288,128]{2,1,0:T(8,128)(2,1)S(1)}, bf16[16,288,128]{2,1,0:T(8,128)(2,1)}, u32[]{:S(2)}, u32[]{:S(2)}) collective-permute-start(bf16[16,288,128]{2,1,0:T(8,128)(2,1)S(1)} %all_to_all.25.same_ref), channel_id=1, source_target_pairs={{0,16},{16,0},{1,17},{17,1},{2,18},{18,2},{3,19},{19,3},{4,20},{20... | collective-permute-start | bytes 3538952 | tf_op jit(solution)/shard_map/ppermute | solution.py:221
  105.3 14.6 %collective-permute-start.6 = (bf16[128,768]{1,0:T(8,128)(2,1)S(1)}, bf16[128,768]{1,0:T(8,128)(2,1)S(1)}, u32[]{:S(2)}, u32[]{:S(2)}) collective-permute-start(bf16[128,768]{1,0:T(8,128)(2,1)S(1)} %pad_maximum_fusion.1), channel_id=1, source_target_pairs={{0,4},{4,8},{8,12},{12,0},{1,5},{5,9},{9,13},{13,1},{2,6},{6,10},{... | collective-permute-start | bytes 589832 | tf_op jit(solution)/shard_map/ppermute | solution.py:183
  110.6 14.4 %collective-permute-start.7 = (bf16[128,768]{1,0:T(8,128)(2,1)S(1)}, bf16[128,768]{1,0:T(8,128)(2,1)S(1)}, u32[]{:S(2)}, u32[]{:S(2)}) collective-permute-start(bf16[128,768]{1,0:T(8,128)(2,1)S(1)} %pad_maximum_fusion.2), channel_id=1, source_target_pairs={{0,8},{4,12},{8,0},{12,4},{1,9},{5,13},{9,1},{13,5},{2,10},{6,14},... | collective-permute-start | bytes 589832 | tf_op jit(solution)/shard_map/ppermute | solution.py:183
  115.5 9.9 %collective-permute-start.8 = (bf16[128,768]{1,0:T(8,128)(2,1)S(1)}, bf16[128,768]{1,0:T(8,128)(2,1)S(1)}, u32[]{:S(2)}, u32[]{:S(2)}) collective-permute-start(bf16[128,768]{1,0:T(8,128)(2,1)S(1)} %pad_maximum_fusion.3), channel_id=1, source_target_pairs={{0,12},{4,0},{8,4},{12,8},{1,13},{5,1},{9,5},{13,9},{2,14},{6,2},{... | collective-permute-start | bytes 589832 | tf_op jit(solution)/shard_map/ppermute | solution.py:183
  125.6 1.7 copy-start.2
  133.9 34.8 %all-to-all-start.2 = ((bf16[4,512,256]{2,1,0:T(8,128)(2,1)}), bf16[4,512,256]{2,1,0:T(8,128)(2,1)S(1)}, u32[]{:S(2)}, u32[]{:S(2)}) async-start(bf16[4,512,256]{2,1,0:T(8,128)(2,1)} %copy-done.4), calls=%async_computation.2 | async-start | bytes 2097152 | tf_op jit(solution)/shard_map/all_to_all | solution.py:193
  143.3 30.1 %all-gather.5.cloned.1.call-start = ((), (), s32[]{:S(2)}) async-start(), calls=%async_computation.6 | async-start | bytes 1310720 | tf_op jit(solution)/shard_map/all_gather | solution.py:226
  169.9 17.2 %all-to-all-start.3 = ((bf16[4,512,256]{2,1,0:T(8,128)(2,1)}), bf16[4,512,256]{2,1,0:T(8,128)(2,1)S(1)}, u32[]{:S(2)}, u32[]{:S(2)}) async-start(bf16[4,512,256]{2,1,0:T(8,128)(2,1)} %broadcast_in_dim.11), calls=%async_computation.3 | async-start | bytes 2097152 | tf_op jit(solution)/shard_map/all_to_all | solution.py:189
  187.1 1.2 copy-start.3
  193.6 16.8 %all-to-all-start.4 = ((bf16[4,128,512]{2,1,0:T(8,128)(2,1)}), bf16[4,128,512]{2,1,0:T(8,128)(2,1)S(1)}, u32[]{:S(2)}, u32[]{:S(2)}) async-start(bf16[4,128,512]{2,1,0:T(8,128)(2,1)} %attend.1), calls=%async_computation.4 | async-start | bytes 1048576 | tf_op jit(solution)/shard_map/all_to_all | solution.py:193
  (2 other events, 1.9 us)
Sparse Core Ops, SparseCore 0:
  25.5 40.4 all-gather.2
  146.8 24.0 all-gather.4

commit v2 on v1

--- a/solution.py
+++ b/solution.py
@@ -202,11 +202,10 @@
     part_all = lax.all_gather(part, "y", axis=0, tiled=True)
 
     sent = exchange(delta, ("x", "c"))
-    hidden_in, _ = lax.optimization_barrier((hidden[0], part))
-    hidden_deal = deal([hidden_in], "zl")
+    hidden_deal = deal([hidden[0]], "zl")
+    sent, *hidden_deal = lax.optimization_barrier((sent, *hidden_deal))
     eighth = jnp.sum(sent.astype(jnp.float32), axis=0).astype(jnp.bfloat16)
     pair = add(eighth, swap(eighth, "zh", [(0, 1), (2, 3)])).astype(jnp.bfloat16)
-    pair, *hidden_deal = lax.optimization_barrier((pair, *hidden_deal))
     mean = add(pair, swap(pair, "zh", [(1, 2), (3, 0)])) / (NX * NZH * NC)
     at = (x * NC + c) * BLOCK
     base_here = lax.dynamic_slice_in_dim(base, at, BLOCK, 1).astype(jnp.float32)
@@ -218,9 +217,9 @@
     both = jnp.stack(deal([queries_in, values_in], "zl"))
 
     same = gather(outer, ("x", "y"), NX * NY)
+    hidden_here, local = local_product(hidden_deal, part_all)
+    same, both, local = lax.optimization_barrier((same, both, local))
     other = lax.ppermute(same, "c", [(0, 1), (1, 0)])
-    hidden_here, local = local_product(hidden_deal, part_all)
-    other, both = lax.optimization_barrier((other, both))
     sums, own = project(place, hidden_here, local, same, other)
 
     value_all = lax.all_gather(both[:, :, 512:].reshape(512, KC // NZL), "y", axis=0)

time: 220 us -> 208 us (0.945); the launches traced: 219 us -> 204 us
  blocking collectives: 21 us -> 0 us
  local copies, waits for them, and re-layouts: 11.2 us -> 17.4 us
    all_to_all x1 -> x0, blocking collectives: 21 us -> none  [gather(): lax.all_to_all(jnp.broadcast_to(array, (size,) + array.shape), axis, 0, 0...]
    all_to_all x3, waiting for transfers between devices: 45.2 us -> 34.1 us  [exchange(): return lax.all_to_all(array, axis, 0, 0, tiled=True)]
    ppermute x2, waiting for transfers between devices: 2.65 us -> 10.4 us  [swap(): return lax.ppermute(array, axis, pairs + [(b, a) for a, b in pairs])]
    all_to_all x1 -> x2, starting transfers between devices: 3.51 us -> 10.5 us  [gather(): lax.all_to_all(jnp.broadcast_to(array, (size,) + array.shape), axis, 0, 0...]
    all_to_all x3, starting transfers between devices: 23.4 us -> 18 us  [exchange(): return lax.all_to_all(array, axis, 0, 0, tiled=True)]
    unnamed x24 -> x32, local copies, waits for them, and re-layouts: 8.8 us -> 14 us
    ppermute x1, waiting for transfers between devices: 0.01 us -> 2.5 us  [on_device(): other = lax.ppermute(same, 'c', [(0, 1), (1, 0)])]
    ppermute x2, starting transfers between devices: 10.9 us -> 13.3 us  [swap(): return lax.ppermute(array, axis, pairs + [(b, a) for a, b in pairs])]
  transfers between devices with their start and end apart: 15 -> 16, of which waited for: 9 -> 10; matrix products, arithmetic and copies ran while one was open for 3% -> 3% of each run, Pallas kernels for 0% -> 1%
where the time goes in v2:
time: 208 us; the launch traced here: 204 us
  waiting for transfers between devices  89.7 us (43%)
  starting transfers between devices  67.7 us (33%)
  local copies, waits for them, and re-layouts  17.4 us (8%)
  between operations  14.4 us (7%)
  Pallas kernels  11.3 us (5%)
  other arithmetic  3.66 us (2%)
    all_to_all x3, waiting for transfers between devices, exchange(): return lax.all_to_all(array, axis, 0, 0, tiled=True)  34.1 us
    ppermute x6, waiting for transfers between devices, deal(): piece = lax.ppermute(piece, axis, [(i, (i + step) % 4) for i in range(4)])  29.3 us
    ppermute x6, starting transfers between devices, deal(): piece = lax.ppermute(piece, axis, [(i, (i + step) % 4) for i in range(4)])  22.9 us
    all_to_all x3, starting transfers between devices, exchange(): return lax.all_to_all(array, axis, 0, 0, tiled=True)  18 us
    unnamed x32, local copies, waits for them, and re-layouts  14 us
    ppermute x2, starting transfers between devices, swap(): return lax.ppermute(array, axis, pairs + [(b, a) for a, b in pairs])  13.3 us
    all_to_all x2, waiting for transfers between devices, gather(): lax.all_to_all(jnp.broadcast_to(array, (size,) + array.shape), axis, 0, 0...  12 us
    all_to_all x2, starting transfers between devices, gather(): lax.all_to_all(jnp.broadcast_to(array, (size,) + array.shape), axis, 0, 0...  10.5 us
  transfers between devices with their start and end apart: 16, of which 10 were waited for; matrix products, arithmetic and copies ran while one was open for 3% of the time, Pallas kernels for 1%

profile of v2, /device:TPU:1, one launch (start us, length us, event | category | flops | bytes accessed | tf_op | source)
XLA Modules:
  0.0 204.1 jit_solution(7966777178814093198)
XLA Ops:
  11.6 10.5 %all-to-all-start = ((bf16[8,288,128]{2,1,0:T(8,128)(2,1)}), bf16[8,288,128]{2,1,0:T(8,128)(2,1)S(1)}, u32[]{:S(2)}, u32[]{:S(2)}) async-start(bf16[8,288,128]{2,1,0:T(8,128)(2,1)} %get-tuple-element.19), calls=%async_computation | async-start | bytes 1179648 | tf_op jit(solution)/shard_map/all_to_all | solution.py:193
  22.2 2.1 %collective-permute-start = (bf16[128,1152]{1,0:T(8,128)(2,1)S(1)}, bf16[128,1152]{1,0:T(8,128)(2,1)S(1)}, u32[]{:S(2)}, u32[]{:S(2)}) collective-permute-start(bf16[128,1152]{1,0:T(8,128)(2,1)S(1)} %get-tuple-element.41), channel_id=1, source_target_pairs={{0,4},{4,8},{8,12},{12,0},{1,5},{5,9},{9,13},{13,1},{2,6},{6,10},{... | collective-permute-start | bytes 884744 | tf_op jit(solution)/shard_map/ppermute | solution.py:183
  26.3 5.1 %collective-permute-start.2 = (bf16[128,1152]{1,0:T(8,128)(2,1)S(1)}, bf16[128,1152]{1,0:T(8,128)(2,1)S(1)}, u32[]{:S(2)}, u32[]{:S(2)}) collective-permute-start(bf16[128,1152]{1,0:T(8,128)(2,1)S(1)} %get-tuple-element.40), channel_id=1, source_target_pairs={{0,12},{4,0},{8,4},{12,8},{1,13},{5,1},{9,5},{13,9},{2,14},{6,2},{... | collective-permute-start | bytes 884744 | tf_op jit(solution)/shard_map/ppermute | solution.py:183
  31.3 3.2 %collective-permute-done.h1_ref = bf16[128,1152]{1,0:T(8,128)(2,1)S(1)} collective-permute-done((bf16[128,1152]{1,0:T(8,128)(2,1)S(1)}, bf16[128,1152]{1,0:T(8,128)(2,1)S(1)}, u32[]{:S(2)}, u32[]{:S(2)}) %collective-permute-start) | collective-permute-done | bytes 294944 | tf_op jit(solution)/shard_map/ppermute | solution.py:183
  34.5 13.2 %collective-permute-done.1.h2_ref = bf16[128,1152]{1,0:T(8,128)(2,1)S(1)} collective-permute-done((bf16[128,1152]{1,0:T(8,128)(2,1)S(1)}, bf16[128,1152]{1,0:T(8,128)(2,1)S(1)}, u32[]{:S(2)}, u32[]{:S(2)}) %collective-permute-start.1) | collective-permute-done | bytes 294944 | tf_op jit(solution)/shard_map/ppermute | solution.py:183
  47.8 5.4 %collective-permute-start.3 = (bf16[288,128]{1,0:T(8,128)(2,1)S(1)}, bf16[288,128]{1,0:T(8,128)(2,1)S(1)}, u32[]{:S(2)}, u32[]{:S(2)}) collective-permute-start(bf16[288,128]{1,0:T(8,128)(2,1)S(1)} %reduce_sum.21), channel_id=1, source_target_pairs={{0,32},{64,96},{32,0},{96,64},{1,33},{65,97},{33,1},{97,65},{2,34}... | collective-permute-start | bytes 221192 | tf_op jit(solution)/shard_map/ppermute | solution.py:165
  53.2 3.6 %collective-permute-done.3 = bf16[288,128]{1,0:T(8,128)(2,1)S(1)} collective-permute-done((bf16[288,128]{1,0:T(8,128)(2,1)S(1)}, bf16[288,128]{1,0:T(8,128)(2,1)S(1)}, u32[]{:S(2)}, u32[]{:S(2)}) %collective-permute-start.3) | collective-permute-done | bytes 73760 | tf_op jit(solution)/shard_map/ppermute | solution.py:165
  56.9 7.9 %collective-permute-start.4 = (bf16[288,128]{1,0:T(8,128)(2,1)S(1)}, bf16[288,128]{1,0:T(8,128)(2,1)S(1)}, u32[]{:S(2)}, u32[]{:S(2)}) collective-permute-start(bf16[288,128]{1,0:T(8,128)(2,1)S(1)} %add_convert_fusion), channel_id=1, source_target_pairs={{32,64},{96,0},{64,32},{0,96},{33,65},{97,1},{65,33},{1,97},{34,66... | collective-permute-start | bytes 221192 | tf_op jit(solution)/shard_map/ppermute | solution.py:165
  64.8 6.7 %collective-permute-done.4 = bf16[288,128]{1,0:T(8,128)(2,1)S(1)} collective-permute-done((bf16[288,128]{1,0:T(8,128)(2,1)S(1)}, bf16[288,128]{1,0:T(8,128)(2,1)S(1)}, u32[]{:S(2)}, u32[]{:S(2)}) %collective-permute-start.4) | collective-permute-done | bytes 73760 | tf_op jit(solution)/shard_map/ppermute | solution.py:165
  73.7 6.5 %all-to-all-start.1 = ((bf16[16,288,128]{2,1,0:T(8,128)(2,1)}), bf16[16,288,128]{2,1,0:T(8,128)(2,1)S(1)}, u32[]{:S(2)}, u32[]{:S(2)}) async-start(bf16[16,288,128]{2,1,0:T(8,128)(2,1)} %broadcast_in_dim.9), calls=%async_computation.1 | async-start | bytes 2359296 | tf_op jit(solution)/shard_map/all_to_all | solution.py:189
  80.5 9.6 %collective-permute-start.7 = (bf16[128,768]{1,0:T(8,128)(2,1)S(1)}, bf16[128,768]{1,0:T(8,128)(2,1)S(1)}, u32[]{:S(2)}, u32[]{:S(2)}) collective-permute-start(bf16[128,768]{1,0:T(8,128)(2,1)S(1)} %pad_maximum_fusion.3), channel_id=1, source_target_pairs={{0,12},{4,0},{8,4},{12,8},{1,13},{5,1},{9,5},{13,9},{2,14},{6,2},{... | collective-permute-start | bytes 589832 | tf_op jit(solution)/shard_map/ppermute | solution.py:183
  92.1 2.2 %collective-permute-start.5 = (bf16[128,768]{1,0:T(8,128)(2,1)S(1)}, bf16[128,768]{1,0:T(8,128)(2,1)S(1)}, u32[]{:S(2)}, u32[]{:S(2)}) collective-permute-start(bf16[128,768]{1,0:T(8,128)(2,1)S(1)} %pad_maximum_fusion.1), channel_id=1, source_target_pairs={{0,4},{4,8},{8,12},{12,0},{1,5},{5,9},{9,13},{13,1},{2,6},{6,10},{... | collective-permute-start | bytes 589832 | tf_op jit(solution)/shard_map/ppermute | solution.py:183
  94.3 12.8 %collective-permute-done.6 = bf16[128,768]{1,0:T(8,128)(2,1)S(1)} collective-permute-done((bf16[128,768]{1,0:T(8,128)(2,1)S(1)}, bf16[128,768]{1,0:T(8,128)(2,1)S(1)}, u32[]{:S(2)}, u32[]{:S(2)}) %collective-permute-start.6) | collective-permute-done | bytes 196640 | tf_op jit(solution)/shard_map/ppermute | solution.py:183
  113.9 2.9 %collective-permute-start.8 = (bf16[16,288,128]{2,1,0:T(8,128)(2,1)S(1)}, bf16[16,288,128]{2,1,0:T(8,128)(2,1)}, u32[]{:S(2)}, u32[]{:S(2)}) collective-permute-start(bf16[16,288,128]{2,1,0:T(8,128)(2,1)S(1)} %all-to-all-done.1.same_ref), channel_id=1, source_target_pairs={{0,16},{16,0},{1,17},{17,1},{2,18},{18,2},{3,19},{19,3},{4,20},{20... | collective-permute-start | bytes 3538952 | tf_op jit(solution)/shard_map/ppermute | solution.py:222
  116.8 2.5 %collective-permute-done.8.other_ref = bf16[16,288,128]{2,1,0:T(8,128)(2,1)} collective-permute-done((bf16[16,288,128]{2,1,0:T(8,128)(2,1)S(1)}, bf16[16,288,128]{2,1,0:T(8,128)(2,1)}, u32[]{:S(2)}, u32[]{:S(2)}) %collective-permute-start.8) | collective-permute-done | bytes 1179680 | tf_op jit(solution)/shard_map/ppermute | solution.py:222
  122.2 3.2 %project.1 = (bf16[4,512,256]{2,1,0:T(8,128)(2,1)S(1)}, bf16[288,1024]{1,0:T(8,128)(2,1)S(1)}) custom-call(s32[3]{0:T(128)S(1)} %pad_add_fusion.place_ref, bf16[512,1152]{1,0:T(8,128)(2,1)S(1)} %copy-done.6, f32[512,1024]{1,0:T(8,128)S(1)} %copy-done.4, bf16[16,288,128]{2,1,0:T(8,128)(2,1)S(1)} %all-to-all-done.1.same_ref, ...), custom_call_target="tpu_custom_call" | custom-call | tf_op jit(solution)/shard_map/project/pallas_call | solution.py:102
  126.4 4.1 %all-to-all-start.2 = ((bf16[4,512,256]{2,1,0:T(8,128)(2,1)}), bf16[4,512,256]{2,1,0:T(8,128)(2,1)S(1)}, u32[]{:S(2)}, u32[]{:S(2)}) async-start(bf16[4,512,256]{2,1,0:T(8,128)(2,1)} %copy-done.8), calls=%async_computation.2 | async-start | bytes 2097152 | tf_op jit(solution)/shard_map/all_to_all | solution.py:193
  131.2 24.6 %all-to-all-done.2 = bf16[4,512,256]{2,1,0:T(8,128)(2,1)S(1)} async-done(((bf16[4,512,256]{2,1,0:T(8,128)(2,1)}), bf16[4,512,256]{2,1,0:T(8,128)(2,1)S(1)}, u32[]{:S(2)}, u32[]{:S(2)}) %all-to-all-start.2) | async-done | bytes 1048608 | tf_op jit(solution)/shard_map/all_to_all | solution.py:193
  157.1 4.0 %all-to-all-start.3 = ((bf16[4,512,256]{2,1,0:T(8,128)(2,1)}), bf16[4,512,256]{2,1,0:T(8,128)(2,1)S(1)}, u32[]{:S(2)}, u32[]{:S(2)}) async-start(bf16[4,512,256]{2,1,0:T(8,128)(2,1)} %broadcast_in_dim.11), calls=%async_computation.3 | async-start | bytes 2097152 | tf_op jit(solution)/shard_map/all_to_all | solution.py:189
  162.5 12.0 %all-to-all-done.3.keys = bf16[4,512,256]{2,1,0:T(8,128)(2,1)S(1)} async-done(((bf16[4,512,256]{2,1,0:T(8,128)(2,1)}), bf16[4,512,256]{2,1,0:T(8,128)(2,1)S(1)}, u32[]{:S(2)}, u32[]{:S(2)}) %all-to-all-start.3) | async-done | bytes 1048608 | tf_op jit(solution)/shard_map/all_to_all | solution.py:189
  175.7 5.2 %attend.1 = bf16[4,128,512]{2,1,0:T(8,128)(2,1)} custom-call(s32[3]{0:T(128)S(1)} %pad_add_fusion.place_ref, bf16[4,128,768]{2,1,0:T(8,128)(2,1)S(1)} %pad_maximum_fusion.q_ref, bf16[4,512,256]{2,1,0:T(8,128)(2,1)S(1)} %all-to-all-done.3.keys, bf16[4,512,256]{2,1,0:T(8,128)(2,1)S(1)} %copy-done.7), custom_call_target="tpu_custom_call" | custom-call | tf_op jit(solution)/shard_map/attend/pallas_call | solution.py:153
  180.9 3.5 %all-to-all-start.4 = ((bf16[4,128,512]{2,1,0:T(8,128)(2,1)}), bf16[4,128,512]{2,1,0:T(8,128)(2,1)S(1)}, u32[]{:S(2)}, u32[]{:S(2)}) async-start(bf16[4,128,512]{2,1,0:T(8,128)(2,1)} %attend.1), calls=%async_computation.4 | async-start | bytes 1048576 | tf_op jit(solution)/shard_map/all_to_all | solution.py:193
  184.4 2.2 %fusion.3 = bf16[1,288,1024]{2,1,0:T(8,128)(2,1)} fusion(bf16[288,1024]{1,0:T(8,128)(2,1)S(1)} %get-tuple-element.33, bf16[288,1024]{1,0:T(8,128)(2,1)S(1)} %copy-done.1, bf16[8,288,128]{2,1,0:T(8,128)(2,1)} %get-tuple-element.19), kind=kLoop, calls=%fused_computation.7 | loop fusion | flops 2359296 | bytes 2359296 | tf_op jit(solution)/shard_map/broadcast_in_dim | solution.py:235
  186.6 9.4 %all-to-all-done.4 = bf16[4,128,512]{2,1,0:T(8,128)(2,1)S(1)} async-done(((bf16[4,128,512]{2,1,0:T(8,128)(2,1)}), bf16[4,128,512]{2,1,0:T(8,128)(2,1)S(1)}, u32[]{:S(2)}, u32[]{:S(2)}) %all-to-all-start.4) | async-done | bytes 524320 | tf_op jit(solution)/shard_map/all_to_all | solution.py:193
  (65 shorter events, 27.3 us)
Async XLA Ops:
  7.2 100.1 %all-gather.3.cloned.1.call-start = ((), (), s32[]{:S(2)}) async-start(), calls=%async_computation.5 | async-start | bytes 2949120 | tf_op jit(solution)/shard_map/all_gather | solution.py:202
  11.6 10.5 %copy-start.12 = (bf16[1,128,4608]{2,1,0:T(8,128)(2,1)S(1)}, bf16[1,128,4608]{2,1,0:T(8,128)(2,1)}, u32[]{:S(2)}) copy-start(bf16[1,128,4608]{2,1,0:T(8,128)(2,1)} %param.7) | copy-start | bytes 3538948
  11.6 36.1 %all-to-all-start = ((bf16[8,288,128]{2,1,0:T(8,128)(2,1)}), bf16[8,288,128]{2,1,0:T(8,128)(2,1)S(1)}, u32[]{:S(2)}, u32[]{:S(2)}) async-start(bf16[8,288,128]{2,1,0:T(8,128)(2,1)} %get-tuple-element.19), calls=%async_computation | async-start | bytes 1179648 | tf_op jit(solution)/shard_map/all_to_all | solution.py:193
  22.1 49.5 %copy-start.1 = (bf16[288,1024]{1,0:T(8,128)(2,1)S(1)}, bf16[288,1024]{1,0:T(8,128)(2,1)}, u32[]{:S(2)}) copy-start(bf16[288,1024]{1,0:T(8,128)(2,1)} %base_ref.1) | copy-start | bytes 1769476
  22.2 12.3 %collective-permute-start = (bf16[128,1152]{1,0:T(8,128)(2,1)S(1)}, bf16[128,1152]{1,0:T(8,128)(2,1)S(1)}, u32[]{:S(2)}, u32[]{:S(2)}) collective-permute-start(bf16[128,1152]{1,0:T(8,128)(2,1)S(1)} %get-tuple-element.41), channel_id=1, source_target_pairs={{0,4},{4,8},{8,12},{12,0},{1,5},{5,9},{9,13},{13,1},{2,6},{6,10},{... | collective-permute-start | bytes 884744 | tf_op jit(solution)/shard_map/ppermute | solution.py:183
  24.2 23.5 %collective-permute-start.1 = (bf16[128,1152]{1,0:T(8,128)(2,1)S(1)}, bf16[128,1152]{1,0:T(8,128)(2,1)S(1)}, u32[]{:S(2)}, u32[]{:S(2)}) collective-permute-start(bf16[128,1152]{1,0:T(8,128)(2,1)S(1)} %get-tuple-element.43), channel_id=1, source_target_pairs={{0,8},{4,12},{8,0},{12,4},{1,9},{5,13},{9,1},{13,5},{2,10},{6,14},... | collective-permute-start | bytes 884744 | tf_op jit(solution)/shard_map/ppermute | solution.py:183
  26.3 21.5 %collective-permute-start.2 = (bf16[128,1152]{1,0:T(8,128)(2,1)S(1)}, bf16[128,1152]{1,0:T(8,128)(2,1)S(1)}, u32[]{:S(2)}, u32[]{:S(2)}) collective-permute-start(bf16[128,1152]{1,0:T(8,128)(2,1)S(1)} %get-tuple-element.40), channel_id=1, source_target_pairs={{0,12},{4,0},{8,4},{12,8},{1,13},{5,1},{9,5},{13,9},{2,14},{6,2},{... | collective-permute-start | bytes 884744 | tf_op jit(solution)/shard_map/ppermute | solution.py:183
  47.7 26.0 %copy-start.10 = (bf16[128,1152]{1,0:T(8,128)(2,1)}, bf16[128,1152]{1,0:T(8,128)(2,1)S(1)}, u32[]{:S(2)}) copy-start(bf16[128,1152]{1,0:T(8,128)(2,1)S(1)} %collective-permute-done.2.h3_ref) | copy-start | bytes 884740
  47.8 9.0 %collective-permute-start.3 = (bf16[288,128]{1,0:T(8,128)(2,1)S(1)}, bf16[288,128]{1,0:T(8,128)(2,1)S(1)}, u32[]{:S(2)}, u32[]{:S(2)}) collective-permute-start(bf16[288,128]{1,0:T(8,128)(2,1)S(1)} %reduce_sum.21), channel_id=1, source_target_pairs={{0,32},{64,96},{32,0},{96,64},{1,33},{65,97},{33,1},{97,65},{2,34}... | collective-permute-start | bytes 221192 | tf_op jit(solution)/shard_map/ppermute | solution.py:165
  56.9 14.7 %collective-permute-start.4 = (bf16[288,128]{1,0:T(8,128)(2,1)S(1)}, bf16[288,128]{1,0:T(8,128)(2,1)S(1)}, u32[]{:S(2)}, u32[]{:S(2)}) collective-permute-start(bf16[288,128]{1,0:T(8,128)(2,1)S(1)} %add_convert_fusion), channel_id=1, source_target_pairs={{32,64},{96,0},{64,32},{0,96},{33,65},{97,1},{65,33},{1,97},{34,66... | collective-permute-start | bytes 221192 | tf_op jit(solution)/shard_map/ppermute | solution.py:165
  73.7 6.6 %copy-start.14 = (bf16[1,128,1024]{2,1,0:T(8,128)(2,1)S(1)}, bf16[1,128,1024]{2,1,0:T(8,128)(2,1)}, u32[]{:S(2)}) copy-start(bf16[1,128,1024]{2,1,0:T(8,128)(2,1)} %param.9) | copy-start | bytes 786436
  73.7 6.7 %copy-start.13 = (bf16[1,128,2048]{2,1,0:T(8,128)(2,1)S(1)}, bf16[1,128,2048]{2,1,0:T(8,128)(2,1)}, u32[]{:S(2)}) copy-start(bf16[1,128,2048]{2,1,0:T(8,128)(2,1)} %param.8) | copy-start | bytes 1572868
  73.7 40.1 %all-to-all-start.1 = ((bf16[16,288,128]{2,1,0:T(8,128)(2,1)}), bf16[16,288,128]{2,1,0:T(8,128)(2,1)S(1)}, u32[]{:S(2)}, u32[]{:S(2)}) async-start(bf16[16,288,128]{2,1,0:T(8,128)(2,1)} %broadcast_in_dim.9), calls=%async_computation.1 | async-start | bytes 2359296 | tf_op jit(solution)/shard_map/all_to_all | solution.py:189
  80.5 13.8 %collective-permute-start.7 = (bf16[128,768]{1,0:T(8,128)(2,1)S(1)}, bf16[128,768]{1,0:T(8,128)(2,1)S(1)}, u32[]{:S(2)}, u32[]{:S(2)}) collective-permute-start(bf16[128,768]{1,0:T(8,128)(2,1)S(1)} %pad_maximum_fusion.3), channel_id=1, source_target_pairs={{0,12},{4,0},{8,4},{12,8},{1,13},{5,1},{9,5},{13,9},{2,14},{6,2},{... | collective-permute-start | bytes 589832 | tf_op jit(solution)/shard_map/ppermute | solution.py:183
  90.1 17.0 %collective-permute-start.6 = (bf16[128,768]{1,0:T(8,128)(2,1)S(1)}, bf16[128,768]{1,0:T(8,128)(2,1)S(1)}, u32[]{:S(2)}, u32[]{:S(2)}) collective-permute-start(bf16[128,768]{1,0:T(8,128)(2,1)S(1)} %pad_maximum_fusion.2), channel_id=1, source_target_pairs={{0,8},{4,12},{8,0},{12,4},{1,9},{5,13},{9,1},{13,5},{2,10},{6,14},... | collective-permute-start | bytes 589832 | tf_op jit(solution)/shard_map/ppermute | solution.py:183
  92.1 15.1 %collective-permute-start.5 = (bf16[128,768]{1,0:T(8,128)(2,1)S(1)}, bf16[128,768]{1,0:T(8,128)(2,1)S(1)}, u32[]{:S(2)}, u32[]{:S(2)}) collective-permute-start(bf16[128,768]{1,0:T(8,128)(2,1)S(1)} %pad_maximum_fusion.1), channel_id=1, source_target_pairs={{0,4},{4,8},{8,12},{12,0},{1,5},{5,9},{9,13},{13,1},{2,6},{6,10},{... | collective-permute-start | bytes 589832 | tf_op jit(solution)/shard_map/ppermute | solution.py:183
  107.3 1.7 copy-start.2
  111.5 1.4 copy-start.3
  113.9 5.5 %collective-permute-start.8 = (bf16[16,288,128]{2,1,0:T(8,128)(2,1)S(1)}, bf16[16,288,128]{2,1,0:T(8,128)(2,1)}, u32[]{:S(2)}, u32[]{:S(2)}) collective-permute-start(bf16[16,288,128]{2,1,0:T(8,128)(2,1)S(1)} %all-to-all-done.1.same_ref), channel_id=1, source_target_pairs={{0,16},{16,0},{1,17},{17,1},{2,18},{18,2},{3,19},{19,3},{4,20},{20... | collective-permute-start | bytes 3538952 | tf_op jit(solution)/shard_map/ppermute | solution.py:222
  119.3 1.6 copy-start.4
  126.4 29.5 %all-to-all-start.2 = ((bf16[4,512,256]{2,1,0:T(8,128)(2,1)}), bf16[4,512,256]{2,1,0:T(8,128)(2,1)S(1)}, u32[]{:S(2)}, u32[]{:S(2)}) async-start(bf16[4,512,256]{2,1,0:T(8,128)(2,1)} %copy-done.8), calls=%async_computation.2 | async-start | bytes 2097152 | tf_op jit(solution)/shard_map/all_to_all | solution.py:193
  130.5 32.0 %all-gather.5.cloned.1.call-start = ((), (), s32[]{:S(2)}) async-start(), calls=%async_computation.6 | async-start | bytes 1310720 | tf_op jit(solution)/shard_map/all_gather | solution.py:225
  157.1 17.4 %all-to-all-start.3 = ((bf16[4,512,256]{2,1,0:T(8,128)(2,1)}), bf16[4,512,256]{2,1,0:T(8,128)(2,1)S(1)}, u32[]{:S(2)}, u32[]{:S(2)}) async-start(bf16[4,512,256]{2,1,0:T(8,128)(2,1)} %broadcast_in_dim.11), calls=%async_computation.3 | async-start | bytes 2097152 | tf_op jit(solution)/shard_map/all_to_all | solution.py:189
  180.9 15.1 %all-to-all-start.4 = ((bf16[4,128,512]{2,1,0:T(8,128)(2,1)}), bf16[4,128,512]{2,1,0:T(8,128)(2,1)S(1)}, u32[]{:S(2)}, u32[]{:S(2)}) async-start(bf16[4,128,512]{2,1,0:T(8,128)(2,1)} %attend.1), calls=%async_computation.4 | async-start | bytes 1048576 | tf_op jit(solution)/shard_map/all_to_all | solution.py:193
  (7 other events, 7.6 us)
Sparse Core Ops, SparseCore 0:
  11.7 46.0 all-gather.2
  134.0 28.4 all-gather.4

commit v3 on v2

v3 whole, which is shorter than its diff:
```python
import math

import jax
import jax.numpy as jnp
from jax import lax
from jax.experimental import pallas as pl
from jax.experimental.pallas import tpu as pltpu
from jax.sharding import Mesh
from jax.sharding import PartitionSpec as P

D = 4608
HD = 128
QH = 16
KVH = 8
BLOCK = 128
KC = 1024
VMEM = pl.BlockSpec(memory_space=pltpu.VMEM)
SMEM = pl.BlockSpec(memory_space=pltpu.SMEM)
ANY = pl.BlockSpec(memory_space=pl.ANY)

momentum_rate = 0.9
outer_rate = 0.7
blend_share = 0.25
logit_cap = 50.0
query_scalar = 12.0

NX, NZH, NC, NZL, NY = 4, 4, 2, 4, 4


def params(mib=58):
    return pltpu.CompilerParams(vmem_limit_bytes=mib << 20)


def start_all(copies):
    for copy in copies:
        copy.start()
    return copies


def prep_kernel(codes_hbm, exps_ref, base_hbm, delta_ref, part_ref, codes, base, sems):
    half = codes.shape[0] // 2
    copies = []
    for i in range(2):
        rows = pl.ds(i * half, half)
        copies.append(pltpu.make_async_copy(codes_hbm.at[rows], codes.at[rows], sems.at[2 * i]))
        copies.append(pltpu.make_async_copy(base_hbm.at[rows], base.at[rows], sems.at[2 * i + 1]))
    start_all(copies)
    factor = jnp.exp2(exps_ref[...].astype(jnp.float32)).T
    for i in range(2):
        copies[2 * i].wait()
        copies[2 * i + 1].wait()
        rows = slice(i * half, (i + 1) * half)
        for j in range(KC // BLOCK):
            cols = slice(j * BLOCK, (j + 1) * BLOCK)
            delta = codes[rows, cols].astype(jnp.float32) * factor[rows, j : j + 1]
            delta_ref[j, rows] = delta.astype(jnp.bfloat16)
            part_ref[rows, cols] = (base[rows, cols].astype(jnp.float32) - delta).astype(
                jnp.bfloat16
            )


def prep(codes, exps, base):
    rows = codes.shape[0]
    return pl.pallas_call(
        prep_kernel,
        out_shape=(
            jax.ShapeDtypeStruct((KC // BLOCK, rows, BLOCK), jnp.bfloat16),
            jax.ShapeDtypeStruct((rows, KC), jnp.bfloat16),
        ),
        in_specs=[ANY, VMEM, ANY],
        out_specs=(VMEM, VMEM),
        scratch_shapes=[
            pltpu.VMEM((rows, KC), jnp.bfloat16),
            pltpu.VMEM((rows, KC), jnp.bfloat16),
            pltpu.SemaphoreType.DMA((4,)),
        ],
        compiler_params=params(),
        name="prep",
    )(codes, exps.T, base)


def step_kernel(place_ref, mine_ref, sent_ref, base_ref, momentum_ref, out_ref):
    mean = (mine_ref[...].astype(jnp.float32) + sent_ref[...].astype(jnp.float32)) * (
        1.0 / (NX * NZH * NC)
    )
    moment_new = momentum_rate * momentum_ref[...].astype(jnp.float32) + mean
    outer = base_ref[...].astype(jnp.float32) - outer_rate * (mean + momentum_rate * moment_new)
    outer = outer.astype(jnp.bfloat16)
    for i in range(out_ref.shape[0]):
        out_ref[i] = outer


def outer_step(place, mine, sent, base, momentum):
    rows = mine.shape[0]
    whole = pl.BlockSpec((rows, BLOCK), lambda i, p: (0, 0))
    block = pl.BlockSpec((rows, BLOCK), lambda i, p: (0, p[3]))
    return pl.pallas_call(
        step_kernel,
        out_shape=jax.ShapeDtypeStruct((NX * NY, rows, BLOCK), jnp.bfloat16),
        grid_spec=pltpu.PrefetchScalarGridSpec(
            num_scalar_prefetch=1,
            grid=(1,),
            in_specs=[whole, whole, block, block],
            out_specs=pl.BlockSpec((NX * NY, rows, BLOCK), lambda i, p: (0, 0, 0)),
        ),
        compiler_params=params(20),
        name="outer_step",
    )(place, mine, sent, base, momentum)


def project_kernel(place_ref, *refs):
    hidden_any, (part_any, same_any, other_any) = refs[:4], refs[4:7]
    out_ref, hidden, parts, outer, weight, part_sems, sems, hidden_sems = refs[7:]
    rows = outer.shape[1]
    c, z = place_ref[0], place_ref[1]
    part_copies, outer_copies, hidden_copies = [], [], []
    for n in range(NZL):
        cols = pl.ds(n * 2 * BLOCK, 2 * BLOCK)
        part_copies.append(
            pltpu.make_async_copy(part_any.at[:, cols], parts.at[n], part_sems.at[n])
        )
        for near, source in enumerate((same_any, other_any)):
            half = lax.rem(c + near, NC)
            at = pl.ds((n * NC + half) * NY, NY)
            outer_copies.append(
                pltpu.make_async_copy(
                    source.at[pl.ds(n * NY, NY)], outer.at[at], sems.at[n * NC + near]
                )
            )
    for s in range(NZL):
        to = pl.ds(pl.multiple_of(lax.rem(z - s + NZL, NZL) * 128, 128), 128)
        hidden_copies.append(
            pltpu.make_async_copy(hidden_any[s], hidden.at[to], hidden_sems.at[s])
        )
    start_all([part_copies[0]] + outer_copies[:2] + hidden_copies)
    for n in range(1, NZL):
        start_all([part_copies[n]] + outer_copies[2 * n : 2 * n + 2])
    for n in range(NZL):
        for copy in [part_copies[n]] + outer_copies[2 * n : 2 * n + 2]:
            copy.wait()
        for half in range(NC):
            cols = slice(half * BLOCK, (half + 1) * BLOCK)
            for y in range(NY):
                at = slice(y * rows, (y + 1) * rows)
                blend = blend_share * parts[n, at, cols].astype(jnp.float32)
                piece = outer[(n * NC + half) * NY + y].astype(jnp.float32)
                blend += (1.0 - blend_share) * piece
                weight[n, at, cols] = blend.astype(jnp.bfloat16)
        if n == 0:
            for copy in hidden_copies:
                copy.wait()
        keys = jnp.dot(hidden[...], weight[n], preferred_element_type=jnp.float32)
        out_ref[n] = keys.astype(jnp.bfloat16)


def project(place, hidden, part, same, other):
    rows = same.shape[1]
    depth = NY * rows
    return pl.pallas_call(
        project_kernel,
        out_shape=jax.ShapeDtypeStruct((NZL, 512, 2 * BLOCK), jnp.bfloat16),
        in_specs=[SMEM] + [ANY] * 7,
        out_specs=VMEM,
        scratch_shapes=[
            pltpu.VMEM((512, depth), jnp.bfloat16),
            pltpu.VMEM((NZL, depth, 2 * BLOCK), jnp.bfloat16),
            pltpu.VMEM((NZL * NC * NY, rows, BLOCK), jnp.bfloat16),
            pltpu.VMEM((NZL, depth, 2 * BLOCK), jnp.bfloat16),
            pltpu.SemaphoreType.DMA((NZL,)),
            pltpu.SemaphoreType.DMA((NZL * NC,)),
            pltpu.SemaphoreType.DMA((NZL,)),
        ],
        compiler_params=params(48),
        name="project",
    )(place, *hidden, part, same, other)


def reduce_kernel(sums_ref, out_ref):
    total = sums_ref[0].astype(jnp.float32)
    for i in range(1, NZL):
        total += sums_ref[i].astype(jnp.float32)
    keys = (total * (1.0 / math.sqrt(D))).astype(jnp.bfloat16)
    for i in range(NY):
        out_ref[i] = keys


def reduce_keys(sums):
    return pl.pallas_call(
        reduce_kernel,
        out_shape=jax.ShapeDtypeStruct((NY,) + sums.shape[1:], jnp.bfloat16),
        in_specs=[VMEM],
        out_specs=VMEM,
        compiler_params=params(20),
        name="reduce_keys",
    )(sums)


def blend_kernel(place_ref, delta_ref, base_ref, same_ref, other_ref, out_ref):
    c = place_ref[0]
    for x in range(NX):
        for near, ref in enumerate((same_ref, other_ref)):
            j = x * NC + lax.rem(c + near, NC)
            cols = pl.ds(pl.multiple_of(j * BLOCK, BLOCK), BLOCK)
            mine = base_ref[:, cols].astype(jnp.float32) - delta_ref[j].astype(jnp.float32)
            outer = ref[x, 0].astype(jnp.float32)
            blend = blend_share * mine + (1.0 - blend_share) * outer
            out_ref[:, cols] = blend.astype(jnp.bfloat16)


def blend(place, delta, base, same, other):
    rows = base.shape[0]
    piece = pl.BlockSpec((NX, 1, rows, BLOCK), lambda i, p: (0, p[2], 0, 0))
    split = (NX, NY, rows, BLOCK)
    return pl.pallas_call(
        blend_kernel,
        out_shape=jax.ShapeDtypeStruct((rows, KC), jnp.bfloat16),
        grid_spec=pltpu.PrefetchScalarGridSpec(
            num_scalar_prefetch=1,
            grid=(1,),
            in_specs=[
                pl.BlockSpec(delta.shape, lambda i, p: (0, 0, 0)),
                pl.BlockSpec((rows, KC), lambda i, p: (0, 0)),
                piece,
                piece,
            ],
            out_specs=pl.BlockSpec((rows, KC), lambda i, p: (0, 0)),
        ),
        compiler_params=params(20),
        name="blend",
    )(place, delta, base, same.reshape(split), other.reshape(split))


def attend_kernel(place_ref, *refs):
    pieces, keys_any, values_any = refs[:4], refs[4], refs[5:9]
    out_ref, queries, keys, values, query_sems, key_sems, value_sems = refs[9:]
    z, y = place_ref[1], place_ref[2]
    query_copies, key_copies, value_copies = [], [], []
    for s, ref in enumerate(pieces):
        at = lax.rem(z - s + NZL, NZL)
        query_copies.append(
            pltpu.make_async_copy(ref.at[:, pl.ds(0, 4 * HD)], queries.at[at], query_sems.at[s])
        )
    for zk in range(NZL):
        rows = pl.ds(zk * 128, 128)
        key_copies.append(
            pltpu.make_async_copy(keys_any.at[:, rows], keys.at[:, rows], key_sems.at[zk])
        )
        rows = pl.ds(pl.multiple_of(lax.rem(z - zk + NZL, NZL) * 128, 128), 128)
        for s in range(NY):
            value_copies.append(
                pltpu.make_async_copy(
                    values_any[s].at[rows],
                    values.at[zk, lax.rem(y - s + NY, NY)],
                    value_sems.at[zk, s],
                )
            )
    start_all(query_copies)
    for zk in range(NZL):
        start_all([key_copies[zk]] + value_copies[zk * NY : (zk + 1) * NY])
    row = lax.broadcasted_iota(jnp.int32, (256, 128), 0) % 128
    col = lax.broadcasted_iota(jnp.int32, (256, 128), 1)
    seen = col - row
    for copy in query_copies:
        copy.wait()
    for zq in range(NZL):
        for copy in [key_copies[zq]] + value_copies[zq * NY : (zq + 1) * NY]:
            copy.wait()
        for half in range(2):
            head = 2 * half * HD
            cols = slice(half * HD, (half + 1) * HD)
            q = jnp.concatenate(
                [queries[zq, :, head : head + HD], queries[zq, :, head + HD : head + 2 * HD]],
                axis=0,
            )
            acc = jnp.zeros((256, HD), jnp.float32)
            total = jnp.zeros((256, 128), jnp.float32)
            for zk in range(zq + 1):
                rows = slice(zk * 128, (zk + 1) * 128)
                for s in range(NY):
                    scores = lax.dot_general(
                        q,
                        keys[s, rows, cols],
                        (((1,), (1,)), ((), ())),
                        preferred_element_type=jnp.float32,
                    )
                    p = jnp.exp(
                        logit_cap * jnp.tanh(scores * (1.0 / (query_scalar * logit_cap)))
                    )
                    if zk == zq:
                        p = jnp.where(seen <= (y - s) * 128, p, 0.0)
                    total += p
                    acc += jnp.dot(
                        p.astype(jnp.bfloat16),
                        values[zk, s, :, cols],
                        preferred_element_type=jnp.float32,
                    )
            out = (acc / jnp.sum(total, axis=1, keepdims=True)).astype(jnp.bfloat16)
            out_ref[zq, :, head : head + HD] = out[:128]
            out_ref[zq, :, head + HD : head + 2 * HD] = out[128:]


def attend(place, queries, keys, values):
    return pl.pallas_call(
        attend_kernel,
        out_shape=jax.ShapeDtypeStruct((NZL, 128, 4 * HD), jnp.bfloat16),
        in_specs=[SMEM] + [ANY] * 9,
        out_specs=VMEM,
        scratch_shapes=[
            pltpu.VMEM((NZL, 128, 4 * HD), jnp.bfloat16),
            pltpu.VMEM((NY, 512, 2 * HD), jnp.bfloat16),
            pltpu.VMEM((NZL, NY, 128, 2 * HD), jnp.bfloat16),
            pltpu.SemaphoreType.DMA((NZL,)),
            pltpu.SemaphoreType.DMA((NZL,)),
            pltpu.SemaphoreType.DMA((NZL, NY)),
        ],
        compiler_params=params(20),
        name="attend",
    )(place, *queries, keys, *values)


def lay_kernel(mixed_any, out_any, sems):
    width = mixed_any.shape[2]
    copies = []
    for z in range(NZL):
        cols = pl.ds(z * width, width)
        copies.append(pltpu.make_async_copy(mixed_any.at[z], out_any.at[:, cols], sems.at[z]))
    for copy in start_all(copies):
        copy.wait()


def lay(mixed):
    places, rows, width = mixed.shape
    return pl.pallas_call(
        lay_kernel,
        out_shape=jax.ShapeDtypeStruct((rows, places * width), jnp.bfloat16),
        in_specs=[ANY],
        out_specs=ANY,
        scratch_shapes=[pltpu.SemaphoreType.DMA((NZL,))],
        compiler_params=params(20),
        name="lay",
    )(mixed)


def swap(array, axis, pairs):
    return lax.ppermute(array, axis, pairs + [(b, a) for a, b in pairs])


def add(a, b):
    return a.astype(jnp.float32) + b.astype(jnp.float32)


def deal(arrays, axis):
    at = lax.axis_index(axis)
    pieces = []
    for step in range(4):
        to = lax.rem(at + step, 4)
        cut = []
        for array in arrays:
            width = array.shape[1] // 4
            cut.append(lax.dynamic_slice_in_dim(array, to * width, width, 1))
        piece = jnp.concatenate(cut, axis=1)
        if step:
            piece = lax.ppermute(piece, axis, [(i, (i + step) % 4) for i in range(4)])
        pieces.append(piece)
    return pieces


def from_ring(array, axis):
    shifts = [[(i, (i + step) % 4) for i in range(4)] for step in (1, 2, 3)]
    return [array] + [lax.ppermute(array, axis, shift) for shift in shifts]


def exchange(array, axis):
    return lax.all_to_all(array, axis, 0, 0, tiled=True)


def on_device(hidden, queries, values, codes, exponents, base, momentum):
    x, c, z, y = (lax.axis_index(name) for name in ("x", "c", "zl", "y"))
    place = jnp.stack([c, z, y, x * NC + c]).astype(jnp.int32)

    delta, part = prep(codes[0], exponents[0], base)
    part_all = lax.all_gather(part, "y", axis=0, tiled=True)

    sent = exchange(delta, ("x", "c"))
    hidden_here = deal([hidden[0]], "zl")
    sent, hidden_here[1] = lax.optimization_barrier((sent, hidden_here[1]))
    eighth = jnp.sum(sent.astype(jnp.float32), axis=0).astype(jnp.bfloat16)
    pair = add(eighth, swap(eighth, "zh", [(0, 1), (2, 3)])).astype(jnp.bfloat16)
    swapped = swap(pair, "zh", [(1, 2), (3, 0)])
    swapped, hidden_here[2], hidden_here[3] = lax.optimization_barrier(
        (swapped, hidden_here[2], hidden_here[3])
    )
    outer = outer_step(place, pair, swapped, base, momentum)

    queries_in, values_in, outer = lax.optimization_barrier((queries[0], values[0], outer))
    both = deal([queries_in, values_in], "zl")

    same = exchange(outer, ("x", "y"))
    value_here = jnp.concatenate([piece[:, 512:] for piece in both])
    same, value_here, *both = lax.optimization_barrier((same, value_here, *both))
    other = lax.ppermute(same, "c", [(0, 1), (1, 0)])

    sums = project(place, hidden_here, part_all, same, other)
    sums, value_here = lax.optimization_barrier((sums, value_here))
    sums = exchange(sums, "zl")
    value_all = from_ring(value_here, "y")
    blended = blend(place, delta, base, same, other)
    sums, blended, *value_all = lax.optimization_barrier((sums, blended, *value_all))
    keys = exchange(reduce_keys(sums), "y")
    mixed = exchange(attend(place, both, keys, value_all), "zl")
    return blended[None], lay(mixed)[None]


def solution(mesh):
    split = Mesh(
        mesh.devices.reshape(NX, NZH, NC, NZL, NY),
        ("x", "zh", "c", "zl", "y"),
    )
    replica, fsdp = ("x", "zh", "c"), ("zl", "y")
    stacked = P(replica, fsdp, None)
    return jax.shard_map(
        on_device,
        mesh=split,
        in_specs=(stacked,) * 5 + (P(fsdp, None),) * 2,
        out_specs=(stacked, stacked),
        check_vma=False,
    )
```

time: 208 us -> 196 us (0.942)
  waiting for transfers between devices: 89.7 us -> 46.1 us
  blocking collectives: 0 us -> 33.2 us
  local copies, waits for them, and re-layouts: 17.4 us -> 6.05 us
  Pallas kernels: 11.3 us -> 21.3 us
  starting transfers between devices: 67.7 us -> 71.2 us
    all_to_all x0 -> x2, blocking collectives: none -> 33.2 us  [exchange(): return lax.all_to_all(array, axis, 0, 0, tiled=True)]
    all_to_all x3, waiting for transfers between devices: 34.1 us -> 2.81 us  [exchange(): return lax.all_to_all(array, axis, 0, 0, tiled=True)]
    all_to_all x2 -> x0, waiting for transfers between devices: 12 us -> none  [gather(): lax.all_to_all(jnp.broadcast_to(array, (size,) + array.shape), axis, 0, 0...]
    all_to_all x2 -> x0, starting transfers between devices: 10.5 us -> none  [gather(): lax.all_to_all(jnp.broadcast_to(array, (size,) + array.shape), axis, 0, 0...]
    ppermute x0 -> x3, starting transfers between devices: none -> 9.38 us  [from_ring(): return [array] + [lax.ppermute(array, axis, shift) for shift in shifts]]
    ppermute x0 -> x3, waiting for transfers between devices: none -> 9.15 us  [from_ring(): return [array] + [lax.ppermute(array, axis, shift) for shift in shifts]]
    unnamed x32 -> x50, local copies, waits for them, and re-layouts: 14 us -> 5.12 us
    ppermute x2, waiting for transfers between devices: 10.4 us -> 1.97 us  [swap(): return lax.ppermute(array, axis, pairs + [(b, a) for a, b in pairs])]
  transfers between devices with their start and end apart: 16 -> 16, of which waited for: 10 -> 8; matrix products, arithmetic and copies ran while one was open for 3% -> 1% of each run, Pallas kernels for 1% -> 2%
where the time goes in v3:
time: 196 us; the launch traced here: 194 us
  starting transfers between devices  71.2 us (36%)
  waiting for transfers between devices  46.1 us (24%)
  blocking collectives  33.2 us (17%)
  Pallas kernels  21.3 us (11%)
  between operations  14.5 us (7%)
  local copies, waits for them, and re-layouts  6.05 us (3%)
    all_to_all x2, blocking collectives, exchange(): return lax.all_to_all(array, axis, 0, 0, tiled=True)  33.2 us
    ppermute x6, waiting for transfers between devices, deal(): piece = lax.ppermute(piece, axis, [(i, (i + step) % 4) for i in range(4)])  29.7 us
    ppermute x6, starting transfers between devices, deal(): piece = lax.ppermute(piece, axis, [(i, (i + step) % 4) for i in range(4)])  24.4 us
    all_to_all x3, starting transfers between devices, exchange(): return lax.all_to_all(array, axis, 0, 0, tiled=True)  22.2 us
    ppermute x2, starting transfers between devices, swap(): return lax.ppermute(array, axis, pairs + [(b, a) for a, b in pairs])  11.6 us
    ppermute x3, starting transfers between devices, from_ring(): return [array] + [lax.ppermute(array, axis, shift) for shift in shifts]  9.38 us
    ppermute x3, waiting for transfers between devices, from_ring(): return [array] + [lax.ppermute(array, axis, shift) for shift in shifts]  9.15 us
    pallas_call x1, Pallas kernels, attend(): pl.pallas_call(attend_kernel, out_shape=jax.ShapeDtypeStruct((NZL, 128, 4...  6.58 us
  transfers between devices with their start and end apart: 16, of which 8 were waited for; matrix products, arithmetic and copies ran while one was open for 1% of the time, Pallas kernels for 2%

profile of v3, /device:TPU:1, one launch (start us, length us, event | category | flops | bytes accessed | tf_op | source)
XLA Modules:
  0.0 194.1 jit_solution(4926591876189530877)
XLA Ops:
  7.2 3.3 %prep.1 = (bf16[8,288,128]{2,1,0:T(8,128)(2,1)}, bf16[288,1024]{1,0:T(8,128)(2,1)}) custom-call(bf16[288,1024]{1,0:T(8,128)(2,1)} %bitcast.25, s32[8,288]{1,0:T(8,128)} %bitcast.29, bf16[288,1024]{1,0:T(8,128)(2,1)} %base_ref.3), custom_call_target="tpu_custom_call" | custom-call | tf_op jit(solution)/shard_map/prep/pallas_call | solution.py:64
  10.5 10.5 %all-to-all-start = ((bf16[8,288,128]{2,1,0:T(8,128)(2,1)}), bf16[8,288,128]{2,1,0:T(8,128)(2,1)S(1)}, u32[]{:S(2)}, u32[]{:S(2)}) async-start(bf16[8,288,128]{2,1,0:T(8,128)(2,1)} %get-tuple-element.26.delta_ref), calls=%async_computation | async-start | bytes 1179648 | tf_op jit(solution)/shard_map/all_to_all | solution.py:374
  23.7 10.2 %collective-permute-done.refs_1_ = bf16[128,1152]{1,0:T(8,128)(2,1)S(1)} collective-permute-done((bf16[128,1152]{1,0:T(8,128)(2,1)S(1)}, bf16[128,1152]{1,0:T(8,128)(2,1)S(1)}, u32[]{:S(2)}, u32[]{:S(2)}) %collective-permute-start) | collective-permute-done | bytes 294944 | tf_op jit(solution)/shard_map/ppermute | solution.py:363
  34.0 5.8 %collective-permute-start.1 = (bf16[288,128]{1,0:T(8,128)(2,1)S(1)}, bf16[288,128]{1,0:T(8,128)(2,1)S(1)}, u32[]{:S(2)}, u32[]{:S(2)}) collective-permute-start(bf16[288,128]{1,0:T(8,128)(2,1)S(1)} %reduce_sum.12), channel_id=1, source_target_pairs={{0,32},{64,96},{32,0},{96,64},{1,33},{65,97},{33,1},{97,65},{2,34}... | collective-permute-start | bytes 221192 | tf_op jit(solution)/shard_map/ppermute | solution.py:345
  39.8 3.2 %collective-permute-start.4 = (bf16[128,1152]{1,0:T(8,128)(2,1)}, bf16[128,1152]{1,0:T(8,128)(2,1)S(1)}, u32[]{:S(2)}, u32[]{:S(2)}) collective-permute-start(bf16[128,1152]{1,0:T(8,128)(2,1)} %get-tuple-element.50), channel_id=1, source_target_pairs={{0,12},{4,0},{8,4},{12,8},{1,13},{5,1},{9,5},{13,9},{2,14},{6,2},{... | collective-permute-start | bytes 884744 | tf_op jit(solution)/shard_map/ppermute | solution.py:363
  46.9 5.9 %collective-permute-start.2 = (bf16[288,128]{1,0:T(8,128)(2,1)S(1)}, bf16[288,128]{1,0:T(8,128)(2,1)S(1)}, u32[]{:S(2)}, u32[]{:S(2)}) collective-permute-start(bf16[288,128]{1,0:T(8,128)(2,1)S(1)} %add_convert_fusion.mine_ref), channel_id=1, source_target_pairs={{32,64},{96,0},{64,32},{0,96},{33,65},{97,1},{65,33},{1,97},{34,66... | collective-permute-start | bytes 221192 | tf_op jit(solution)/shard_map/ppermute | solution.py:345
  52.9 12.5 %collective-permute-done.3.refs_2_ = bf16[128,1152]{1,0:T(8,128)(2,1)S(1)} collective-permute-done((bf16[128,1152]{1,0:T(8,128)(2,1)S(1)}, bf16[128,1152]{1,0:T(8,128)(2,1)S(1)}, u32[]{:S(2)}, u32[]{:S(2)}) %collective-permute-start.3) | collective-permute-done | bytes 294944 | tf_op jit(solution)/shard_map/ppermute | solution.py:363
  67.2 5.0 %all-to-all-start.1 = ((bf16[16,288,128]{2,1,0:T(8,128)(2,1)}), bf16[16,288,128]{2,1,0:T(8,128)(2,1)S(1)}, u32[]{:S(2)}, u32[]{:S(2)}) async-start(bf16[16,288,128]{2,1,0:T(8,128)(2,1)} %outer_step.1), calls=%async_computation.1 | async-start | bytes 2359296 | tf_op jit(solution)/shard_map/all_to_all | solution.py:374
  72.4 11.5 %collective-permute-start.5 = (bf16[128,768]{1,0:T(8,128)(2,1)S(1)}, bf16[128,768]{1,0:T(8,128)(2,1)S(1)}, u32[]{:S(2)}, u32[]{:S(2)}) collective-permute-start(bf16[128,768]{1,0:T(8,128)(2,1)S(1)} %pad_maximum_fusion.1), channel_id=1, source_target_pairs={{0,4},{4,8},{8,12},{12,0},{1,5},{5,9},{9,13},{13,1},{2,6},{6,10},{... | collective-permute-start | bytes 589832 | tf_op jit(solution)/shard_map/ppermute | solution.py:363
  85.9 4.0 %collective-permute-start.7 = (bf16[128,768]{1,0:T(8,128)(2,1)S(1)}, bf16[128,768]{1,0:T(8,128)(2,1)S(1)}, u32[]{:S(2)}, u32[]{:S(2)}) collective-permute-start(bf16[128,768]{1,0:T(8,128)(2,1)S(1)} %pad_maximum_fusion.3), channel_id=1, source_target_pairs={{0,12},{4,0},{8,4},{12,8},{1,13},{5,1},{9,5},{13,9},{2,14},{6,2},{... | collective-permute-start | bytes 589832 | tf_op jit(solution)/shard_map/ppermute | solution.py:363
  90.6 6.9 %collective-permute-done.6.refs_2_ = bf16[128,768]{1,0:T(8,128)(2,1)S(1)} collective-permute-done((bf16[128,768]{1,0:T(8,128)(2,1)S(1)}, bf16[128,768]{1,0:T(8,128)(2,1)S(1)}, u32[]{:S(2)}, u32[]{:S(2)}) %collective-permute-start.6) | collective-permute-done | bytes 196640 | tf_op jit(solution)/shard_map/ppermute | solution.py:363
  98.4 3.5 %collective-permute-start.8 = (bf16[16,288,128]{2,1,0:T(8,128)(2,1)S(1)}, bf16[16,288,128]{2,1,0:T(8,128)(2,1)S(1)}, u32[]{:S(2)}, u32[]{:S(2)}) collective-permute-start(bf16[16,288,128]{2,1,0:T(8,128)(2,1)S(1)} %all-to-all-done.1.refs_5_), channel_id=1, source_target_pairs={{0,16},{16,0},{1,17},{17,1},{2,18},{18,2},{3,19},{19,3},{4,20},{20... | collective-permute-start | bytes 3538952 | tf_op jit(solution)/shard_map/ppermute | solution.py:401
  101.9 2.5 %collective-permute-done.8.refs_6_ = bf16[16,288,128]{2,1,0:T(8,128)(2,1)S(1)} collective-permute-done((bf16[16,288,128]{2,1,0:T(8,128)(2,1)S(1)}, bf16[16,288,128]{2,1,0:T(8,128)(2,1)S(1)}, u32[]{:S(2)}, u32[]{:S(2)}) %collective-permute-start.8) | collective-permute-done | bytes 1179680 | tf_op jit(solution)/shard_map/ppermute | solution.py:401
  106.3 5.6 %project.1 = bf16[4,512,256]{2,1,0:T(8,128)(2,1)S(1)} custom-call(s32[4]{0:T(128)S(1)} %pad_add_fusion.place_ref, bf16[128,1152]{1,0:T(8,128)(2,1)S(1)} %get-tuple-element.52.refs_0_, bf16[128,1152]{1,0:T(8,128)(2,1)S(1)} %collective-permute-done.refs_1_, bf16[128,1152]{1,0:T(8,128)(2,1)S(1)} %copy-done.15, bf16[128,1152]{1,0:T(8,128)(2,1)S(1)} %copy-done.13, ...), custom_call_target="tpu_custom_call" | custom-call | tf_op jit(solution)/shard_map/project/pallas_call | solution.py:159
  113.0 6.7 %all-to-all-start.2 = ((bf16[4,512,256]{2,1,0:T(8,128)(2,1)}), bf16[4,512,256]{2,1,0:T(8,128)(2,1)}, u32[]{:S(2)}, u32[]{:S(2)}) async-start(bf16[4,512,256]{2,1,0:T(8,128)(2,1)} %copy-done.1), calls=%async_computation.2 | async-start | bytes 2097152 | tf_op jit(solution)/shard_map/all_to_all | solution.py:374
  119.7 4.4 %collective-permute-start.11 = (bf16[512,256]{1,0:T(8,128)(2,1)}, bf16[512,256]{1,0:T(8,128)(2,1)S(1)}, u32[]{:S(2)}, u32[]{:S(2)}) collective-permute-start(bf16[512,256]{1,0:T(8,128)(2,1)} %pad_maximum_fusion.refs_5_), channel_id=1, source_target_pairs={{0,3},{1,0},{2,1},{3,2},{4,7},{5,4},{6,5},{7,6},{8,11},{9,8},{10,9... | collective-permute-start | bytes 786440 | tf_op jit(solution)/shard_map/ppermute | solution.py:370
  124.1 2.5 %collective-permute-start.10 = (bf16[512,256]{1,0:T(8,128)(2,1)}, bf16[512,256]{1,0:T(8,128)(2,1)S(1)}, u32[]{:S(2)}, u32[]{:S(2)}) collective-permute-start(bf16[512,256]{1,0:T(8,128)(2,1)} %pad_maximum_fusion.refs_5_), channel_id=1, source_target_pairs={{0,2},{1,3},{2,0},{3,1},{4,6},{5,7},{6,4},{7,5},{8,10},{9,11},{10,... | collective-permute-start | bytes 786440 | tf_op jit(solution)/shard_map/ppermute | solution.py:370
  126.6 2.5 %collective-permute-start.9 = (bf16[512,256]{1,0:T(8,128)(2,1)}, bf16[512,256]{1,0:T(8,128)(2,1)S(1)}, u32[]{:S(2)}, u32[]{:S(2)}) collective-permute-start(bf16[512,256]{1,0:T(8,128)(2,1)} %pad_maximum_fusion.refs_5_), channel_id=1, source_target_pairs={{0,1},{1,2},{2,3},{3,0},{4,5},{5,6},{6,7},{7,4},{8,9},{9,10},{10,1... | collective-permute-start | bytes 786440 | tf_op jit(solution)/shard_map/ppermute | solution.py:370
  131.7 2.9 %collective-permute-done.10.refs_7_ = bf16[512,256]{1,0:T(8,128)(2,1)S(1)} collective-permute-done((bf16[512,256]{1,0:T(8,128)(2,1)}, bf16[512,256]{1,0:T(8,128)(2,1)S(1)}, u32[]{:S(2)}, u32[]{:S(2)}) %collective-permute-start.10) | collective-permute-done | bytes 262176 | tf_op jit(solution)/shard_map/ppermute | solution.py:370
  135.3 6.2 %collective-permute-done.9.refs_6_ = bf16[512,256]{1,0:T(8,128)(2,1)S(1)} collective-permute-done((bf16[512,256]{1,0:T(8,128)(2,1)}, bf16[512,256]{1,0:T(8,128)(2,1)S(1)}, u32[]{:S(2)}, u32[]{:S(2)}) %collective-permute-start.9) | collective-permute-done | bytes 262176 | tf_op jit(solution)/shard_map/ppermute | solution.py:370
  142.3 2.8 %all-to-all-done.2.sums_ref = bf16[4,512,256]{2,1,0:T(8,128)(2,1)} async-done(((bf16[4,512,256]{2,1,0:T(8,128)(2,1)}), bf16[4,512,256]{2,1,0:T(8,128)(2,1)}, u32[]{:S(2)}, u32[]{:S(2)}) %all-to-all-start.2) | async-done | bytes 1048608 | tf_op jit(solution)/shard_map/all_to_all | solution.py:374
  146.5 17.5 %all_to_all.25.refs_4_ = bf16[4,512,256]{2,1,0:T(8,128)(2,1)S(1)} all-to-all(bf16[4,512,256]{2,1,0:T(8,128)(2,1)S(1)} %reduce_keys.1), channel_id=1, replica_groups=mesh['x'=4,'zh'=4,'c'=2,'zl'=4,'y'=4] {'y'}, dimensions={0} | all-to-all | bytes 2097152 | tf_op jit(solution)/shard_map/all_to_all | solution.py:374
  164.0 6.6 %attend.1 = bf16[4,128,512]{2,1,0:T(8,128)(2,1)S(1)} custom-call(s32[4]{0:T(128)S(1)} %pad_add_fusion.place_ref, bf16[128,768]{1,0:T(8,128)(2,1)S(1)} %copy-done.4, bf16[128,768]{1,0:T(8,128)(2,1)S(1)} %copy-done.7, bf16[128,768]{1,0:T(8,128)(2,1)S(1)} %copy-done.9, bf16[128,768]{1,0:T(8,128)(2,1)S(1)} %copy-done.11, ...), custom_call_target="tpu_custom_call" | custom-call | tf_op jit(solution)/shard_map/attend/pallas_call | solution.py:303
  170.6 15.7 %all_to_all.26.mixed_any = bf16[4,128,512]{2,1,0:T(8,128)(2,1)S(1)} all-to-all(bf16[4,128,512]{2,1,0:T(8,128)(2,1)S(1)} %attend.1), channel_id=1, replica_groups=mesh['x'=4,'zh'=4,'c'=2,'zl'=4,'y'=4] {'zl'}, dimensions={0} | all-to-all | bytes 1048576 | tf_op jit(solution)/shard_map/all_to_all | solution.py:374
  (82 shorter events, 21.4 us)
Async XLA Ops:
  7.2 97.2 %all-gather.2.cloned.1.call-start = ((), (), s32[]{:S(2)}) async-start(), calls=%async_computation.5 | async-start | bytes 2949120 | tf_op jit(solution)/shard_map/all_gather | solution.py:382
  10.5 23.4 %all-to-all-start = ((bf16[8,288,128]{2,1,0:T(8,128)(2,1)}), bf16[8,288,128]{2,1,0:T(8,128)(2,1)S(1)}, u32[]{:S(2)}, u32[]{:S(2)}) async-start(bf16[8,288,128]{2,1,0:T(8,128)(2,1)} %get-tuple-element.26.delta_ref), calls=%async_computation | async-start | bytes 1179648 | tf_op jit(solution)/shard_map/all_to_all | solution.py:374
  21.0 44.4 %copy-start = (bf16[288,1024]{1,0:T(8,128)(2,1)S(1)}, bf16[288,1024]{1,0:T(8,128)(2,1)}, u32[]{:S(2)}) copy-start(bf16[288,1024]{1,0:T(8,128)(2,1)} %base_ref.3) | copy-start | bytes 1769476
  21.0 44.4 %copy-start.5 = (bf16[288,1024]{1,0:T(8,128)(2,1)S(1)}, bf16[288,1024]{1,0:T(8,128)(2,1)}, u32[]{:S(2)}) copy-start(bf16[288,1024]{1,0:T(8,128)(2,1)} %momentum_ref.1) | copy-start | bytes 1769476
  21.8 12.1 %collective-permute-start = (bf16[128,1152]{1,0:T(8,128)(2,1)S(1)}, bf16[128,1152]{1,0:T(8,128)(2,1)S(1)}, u32[]{:S(2)}, u32[]{:S(2)}) collective-permute-start(bf16[128,1152]{1,0:T(8,128)(2,1)S(1)} %get-tuple-element.51), channel_id=1, source_target_pairs={{0,4},{4,8},{8,12},{12,0},{1,5},{5,9},{9,13},{13,1},{2,6},{6,10},{... | collective-permute-start | bytes 884744 | tf_op jit(solution)/shard_map/ppermute | solution.py:363
  34.0 12.8 %collective-permute-start.1 = (bf16[288,128]{1,0:T(8,128)(2,1)S(1)}, bf16[288,128]{1,0:T(8,128)(2,1)S(1)}, u32[]{:S(2)}, u32[]{:S(2)}) collective-permute-start(bf16[288,128]{1,0:T(8,128)(2,1)S(1)} %reduce_sum.12), channel_id=1, source_target_pairs={{0,32},{64,96},{32,0},{96,64},{1,33},{65,97},{33,1},{97,65},{2,34}... | collective-permute-start | bytes 221192 | tf_op jit(solution)/shard_map/ppermute | solution.py:345
  39.8 13.0 %collective-permute-start.4 = (bf16[128,1152]{1,0:T(8,128)(2,1)}, bf16[128,1152]{1,0:T(8,128)(2,1)S(1)}, u32[]{:S(2)}, u32[]{:S(2)}) collective-permute-start(bf16[128,1152]{1,0:T(8,128)(2,1)} %get-tuple-element.50), channel_id=1, source_target_pairs={{0,12},{4,0},{8,4},{12,8},{1,13},{5,1},{9,5},{13,9},{2,14},{6,2},{... | collective-permute-start | bytes 884744 | tf_op jit(solution)/shard_map/ppermute | solution.py:363
  43.0 22.4 %collective-permute-start.3 = (bf16[128,1152]{1,0:T(8,128)(2,1)S(1)}, bf16[128,1152]{1,0:T(8,128)(2,1)S(1)}, u32[]{:S(2)}, u32[]{:S(2)}) collective-permute-start(bf16[128,1152]{1,0:T(8,128)(2,1)S(1)} %get-tuple-element.53), channel_id=1, source_target_pairs={{0,8},{4,12},{8,0},{12,4},{1,9},{5,13},{9,1},{13,5},{2,10},{6,14},... | collective-permute-start | bytes 884744 | tf_op jit(solution)/shard_map/ppermute | solution.py:363
  46.9 18.5 %collective-permute-start.2 = (bf16[288,128]{1,0:T(8,128)(2,1)S(1)}, bf16[288,128]{1,0:T(8,128)(2,1)S(1)}, u32[]{:S(2)}, u32[]{:S(2)}) collective-permute-start(bf16[288,128]{1,0:T(8,128)(2,1)S(1)} %add_convert_fusion.mine_ref), channel_id=1, source_target_pairs={{32,64},{96,0},{64,32},{0,96},{33,65},{97,1},{65,33},{1,97},{34,66... | collective-permute-start | bytes 221192 | tf_op jit(solution)/shard_map/ppermute | solution.py:345
  67.2 31.2 %all-to-all-start.1 = ((bf16[16,288,128]{2,1,0:T(8,128)(2,1)}), bf16[16,288,128]{2,1,0:T(8,128)(2,1)S(1)}, u32[]{:S(2)}, u32[]{:S(2)}) async-start(bf16[16,288,128]{2,1,0:T(8,128)(2,1)} %outer_step.1), calls=%async_computation.1 | async-start | bytes 2359296 | tf_op jit(solution)/shard_map/all_to_all | solution.py:374
  72.4 18.2 %collective-permute-start.5 = (bf16[128,768]{1,0:T(8,128)(2,1)S(1)}, bf16[128,768]{1,0:T(8,128)(2,1)S(1)}, u32[]{:S(2)}, u32[]{:S(2)}) collective-permute-start(bf16[128,768]{1,0:T(8,128)(2,1)S(1)} %pad_maximum_fusion.1), channel_id=1, source_target_pairs={{0,4},{4,8},{8,12},{12,0},{1,5},{5,9},{9,13},{13,1},{2,6},{6,10},{... | collective-permute-start | bytes 589832 | tf_op jit(solution)/shard_map/ppermute | solution.py:363
  84.0 13.6 %collective-permute-start.6 = (bf16[128,768]{1,0:T(8,128)(2,1)S(1)}, bf16[128,768]{1,0:T(8,128)(2,1)S(1)}, u32[]{:S(2)}, u32[]{:S(2)}) collective-permute-start(bf16[128,768]{1,0:T(8,128)(2,1)S(1)} %pad_maximum_fusion.2), channel_id=1, source_target_pairs={{0,8},{4,12},{8,0},{12,4},{1,9},{5,13},{9,1},{13,5},{2,10},{6,14},... | collective-permute-start | bytes 589832 | tf_op jit(solution)/shard_map/ppermute | solution.py:363
  85.9 11.7 %collective-permute-start.7 = (bf16[128,768]{1,0:T(8,128)(2,1)S(1)}, bf16[128,768]{1,0:T(8,128)(2,1)S(1)}, u32[]{:S(2)}, u32[]{:S(2)}) collective-permute-start(bf16[128,768]{1,0:T(8,128)(2,1)S(1)} %pad_maximum_fusion.3), channel_id=1, source_target_pairs={{0,12},{4,0},{8,4},{12,8},{1,13},{5,1},{9,5},{13,9},{2,14},{6,2},{... | collective-permute-start | bytes 589832 | tf_op jit(solution)/shard_map/ppermute | solution.py:363
  98.4 6.0 %collective-permute-start.8 = (bf16[16,288,128]{2,1,0:T(8,128)(2,1)S(1)}, bf16[16,288,128]{2,1,0:T(8,128)(2,1)S(1)}, u32[]{:S(2)}, u32[]{:S(2)}) collective-permute-start(bf16[16,288,128]{2,1,0:T(8,128)(2,1)S(1)} %all-to-all-done.1.refs_5_), channel_id=1, source_target_pairs={{0,16},{16,0},{1,17},{17,1},{2,18},{18,2},{3,19},{19,3},{4,20},{20... | collective-permute-start | bytes 3538952 | tf_op jit(solution)/shard_map/ppermute | solution.py:401
  113.0 32.1 %all-to-all-start.2 = ((bf16[4,512,256]{2,1,0:T(8,128)(2,1)}), bf16[4,512,256]{2,1,0:T(8,128)(2,1)}, u32[]{:S(2)}, u32[]{:S(2)}) async-start(bf16[4,512,256]{2,1,0:T(8,128)(2,1)} %copy-done.1), calls=%async_computation.2 | async-start | bytes 2097152 | tf_op jit(solution)/shard_map/all_to_all | solution.py:374
  119.7 11.3 %collective-permute-start.11 = (bf16[512,256]{1,0:T(8,128)(2,1)}, bf16[512,256]{1,0:T(8,128)(2,1)S(1)}, u32[]{:S(2)}, u32[]{:S(2)}) collective-permute-start(bf16[512,256]{1,0:T(8,128)(2,1)} %pad_maximum_fusion.refs_5_), channel_id=1, source_target_pairs={{0,3},{1,0},{2,1},{3,2},{4,7},{5,4},{6,5},{7,6},{8,11},{9,8},{10,9... | collective-permute-start | bytes 786440 | tf_op jit(solution)/shard_map/ppermute | solution.py:370
  124.1 10.5 %collective-permute-start.10 = (bf16[512,256]{1,0:T(8,128)(2,1)}, bf16[512,256]{1,0:T(8,128)(2,1)S(1)}, u32[]{:S(2)}, u32[]{:S(2)}) collective-permute-start(bf16[512,256]{1,0:T(8,128)(2,1)} %pad_maximum_fusion.refs_5_), channel_id=1, source_target_pairs={{0,2},{1,3},{2,0},{3,1},{4,6},{5,7},{6,4},{7,5},{8,10},{9,11},{10,... | collective-permute-start | bytes 786440 | tf_op jit(solution)/shard_map/ppermute | solution.py:370
  126.6 15.0 %collective-permute-start.9 = (bf16[512,256]{1,0:T(8,128)(2,1)}, bf16[512,256]{1,0:T(8,128)(2,1)S(1)}, u32[]{:S(2)}, u32[]{:S(2)}) collective-permute-start(bf16[512,256]{1,0:T(8,128)(2,1)} %pad_maximum_fusion.refs_5_), channel_id=1, source_target_pairs={{0,1},{1,2},{2,3},{3,0},{4,5},{5,6},{6,7},{7,4},{8,9},{9,10},{10,1... | collective-permute-start | bytes 786440 | tf_op jit(solution)/shard_map/ppermute | solution.py:370
  146.4 17.5 %copy-start.3 = (bf16[512,256]{1,0:T(8,128)(2,1)S(1)}, bf16[512,256]{1,0:T(8,128)(2,1)}, u32[]{:S(2)}) copy-start(bf16[512,256]{1,0:T(8,128)(2,1)} %pad_maximum_fusion.refs_5_) | copy-start | bytes 786436
  146.5 17.5 %copy-start.4 = (bf16[128,768]{1,0:T(8,128)(2,1)S(1)}, bf16[128,768]{1,0:T(8,128)(2,1)}, u32[]{:S(2)}) copy-start(bf16[128,768]{1,0:T(8,128)(2,1)} %pad_maximum_fusion.4.refs_0_) | copy-start | bytes 589828
  146.5 17.5 %copy-start.7 = (bf16[128,768]{1,0:T(8,128)(2,1)S(1)}, bf16[128,768]{1,0:T(8,128)(2,1)}, u32[]{:S(2)}) copy-start(bf16[128,768]{1,0:T(8,128)(2,1)} %copy-done.6) | copy-start | bytes 589828
  146.5 17.5 %copy-start.9 = (bf16[128,768]{1,0:T(8,128)(2,1)S(1)}, bf16[128,768]{1,0:T(8,128)(2,1)}, u32[]{:S(2)}) copy-start(bf16[128,768]{1,0:T(8,128)(2,1)} %copy-done.8) | copy-start | bytes 589828
  146.5 17.5 %copy-start.11 = (bf16[128,768]{1,0:T(8,128)(2,1)S(1)}, bf16[128,768]{1,0:T(8,128)(2,1)}, u32[]{:S(2)}) copy-start(bf16[128,768]{1,0:T(8,128)(2,1)} %copy-done.10) | copy-start | bytes 589828
  146.5 17.5 %copy-start.17 = (bf16[512,256]{1,0:T(8,128)(2,1)S(1)}, bf16[512,256]{1,0:T(8,128)(2,1)}, u32[]{:S(2)}) copy-start(bf16[512,256]{1,0:T(8,128)(2,1)} %copy-done.16) | copy-start | bytes 786436
  (17 other events, 102.5 us)
Sparse Core Ops, SparseCore 0:
  10.6 46.0 all-gather.1

commit v4 on v3

--- a/solution.py
+++ b/solution.py
@@ -170,29 +170,65 @@
             pltpu.SemaphoreType.DMA((NZL * NC,)),
             pltpu.SemaphoreType.DMA((NZL,)),
         ],
-        compiler_params=params(48),
+        compiler_params=params(46),
         name="project",
     )(place, *hidden, part, same, other)
 
 
 def reduce_kernel(sums_ref, out_ref):
-    total = sums_ref[0].astype(jnp.float32)
-    for i in range(1, NZL):
-        total += sums_ref[i].astype(jnp.float32)
-    keys = (total * (1.0 / math.sqrt(D))).astype(jnp.bfloat16)
-    for i in range(NY):
-        out_ref[i] = keys
+    for head in range(2):
+        cols = slice(head * HD, (head + 1) * HD)
+        total = sums_ref[0, :, cols].astype(jnp.float32)
+        for i in range(1, NZL):
+            total += sums_ref[i, :, cols].astype(jnp.float32)
+        keys = (total * (1.0 / math.sqrt(D))).astype(jnp.bfloat16)
+        out_ref[2 * head] = keys
+        out_ref[2 * head + 1] = keys
 
 
 def reduce_keys(sums):
     return pl.pallas_call(
         reduce_kernel,
-        out_shape=jax.ShapeDtypeStruct((NY,) + sums.shape[1:], jnp.bfloat16),
+        out_shape=jax.ShapeDtypeStruct((NY, sums.shape[1], HD), jnp.bfloat16),
         in_specs=[VMEM],
         out_specs=VMEM,
         compiler_params=params(20),
         name="reduce_keys",
     )(sums)
+
+
+def regroup_kernel(place_ref, *refs):
+    pieces, outs, sems = refs[:4], refs[4:8], refs[8]
+    z, y = place_ref[1], place_ref[2]
+    copies = []
+    for step in range(NY):
+        to_y = lax.rem(y + step, NY)
+        query_at = pl.multiple_of(to_y * HD, HD)
+        value_at = pl.multiple_of(4 * HD + (to_y // 2) * HD, HD)
+        for s in range(NZL):
+            rows = pl.ds(pl.multiple_of(lax.rem(z - s + NZL, NZL) * 128, 128), 128)
+            for i, at in enumerate((query_at, value_at)):
+                copies.append(
+                    pltpu.make_async_copy(
+                        pieces[s].at[:, pl.ds(at, HD)],
+                        outs[step].at[rows, pl.ds(i * HD, HD)],
+                        sems.at[step, s, i],
+                    )
+                )
+    for copy in start_all(copies):
+        copy.wait()
+
+
+def regroup(place, pieces):
+    return pl.pallas_call(
+        regroup_kernel,
+        out_shape=[jax.ShapeDtypeStruct((512, 2 * HD), jnp.bfloat16)] * NY,
+        in_specs=[SMEM] + [ANY] * 4,
+        out_specs=[ANY] * NY,
+        scratch_shapes=[pltpu.SemaphoreType.DMA((NY, NZL, 2))],
+        compiler_params=params(20),
+        name="regroup",
+    )(place, *pieces)
 
 
 def blend_kernel(place_ref, delta_ref, base_ref, same_ref, other_ref, out_ref):
@@ -230,100 +266,73 @@
     )(place, delta, base, same.reshape(split), other.reshape(split))
 
 
-def attend_kernel(place_ref, *refs):
-    pieces, keys_any, values_any = refs[:4], refs[4], refs[5:9]
-    out_ref, queries, keys, values, query_sems, key_sems, value_sems = refs[9:]
-    z, y = place_ref[1], place_ref[2]
-    query_copies, key_copies, value_copies = [], [], []
-    for s, ref in enumerate(pieces):
-        at = lax.rem(z - s + NZL, NZL)
-        query_copies.append(
-            pltpu.make_async_copy(ref.at[:, pl.ds(0, 4 * HD)], queries.at[at], query_sems.at[s])
-        )
-    for zk in range(NZL):
-        rows = pl.ds(zk * 128, 128)
-        key_copies.append(
-            pltpu.make_async_copy(keys_any.at[:, rows], keys.at[:, rows], key_sems.at[zk])
-        )
-        rows = pl.ds(pl.multiple_of(lax.rem(z - zk + NZL, NZL) * 128, 128), 128)
+def attend_kernel(place_ref, keys_any, *refs):
+    pieces, (out_ref, queries, keys, values, sems) = refs[:4], refs[4:]
+    y = place_ref[2]
+    copies = [pltpu.make_async_copy(keys_any, keys, sems.at[0])]
+    for i, target in enumerate((queries, values)):
         for s in range(NY):
-            value_copies.append(
+            copies.append(
                 pltpu.make_async_copy(
-                    values_any[s].at[rows],
-                    values.at[zk, lax.rem(y - s + NY, NY)],
-                    value_sems.at[zk, s],
+                    pieces[s].at[:, pl.ds(i * HD, HD)],
+                    target.at[lax.rem(y - s + NY, NY)],
+                    sems.at[1 + i * NY + s],
                 )
             )
-    start_all(query_copies)
-    for zk in range(NZL):
-        start_all([key_copies[zk]] + value_copies[zk * NY : (zk + 1) * NY])
-    row = lax.broadcasted_iota(jnp.int32, (256, 128), 0) % 128
-    col = lax.broadcasted_iota(jnp.int32, (256, 128), 1)
-    seen = col - row
-    for copy in query_copies:
+    start_all(copies)
+    seen = lax.broadcasted_iota(jnp.int32, (256, 256), 1) <= lax.broadcasted_iota(
+        jnp.int32, (256, 256), 0
+    )
+    for copy in copies:
         copy.wait()
-    for zq in range(NZL):
-        for copy in [key_copies[zq]] + value_copies[zq * NY : (zq + 1) * NY]:
-            copy.wait()
-        for half in range(2):
-            head = 2 * half * HD
-            cols = slice(half * HD, (half + 1) * HD)
-            q = jnp.concatenate(
-                [queries[zq, :, head : head + HD], queries[zq, :, head + HD : head + 2 * HD]],
-                axis=0,
+
+    def pair(ref, z, at):
+        return ref[2 * at : 2 * at + 2, z * 128 : (z + 1) * 128, :].reshape(256, HD)
+
+    for at in range(2 * NZL):
+        q = pair(queries, at // 2, at % 2)
+        acc = jnp.zeros((256, HD), jnp.float32)
+        total = jnp.zeros((256, 128), jnp.float32)
+        for by in range(at + 1):
+            scores = lax.dot_general(
+                q,
+                pair(keys, by // 2, by % 2),
+                (((1,), (1,)), ((), ())),
+                preferred_element_type=jnp.float32,
             )
-            acc = jnp.zeros((256, HD), jnp.float32)
-            total = jnp.zeros((256, 128), jnp.float32)
-            for zk in range(zq + 1):
-                rows = slice(zk * 128, (zk + 1) * 128)
-                for s in range(NY):
-                    scores = lax.dot_general(
-                        q,
-                        keys[s, rows, cols],
-                        (((1,), (1,)), ((), ())),
-                        preferred_element_type=jnp.float32,
-                    )
-                    p = jnp.exp(
-                        logit_cap * jnp.tanh(scores * (1.0 / (query_scalar * logit_cap)))
-                    )
-                    if zk == zq:
-                        p = jnp.where(seen <= (y - s) * 128, p, 0.0)
-                    total += p
-                    acc += jnp.dot(
-                        p.astype(jnp.bfloat16),
-                        values[zk, s, :, cols],
-                        preferred_element_type=jnp.float32,
-                    )
-            out = (acc / jnp.sum(total, axis=1, keepdims=True)).astype(jnp.bfloat16)
-            out_ref[zq, :, head : head + HD] = out[:128]
-            out_ref[zq, :, head + HD : head + 2 * HD] = out[128:]
-
-
-def attend(place, queries, keys, values):
+            p = jnp.exp(logit_cap * jnp.tanh(scores * (1.0 / (query_scalar * logit_cap))))
+            if by == at:
+                p = jnp.where(seen, p, 0.0)
+            total += p[:, :128] + p[:, 128:]
+            acc += jnp.dot(
+                p.astype(jnp.bfloat16),
+                pair(values, by // 2, by % 2),
+                preferred_element_type=jnp.float32,
+            )
+        out = (acc / jnp.sum(total, axis=1, keepdims=True)).astype(jnp.bfloat16)
+        out_ref[2 * at] = out[:128]
+        out_ref[2 * at + 1] = out[128:]
+
+
+def attend(place, keys, pieces):
+    whole = pltpu.VMEM((NY, 512, HD), jnp.bfloat16)
     return pl.pallas_call(
         attend_kernel,
-        out_shape=jax.ShapeDtypeStruct((NZL, 128, 4 * HD), jnp.bfloat16),
-        in_specs=[SMEM] + [ANY] * 9,
+        out_shape=jax.ShapeDtypeStruct((NZL * NY, 128, HD), jnp.bfloat16),
+        in_specs=[SMEM] + [ANY] * 5,
         out_specs=VMEM,
-        scratch_shapes=[
-            pltpu.VMEM((NZL, 128, 4 * HD), jnp.bfloat16),
-            pltpu.VMEM((NY, 512, 2 * HD), jnp.bfloat16),
-            pltpu.VMEM((NZL, NY, 128, 2 * HD), jnp.bfloat16),
-            pltpu.SemaphoreType.DMA((NZL,)),
-            pltpu.SemaphoreType.DMA((NZL,)),
-            pltpu.SemaphoreType.DMA((NZL, NY)),
-        ],
+        scratch_shapes=[whole, whole, whole, pltpu.SemaphoreType.DMA((1 + 2 * NY,))],
         compiler_params=params(20),
         name="attend",
-    )(place, *queries, keys, *values)
+    )(place, keys, *pieces)
 
 
 def lay_kernel(mixed_any, out_any, sems):
-    width = mixed_any.shape[2]
+    places, _, width = mixed_any.shape
     copies = []
-    for z in range(NZL):
-        cols = pl.ds(z * width, width)
-        copies.append(pltpu.make_async_copy(mixed_any.at[z], out_any.at[:, cols], sems.at[z]))
+    for i in range(places):
+        cols = pl.ds(i * width, width)
+        copies.append(pltpu.make_async_copy(mixed_any.at[i], out_any.at[:, cols], sems.at[i]))
     for copy in start_all(copies):
         copy.wait()
 
@@ -335,7 +344,7 @@
         out_shape=jax.ShapeDtypeStruct((rows, places * width), jnp.bfloat16),
         in_specs=[ANY],
         out_specs=ANY,
-        scratch_shapes=[pltpu.SemaphoreType.DMA((NZL,))],
+        scratch_shapes=[pltpu.SemaphoreType.DMA((places,))],
         compiler_params=params(20),
         name="lay",
     )(mixed)
@@ -365,9 +374,9 @@
     return pieces
 
 
-def from_ring(array, axis):
+def turn(arrays, axis):
     shifts = [[(i, (i + step) % 4) for i in range(4)] for step in (1, 2, 3)]
-    return [array] + [lax.ppermute(array, axis, shift) for shift in shifts]
+    return arrays[:1] + [lax.ppermute(a, axis, shift) for a, shift in zip(arrays[1:], shifts)]
 
 
 def exchange(array, axis):
@@ -383,12 +392,12 @@
 
     sent = exchange(delta, ("x", "c"))
     hidden_here = deal([hidden[0]], "zl")
-    sent, hidden_here[1] = lax.optimization_barrier((sent, hidden_here[1]))
+    sent, hidden_here[2] = lax.optimization_barrier((sent, hidden_here[2]))
     eighth = jnp.sum(sent.astype(jnp.float32), axis=0).astype(jnp.bfloat16)
     pair = add(eighth, swap(eighth, "zh", [(0, 1), (2, 3)])).astype(jnp.bfloat16)
     swapped = swap(pair, "zh", [(1, 2), (3, 0)])
-    swapped, hidden_here[2], hidden_here[3] = lax.optimization_barrier(
-        (swapped, hidden_here[2], hidden_here[3])
+    swapped, hidden_here[1], hidden_here[3] = lax.optimization_barrier(
+        (swapped, hidden_here[1], hidden_here[3])
     )
     outer = outer_step(place, pair, swapped, base, momentum)
 
@@ -396,18 +405,17 @@
     both = deal([queries_in, values_in], "zl")
 
     same = exchange(outer, ("x", "y"))
-    value_here = jnp.concatenate([piece[:, 512:] for piece in both])
-    same, value_here, *both = lax.optimization_barrier((same, value_here, *both))
+    same, *both = lax.optimization_barrier((same, *both))
     other = lax.ppermute(same, "c", [(0, 1), (1, 0)])
 
     sums = project(place, hidden_here, part_all, same, other)
-    sums, value_here = lax.optimization_barrier((sums, value_here))
+    sums, *both = lax.optimization_barrier((sums, *both))
     sums = exchange(sums, "zl")
-    value_all = from_ring(value_here, "y")
+    by_head = turn(list(regroup(place, both)), "y")
     blended = blend(place, delta, base, same, other)
-    sums, blended, *value_all = lax.optimization_barrier((sums, blended, *value_all))
+    sums, blended, *by_head = lax.optimization_barrier((sums, blended, *by_head))
     keys = exchange(reduce_keys(sums), "y")
-    mixed = exchange(attend(place, both, keys, value_all), "zl")
+    mixed = exchange(attend(place, keys, by_head), ("zl", "y"))
     return blended[None], lay(mixed)[None]
 
 

time: 196 us -> 197 us (level)
  the two profiles are of different devices: /device:TPU:1 before, /device:TPU:2 now
where the time goes in v4:
time: 197 us; the launch traced here: 196 us
  starting transfers between devices  76.7 us (39%)
  waiting for transfers between devices  38.6 us (20%)
  blocking collectives  30.7 us (16%)
  Pallas kernels  21.1 us (11%)
  between operations  14.3 us (7%)
  local copies, waits for them, and re-layouts  13.5 us (7%)
    all_to_all x2, blocking collectives, exchange(): return lax.all_to_all(array, axis, 0, 0, tiled=True)  30.7 us
    all_to_all x3, starting transfers between devices, exchange(): return lax.all_to_all(array, axis, 0, 0, tiled=True)  25.6 us
    ppermute x6, waiting for transfers between devices, deal(): piece = lax.ppermute(piece, axis, [(i, (i + step) % 4) for i in range(4)])  23.3 us
    ppermute x6, starting transfers between devices, deal(): piece = lax.ppermute(piece, axis, [(i, (i + step) % 4) for i in range(4)])  23.2 us
    ppermute x2, starting transfers between devices, swap(): return lax.ppermute(array, axis, pairs + [(b, a) for a, b in pairs])  14.7 us
    unnamed x54, local copies, waits for them, and re-layouts  12.5 us
    ppermute x3, starting transfers between devices, turn(): lax.ppermute(a, axis, shift)  11.3 us
    ppermute x2, waiting for transfers between devices, swap(): return lax.ppermute(array, axis, pairs + [(b, a) for a, b in pairs])  6.5 us
  transfers between devices with their start and end apart: 16, of which 8 were waited for; matrix products, arithmetic and copies ran while one was open for 1% of the time, Pallas kernels for 2%

profile of v4, /device:TPU:2, one launch (start us, length us, event | category | flops | bytes accessed | tf_op | source)
XLA Modules:
  0.0 195.8 jit_solution(13966512749031276764)
XLA Ops:
  7.2 3.3 %prep.1 = (bf16[8,288,128]{2,1,0:T(8,128)(2,1)}, bf16[288,1024]{1,0:T(8,128)(2,1)}) custom-call(bf16[288,1024]{1,0:T(8,128)(2,1)} %bitcast.25, s32[8,288]{1,0:T(8,128)} %bitcast.29, bf16[288,1024]{1,0:T(8,128)(2,1)} %base_ref.3), custom_call_target="tpu_custom_call" | custom-call | tf_op jit(solution)/shard_map/prep/pallas_call | solution.py:64
  10.5 9.5 %all-to-all-start = ((bf16[8,288,128]{2,1,0:T(8,128)(2,1)}), bf16[8,288,128]{2,1,0:T(8,128)(2,1)S(1)}, u32[]{:S(2)}, u32[]{:S(2)}) async-start(bf16[8,288,128]{2,1,0:T(8,128)(2,1)} %get-tuple-element.32.delta_ref), calls=%async_computation | async-start | bytes 1179648 | tf_op jit(solution)/shard_map/all_to_all | solution.py:383
  22.8 13.7 %collective-permute-done.refs_2_ = bf16[128,1152]{1,0:T(8,128)(2,1)S(1)} collective-permute-done((bf16[128,1152]{1,0:T(8,128)(2,1)S(1)}, bf16[128,1152]{1,0:T(8,128)(2,1)S(1)}, u32[]{:S(2)}, u32[]{:S(2)}) %collective-permute-start) | collective-permute-done | bytes 294944 | tf_op jit(solution)/shard_map/ppermute | solution.py:372
  36.6 7.7 %collective-permute-start.1 = (bf16[288,128]{1,0:T(8,128)(2,1)S(1)}, bf16[288,128]{1,0:T(8,128)(2,1)S(1)}, u32[]{:S(2)}, u32[]{:S(2)}) collective-permute-start(bf16[288,128]{1,0:T(8,128)(2,1)S(1)} %reduce_sum.12), channel_id=1, source_target_pairs={{0,32},{64,96},{32,0},{96,64},{1,33},{65,97},{33,1},{97,65},{2,34}... | collective-permute-start | bytes 221192 | tf_op jit(solution)/shard_map/ppermute | solution.py:354
  44.3 5.4 %collective-permute-start.4 = (bf16[128,1152]{1,0:T(8,128)(2,1)}, bf16[128,1152]{1,0:T(8,128)(2,1)S(1)}, u32[]{:S(2)}, u32[]{:S(2)}) collective-permute-start(bf16[128,1152]{1,0:T(8,128)(2,1)} %get-tuple-element.62), channel_id=1, source_target_pairs={{0,12},{4,0},{8,4},{12,8},{1,13},{5,1},{9,5},{13,9},{2,14},{6,2},{... | collective-permute-start | bytes 884744 | tf_op jit(solution)/shard_map/ppermute | solution.py:372
  49.8 1.9 collective-permute-start.3
  51.8 6.9 %collective-permute-start.2 = (bf16[288,128]{1,0:T(8,128)(2,1)S(1)}, bf16[288,128]{1,0:T(8,128)(2,1)S(1)}, u32[]{:S(2)}, u32[]{:S(2)}) collective-permute-start(bf16[288,128]{1,0:T(8,128)(2,1)S(1)} %add_convert_fusion.mine_ref), channel_id=1, source_target_pairs={{32,64},{96,0},{64,32},{0,96},{33,65},{97,1},{65,33},{1,97},{34,66... | collective-permute-start | bytes 221192 | tf_op jit(solution)/shard_map/ppermute | solution.py:354
  58.8 5.3 %collective-permute-done.3.refs_1_ = bf16[128,1152]{1,0:T(8,128)(2,1)S(1)} collective-permute-done((bf16[128,1152]{1,0:T(8,128)(2,1)S(1)}, bf16[128,1152]{1,0:T(8,128)(2,1)S(1)}, u32[]{:S(2)}, u32[]{:S(2)}) %collective-permute-start.3) | collective-permute-done | bytes 294944 | tf_op jit(solution)/shard_map/ppermute | solution.py:372
  64.1 6.5 %collective-permute-done.2.sent_ref = bf16[288,128]{1,0:T(8,128)(2,1)S(1)} collective-permute-done((bf16[288,128]{1,0:T(8,128)(2,1)S(1)}, bf16[288,128]{1,0:T(8,128)(2,1)S(1)}, u32[]{:S(2)}, u32[]{:S(2)}) %collective-permute-start.2) | collective-permute-done | bytes 73760 | tf_op jit(solution)/shard_map/ppermute | solution.py:354
  72.4 7.5 %all-to-all-start.1 = ((bf16[16,288,128]{2,1,0:T(8,128)(2,1)}), bf16[16,288,128]{2,1,0:T(8,128)(2,1)S(1)}, u32[]{:S(2)}, u32[]{:S(2)}) async-start(bf16[16,288,128]{2,1,0:T(8,128)(2,1)} %outer_step.1), calls=%async_computation.1 | async-start | bytes 2359296 | tf_op jit(solution)/shard_map/all_to_all | solution.py:383
  80.0 4.8 %collective-permute-start.5 = (bf16[128,768]{1,0:T(8,128)(2,1)S(1)}, bf16[128,768]{1,0:T(8,128)(2,1)S(1)}, u32[]{:S(2)}, u32[]{:S(2)}) collective-permute-start(bf16[128,768]{1,0:T(8,128)(2,1)S(1)} %pad_maximum_fusion.1), channel_id=1, source_target_pairs={{0,4},{4,8},{8,12},{12,0},{1,5},{5,9},{9,13},{13,1},{2,6},{6,10},{... | collective-permute-start | bytes 589832 | tf_op jit(solution)/shard_map/ppermute | solution.py:372
  84.8 4.3 %collective-permute-start.6 = (bf16[128,768]{1,0:T(8,128)(2,1)S(1)}, bf16[128,768]{1,0:T(8,128)(2,1)S(1)}, u32[]{:S(2)}, u32[]{:S(2)}) collective-permute-start(bf16[128,768]{1,0:T(8,128)(2,1)S(1)} %pad_maximum_fusion.2), channel_id=1, source_target_pairs={{0,8},{4,12},{8,0},{12,4},{1,9},{5,13},{9,1},{13,5},{2,10},{6,14},... | collective-permute-start | bytes 589832 | tf_op jit(solution)/shard_map/ppermute | solution.py:372
  89.2 4.8 %collective-permute-start.7 = (bf16[128,768]{1,0:T(8,128)(2,1)S(1)}, bf16[128,768]{1,0:T(8,128)(2,1)S(1)}, u32[]{:S(2)}, u32[]{:S(2)}) collective-permute-start(bf16[128,768]{1,0:T(8,128)(2,1)S(1)} %pad_maximum_fusion.3), channel_id=1, source_target_pairs={{0,12},{4,0},{8,4},{12,8},{1,13},{5,1},{9,5},{13,9},{2,14},{6,2},{... | collective-permute-start | bytes 589832 | tf_op jit(solution)/shard_map/ppermute | solution.py:372
  95.4 4.3 %collective-permute-done.6.refs_2_ = bf16[128,768]{1,0:T(8,128)(2,1)S(1)} collective-permute-done((bf16[128,768]{1,0:T(8,128)(2,1)S(1)}, bf16[128,768]{1,0:T(8,128)(2,1)S(1)}, u32[]{:S(2)}, u32[]{:S(2)}) %collective-permute-start.6) | collective-permute-done | bytes 196640 | tf_op jit(solution)/shard_map/ppermute | solution.py:372
  103.0 2.8 %collective-permute-done.8.refs_6_ = bf16[16,288,128]{2,1,0:T(8,128)(2,1)S(1)} collective-permute-done((bf16[16,288,128]{2,1,0:T(8,128)(2,1)S(1)}, bf16[16,288,128]{2,1,0:T(8,128)(2,1)S(1)}, u32[]{:S(2)}, u32[]{:S(2)}) %collective-permute-start.8) | collective-permute-done | bytes 1179680 | tf_op jit(solution)/shard_map/ppermute | solution.py:409
  109.4 5.6 %project.1 = bf16[4,512,256]{2,1,0:T(8,128)(2,1)S(1)} custom-call(s32[4]{0:T(128)S(1)} %pad_add_fusion.place_ref, bf16[128,1152]{1,0:T(8,128)(2,1)S(1)} %get-tuple-element.64.refs_0_, bf16[128,1152]{1,0:T(8,128)(2,1)S(1)} %copy-done.9, bf16[128,1152]{1,0:T(8,128)(2,1)S(1)} %collective-permute-done.refs_2_, bf16[128,1152]{1,0:T(8,128)(2,1)S(1)} %copy-done.7, ...), custom_call_target="tpu_custom_call" | custom-call | tf_op jit(solution)/shard_map/project/pallas_call | solution.py:159
  116.0 8.6 %all-to-all-start.2 = ((bf16[4,512,256]{2,1,0:T(8,128)(2,1)}), bf16[4,512,256]{2,1,0:T(8,128)(2,1)}, u32[]{:S(2)}, u32[]{:S(2)}) async-start(bf16[4,512,256]{2,1,0:T(8,128)(2,1)} %copy-done.1), calls=%async_computation.2 | async-start | bytes 2097152 | tf_op jit(solution)/shard_map/all_to_all | solution.py:383
  129.5 3.4 %collective-permute-start.9 = (bf16[512,256]{1,0:T(8,128)(2,1)S(1)}, bf16[512,256]{1,0:T(8,128)(2,1)S(1)}, u32[]{:S(2)}, u32[]{:S(2)}) collective-permute-start(bf16[512,256]{1,0:T(8,128)(2,1)S(1)} %get-tuple-element.53), channel_id=1, source_target_pairs={{0,1},{1,2},{2,3},{3,0},{4,5},{5,6},{6,7},{7,4},{8,9},{9,10},{10,1... | collective-permute-start | bytes 786440 | tf_op jit(solution)/shard_map/ppermute | solution.py:379
  132.8 4.6 %collective-permute-start.10 = (bf16[512,256]{1,0:T(8,128)(2,1)S(1)}, bf16[512,256]{1,0:T(8,128)(2,1)S(1)}, u32[]{:S(2)}, u32[]{:S(2)}) collective-permute-start(bf16[512,256]{1,0:T(8,128)(2,1)S(1)} %get-tuple-element.54), channel_id=1, source_target_pairs={{0,2},{1,3},{2,0},{3,1},{4,6},{5,7},{6,4},{7,5},{8,10},{9,11},{10,... | collective-permute-start | bytes 786440 | tf_op jit(solution)/shard_map/ppermute | solution.py:379
  137.4 3.4 %collective-permute-start.11 = (bf16[512,256]{1,0:T(8,128)(2,1)S(1)}, bf16[512,256]{1,0:T(8,128)(2,1)S(1)}, u32[]{:S(2)}, u32[]{:S(2)}) collective-permute-start(bf16[512,256]{1,0:T(8,128)(2,1)S(1)} %get-tuple-element.55), channel_id=1, source_target_pairs={{0,3},{1,0},{2,1},{3,2},{4,7},{5,4},{6,5},{7,6},{8,11},{9,8},{10,9... | collective-permute-start | bytes 786440 | tf_op jit(solution)/shard_map/ppermute | solution.py:379
  143.4 3.7 %collective-permute-done.10.refs_2_ = bf16[512,256]{1,0:T(8,128)(2,1)S(1)} collective-permute-done((bf16[512,256]{1,0:T(8,128)(2,1)S(1)}, bf16[512,256]{1,0:T(8,128)(2,1)S(1)}, u32[]{:S(2)}, u32[]{:S(2)}) %collective-permute-start.10) | collective-permute-done | bytes 262176 | tf_op jit(solution)/shard_map/ppermute | solution.py:379
  152.2 12.8 %all_to_all.25.keys_any = bf16[4,512,128]{2,1,0:T(8,128)(2,1)S(1)} all-to-all(bf16[4,512,128]{2,1,0:T(8,128)(2,1)S(1)} %reduce_keys.1), channel_id=1, replica_groups=mesh['x'=4,'zh'=4,'c'=2,'zl'=4,'y'=4] {'y'}, dimensions={0} | all-to-all | bytes 1048576 | tf_op jit(solution)/shard_map/all_to_all | solution.py:383
  165.0 5.1 %attend.1 = bf16[16,128,128]{2,1,0:T(8,128)(2,1)S(1)} custom-call(s32[4]{0:T(128)S(1)} %pad_add_fusion.place_ref, bf16[4,512,128]{2,1,0:T(8,128)(2,1)S(1)} %all_to_all.25.keys_any, bf16[512,256]{1,0:T(8,128)(2,1)S(1)} %copy-done.11, bf16[512,256]{1,0:T(8,128)(2,1)S(1)} %copy-done.13, bf16[512,256]{1,0:T(8,128)(2,1)S(1)} %copy-done.15, ...), custom_call_target="tpu_custom_call" | custom-call | tf_op jit(solution)/shard_map/attend/pallas_call | solution.py:319
  170.1 17.9 %all_to_all.26.mixed_any = bf16[16,128,128]{2,1,0:T(8,128)(2,1)S(1)} all-to-all(bf16[16,128,128]{2,1,0:T(8,128)(2,1)S(1)} %attend.1), channel_id=1, replica_groups=mesh['x'=4,'zh'=4,'c'=2,'zl'=4,'y'=4] {'zl','y'}, dimensions={0} | all-to-all | bytes 1048576 | tf_op jit(solution)/shard_map/all_to_all | solution.py:383
  (83 shorter events, 27.5 us)
Async XLA Ops:
  7.2 98.6 %all-gather.2.cloned.1.call-start = ((), (), s32[]{:S(2)}) async-start(), calls=%async_computation.5 | async-start | bytes 2949120 | tf_op jit(solution)/shard_map/all_gather | solution.py:391
  10.5 26.0 %all-to-all-start = ((bf16[8,288,128]{2,1,0:T(8,128)(2,1)}), bf16[8,288,128]{2,1,0:T(8,128)(2,1)S(1)}, u32[]{:S(2)}, u32[]{:S(2)}) async-start(bf16[8,288,128]{2,1,0:T(8,128)(2,1)} %get-tuple-element.32.delta_ref), calls=%async_computation | async-start | bytes 1179648 | tf_op jit(solution)/shard_map/all_to_all | solution.py:383
  20.0 50.6 %copy-start = (bf16[288,1024]{1,0:T(8,128)(2,1)S(1)}, bf16[288,1024]{1,0:T(8,128)(2,1)}, u32[]{:S(2)}) copy-start(bf16[288,1024]{1,0:T(8,128)(2,1)} %base_ref.3) | copy-start | bytes 1769476
  20.0 50.6 %copy-start.5 = (bf16[288,1024]{1,0:T(8,128)(2,1)S(1)}, bf16[288,1024]{1,0:T(8,128)(2,1)}, u32[]{:S(2)}) copy-start(bf16[288,1024]{1,0:T(8,128)(2,1)} %momentum_ref.1) | copy-start | bytes 1769476
  20.9 15.6 %collective-permute-start = (bf16[128,1152]{1,0:T(8,128)(2,1)S(1)}, bf16[128,1152]{1,0:T(8,128)(2,1)S(1)}, u32[]{:S(2)}, u32[]{:S(2)}) collective-permute-start(bf16[128,1152]{1,0:T(8,128)(2,1)S(1)} %get-tuple-element.63), channel_id=1, source_target_pairs={{0,8},{4,12},{8,0},{12,4},{1,9},{5,13},{9,1},{13,5},{2,10},{6,14},... | collective-permute-start | bytes 884744 | tf_op jit(solution)/shard_map/ppermute | solution.py:372
  36.6 15.1 %collective-permute-start.1 = (bf16[288,128]{1,0:T(8,128)(2,1)S(1)}, bf16[288,128]{1,0:T(8,128)(2,1)S(1)}, u32[]{:S(2)}, u32[]{:S(2)}) collective-permute-start(bf16[288,128]{1,0:T(8,128)(2,1)S(1)} %reduce_sum.12), channel_id=1, source_target_pairs={{0,32},{64,96},{32,0},{96,64},{1,33},{65,97},{33,1},{97,65},{2,34}... | collective-permute-start | bytes 221192 | tf_op jit(solution)/shard_map/ppermute | solution.py:354
  44.3 14.5 %collective-permute-start.4 = (bf16[128,1152]{1,0:T(8,128)(2,1)}, bf16[128,1152]{1,0:T(8,128)(2,1)S(1)}, u32[]{:S(2)}, u32[]{:S(2)}) collective-permute-start(bf16[128,1152]{1,0:T(8,128)(2,1)} %get-tuple-element.62), channel_id=1, source_target_pairs={{0,12},{4,0},{8,4},{12,8},{1,13},{5,1},{9,5},{13,9},{2,14},{6,2},{... | collective-permute-start | bytes 884744 | tf_op jit(solution)/shard_map/ppermute | solution.py:372
  49.8 14.3 %collective-permute-start.3 = (bf16[128,1152]{1,0:T(8,128)(2,1)S(1)}, bf16[128,1152]{1,0:T(8,128)(2,1)S(1)}, u32[]{:S(2)}, u32[]{:S(2)}) collective-permute-start(bf16[128,1152]{1,0:T(8,128)(2,1)S(1)} %get-tuple-element.65), channel_id=1, source_target_pairs={{0,4},{4,8},{8,12},{12,0},{1,5},{5,9},{9,13},{13,1},{2,6},{6,10},{... | collective-permute-start | bytes 884744 | tf_op jit(solution)/shard_map/ppermute | solution.py:372
  51.8 18.8 %collective-permute-start.2 = (bf16[288,128]{1,0:T(8,128)(2,1)S(1)}, bf16[288,128]{1,0:T(8,128)(2,1)S(1)}, u32[]{:S(2)}, u32[]{:S(2)}) collective-permute-start(bf16[288,128]{1,0:T(8,128)(2,1)S(1)} %add_convert_fusion.mine_ref), channel_id=1, source_target_pairs={{32,64},{96,0},{64,32},{0,96},{33,65},{97,1},{65,33},{1,97},{34,66... | collective-permute-start | bytes 221192 | tf_op jit(solution)/shard_map/ppermute | solution.py:354
  58.8 13.6 %copy-start.6 = (bf16[128,1152]{1,0:T(8,128)(2,1)}, bf16[128,1152]{1,0:T(8,128)(2,1)S(1)}, u32[]{:S(2)}) copy-start(bf16[128,1152]{1,0:T(8,128)(2,1)S(1)} %collective-permute-done.4.refs_3_) | copy-start | bytes 884740
  72.4 28.7 %all-to-all-start.1 = ((bf16[16,288,128]{2,1,0:T(8,128)(2,1)}), bf16[16,288,128]{2,1,0:T(8,128)(2,1)S(1)}, u32[]{:S(2)}, u32[]{:S(2)}) async-start(bf16[16,288,128]{2,1,0:T(8,128)(2,1)} %outer_step.1), calls=%async_computation.1 | async-start | bytes 2359296 | tf_op jit(solution)/shard_map/all_to_all | solution.py:383
  80.0 14.7 %collective-permute-start.5 = (bf16[128,768]{1,0:T(8,128)(2,1)S(1)}, bf16[128,768]{1,0:T(8,128)(2,1)S(1)}, u32[]{:S(2)}, u32[]{:S(2)}) collective-permute-start(bf16[128,768]{1,0:T(8,128)(2,1)S(1)} %pad_maximum_fusion.1), channel_id=1, source_target_pairs={{0,4},{4,8},{8,12},{12,0},{1,5},{5,9},{9,13},{13,1},{2,6},{6,10},{... | collective-permute-start | bytes 589832 | tf_op jit(solution)/shard_map/ppermute | solution.py:372
  84.8 14.8 %collective-permute-start.6 = (bf16[128,768]{1,0:T(8,128)(2,1)S(1)}, bf16[128,768]{1,0:T(8,128)(2,1)S(1)}, u32[]{:S(2)}, u32[]{:S(2)}) collective-permute-start(bf16[128,768]{1,0:T(8,128)(2,1)S(1)} %pad_maximum_fusion.2), channel_id=1, source_target_pairs={{0,8},{4,12},{8,0},{12,4},{1,9},{5,13},{9,1},{13,5},{2,10},{6,14},... | collective-permute-start | bytes 589832 | tf_op jit(solution)/shard_map/ppermute | solution.py:372
  89.2 11.2 %collective-permute-start.7 = (bf16[128,768]{1,0:T(8,128)(2,1)S(1)}, bf16[128,768]{1,0:T(8,128)(2,1)S(1)}, u32[]{:S(2)}, u32[]{:S(2)}) collective-permute-start(bf16[128,768]{1,0:T(8,128)(2,1)S(1)} %pad_maximum_fusion.3), channel_id=1, source_target_pairs={{0,12},{4,0},{8,4},{12,8},{1,13},{5,1},{9,5},{13,9},{2,14},{6,2},{... | collective-permute-start | bytes 589832 | tf_op jit(solution)/shard_map/ppermute | solution.py:372
  101.1 4.7 %collective-permute-start.8 = (bf16[16,288,128]{2,1,0:T(8,128)(2,1)S(1)}, bf16[16,288,128]{2,1,0:T(8,128)(2,1)S(1)}, u32[]{:S(2)}, u32[]{:S(2)}) collective-permute-start(bf16[16,288,128]{2,1,0:T(8,128)(2,1)S(1)} %all-to-all-done.1.refs_5_), channel_id=1, source_target_pairs={{0,16},{16,0},{1,17},{17,1},{2,18},{18,2},{3,19},{19,3},{4,20},{20... | collective-permute-start | bytes 3538952 | tf_op jit(solution)/shard_map/ppermute | solution.py:409
  116.0 24.8 %copy-start.2 = (bf16[8,288,128]{2,1,0:T(8,128)(2,1)S(1)}, bf16[8,288,128]{2,1,0:T(8,128)(2,1)}, u32[]{:S(2)}) copy-start(bf16[8,288,128]{2,1,0:T(8,128)(2,1)} %get-tuple-element.32.delta_ref) | copy-start | bytes 1769476
  116.0 34.7 %all-to-all-start.2 = ((bf16[4,512,256]{2,1,0:T(8,128)(2,1)}), bf16[4,512,256]{2,1,0:T(8,128)(2,1)}, u32[]{:S(2)}, u32[]{:S(2)}) async-start(bf16[4,512,256]{2,1,0:T(8,128)(2,1)} %copy-done.1), calls=%async_computation.2 | async-start | bytes 2097152 | tf_op jit(solution)/shard_map/all_to_all | solution.py:383
  129.5 13.2 %collective-permute-start.9 = (bf16[512,256]{1,0:T(8,128)(2,1)S(1)}, bf16[512,256]{1,0:T(8,128)(2,1)S(1)}, u32[]{:S(2)}, u32[]{:S(2)}) collective-permute-start(bf16[512,256]{1,0:T(8,128)(2,1)S(1)} %get-tuple-element.53), channel_id=1, source_target_pairs={{0,1},{1,2},{2,3},{3,0},{4,5},{5,6},{6,7},{7,4},{8,9},{9,10},{10,1... | collective-permute-start | bytes 786440 | tf_op jit(solution)/shard_map/ppermute | solution.py:379
  132.8 14.3 %collective-permute-start.10 = (bf16[512,256]{1,0:T(8,128)(2,1)S(1)}, bf16[512,256]{1,0:T(8,128)(2,1)S(1)}, u32[]{:S(2)}, u32[]{:S(2)}) collective-permute-start(bf16[512,256]{1,0:T(8,128)(2,1)S(1)} %get-tuple-element.54), channel_id=1, source_target_pairs={{0,2},{1,3},{2,0},{3,1},{4,6},{5,7},{6,4},{7,5},{8,10},{9,11},{10,... | collective-permute-start | bytes 786440 | tf_op jit(solution)/shard_map/ppermute | solution.py:379
  137.4 11.3 %collective-permute-start.11 = (bf16[512,256]{1,0:T(8,128)(2,1)S(1)}, bf16[512,256]{1,0:T(8,128)(2,1)S(1)}, u32[]{:S(2)}, u32[]{:S(2)}) collective-permute-start(bf16[512,256]{1,0:T(8,128)(2,1)S(1)} %get-tuple-element.55), channel_id=1, source_target_pairs={{0,3},{1,0},{2,1},{3,2},{4,7},{5,4},{6,5},{7,6},{8,11},{9,8},{10,9... | collective-permute-start | bytes 786440 | tf_op jit(solution)/shard_map/ppermute | solution.py:379
  150.7 14.3 %copy-start.11 = (bf16[512,256]{1,0:T(8,128)(2,1)S(1)}, bf16[512,256]{1,0:T(8,128)(2,1)}, u32[]{:S(2)}) copy-start(bf16[512,256]{1,0:T(8,128)(2,1)} %copy-done.10) | copy-start | bytes 786436
  150.7 14.3 %copy-start.13 = (bf16[512,256]{1,0:T(8,128)(2,1)S(1)}, bf16[512,256]{1,0:T(8,128)(2,1)}, u32[]{:S(2)}) copy-start(bf16[512,256]{1,0:T(8,128)(2,1)} %copy-done.12) | copy-start | bytes 786436
  150.7 14.3 %copy-start.15 = (bf16[512,256]{1,0:T(8,128)(2,1)S(1)}, bf16[512,256]{1,0:T(8,128)(2,1)}, u32[]{:S(2)}) copy-start(bf16[512,256]{1,0:T(8,128)(2,1)} %copy-done.14) | copy-start | bytes 786436
  150.7 14.3 %copy-start.17 = (bf16[512,256]{1,0:T(8,128)(2,1)S(1)}, bf16[512,256]{1,0:T(8,128)(2,1)}, u32[]{:S(2)}) copy-start(bf16[512,256]{1,0:T(8,128)(2,1)} %copy-done.16) | copy-start | bytes 786436
  (19 other events, 58.6 us)
Sparse Core Ops, SparseCore 0:
  10.7 45.1 all-gather.1

commit v5 on v4

--- a/solution.py
+++ b/solution.py
@@ -170,7 +170,7 @@
             pltpu.SemaphoreType.DMA((NZL * NC,)),
             pltpu.SemaphoreType.DMA((NZL,)),
         ],
-        compiler_params=params(46),
+        compiler_params=params(48),
         name="project",
     )(place, *hidden, part, same, other)
 
@@ -392,17 +392,15 @@
 
     sent = exchange(delta, ("x", "c"))
     hidden_here = deal([hidden[0]], "zl")
-    sent, hidden_here[2] = lax.optimization_barrier((sent, hidden_here[2]))
+    sent, hidden_here[1] = lax.optimization_barrier((sent, hidden_here[1]))
     eighth = jnp.sum(sent.astype(jnp.float32), axis=0).astype(jnp.bfloat16)
     pair = add(eighth, swap(eighth, "zh", [(0, 1), (2, 3)])).astype(jnp.bfloat16)
     swapped = swap(pair, "zh", [(1, 2), (3, 0)])
-    swapped, hidden_here[1], hidden_here[3] = lax.optimization_barrier(
-        (swapped, hidden_here[1], hidden_here[3])
+    both = deal([queries[0], values[0]], "zl")
+    swapped, hidden_here[2], hidden_here[3], both[1], both[3] = lax.optimization_barrier(
+        (swapped, hidden_here[2], hidden_here[3], both[1], both[3])
     )
     outer = outer_step(place, pair, swapped, base, momentum)
-
-    queries_in, values_in, outer = lax.optimization_barrier((queries[0], values[0], outer))
-    both = deal([queries_in, values_in], "zl")
 
     same = exchange(outer, ("x", "y"))
     same, *both = lax.optimization_barrier((same, *both))

time: 197 us -> 193 us (0.980)
  the two profiles are of different devices: /device:TPU:2 before, /device:TPU:1 now
where the time goes in v5:
time: 193 us; the launch traced here: 191 us
  starting transfers between devices  68.2 us (35%)
  waiting for transfers between devices  42.4 us (22%)
  blocking collectives  29.2 us (15%)
  Pallas kernels  21.1 us (11%)
  between operations  14.4 us (7%)
  local copies, waits for them, and re-layouts  11.2 us (6%)
  other arithmetic  4.04 us (2%)
    all_to_all x2, blocking collectives, exchange(): return lax.all_to_all(array, axis, 0, 0, tiled=True)  29.2 us
    all_to_all x3, starting transfers between devices, exchange(): return lax.all_to_all(array, axis, 0, 0, tiled=True)  26 us
    ppermute x6, waiting for transfers between devices, deal(): piece = lax.ppermute(piece, axis, [(i, (i + step) % 4) for i in range(4)])  24.3 us
    ppermute x6, starting transfers between devices, deal(): piece = lax.ppermute(piece, axis, [(i, (i + step) % 4) for i in range(4)])  14.9 us
    ppermute x2, starting transfers between devices, swap(): return lax.ppermute(array, axis, pairs + [(b, a) for a, b in pairs])  13.3 us
    unnamed x52, local copies, waits for them, and re-layouts  9.49 us
    all_to_all x3, waiting for transfers between devices, exchange(): return lax.all_to_all(array, axis, 0, 0, tiled=True)  8.92 us
    ppermute x3, starting transfers between devices, turn(): lax.ppermute(a, axis, shift)  8.41 us
  transfers between devices with their start and end apart: 16, of which 8 were waited for; matrix products, arithmetic and copies ran while one was open for 3% of the time, Pallas kernels for 2%

profile of v5, /device:TPU:1, one launch (start us, length us, event | category | flops | bytes accessed | tf_op | source)
XLA Modules:
  0.0 190.6 jit_solution(10702176196063012078)
XLA Ops:
  7.2 3.3 %prep.1 = (bf16[8,288,128]{2,1,0:T(8,128)(2,1)}, bf16[288,1024]{1,0:T(8,128)(2,1)}) custom-call(bf16[288,1024]{1,0:T(8,128)(2,1)} %bitcast.39, s32[8,288]{1,0:T(8,128)} %bitcast.41, bf16[288,1024]{1,0:T(8,128)(2,1)} %base_ref.3), custom_call_target="tpu_custom_call" | custom-call | tf_op jit(solution)/shard_map/prep/pallas_call | solution.py:64
  10.5 10.5 %all-to-all-start = ((bf16[8,288,128]{2,1,0:T(8,128)(2,1)}), bf16[8,288,128]{2,1,0:T(8,128)(2,1)S(1)}, u32[]{:S(2)}, u32[]{:S(2)}) async-start(bf16[8,288,128]{2,1,0:T(8,128)(2,1)} %get-tuple-element.31.delta_ref), calls=%async_computation | async-start | bytes 1179648 | tf_op jit(solution)/shard_map/all_to_all | solution.py:383
  28.2 6.1 %collective-permute-done.refs_1_ = bf16[128,1152]{1,0:T(8,128)(2,1)S(1)} collective-permute-done((bf16[128,1152]{1,0:T(8,128)(2,1)}, bf16[128,1152]{1,0:T(8,128)(2,1)S(1)}, u32[]{:S(2)}, u32[]{:S(2)}) %collective-permute-start) | collective-permute-done | bytes 294944 | tf_op jit(solution)/shard_map/ppermute | solution.py:372
  34.4 5.8 %collective-permute-start.1 = (bf16[288,128]{1,0:T(8,128)(2,1)S(1)}, bf16[288,128]{1,0:T(8,128)(2,1)S(1)}, u32[]{:S(2)}, u32[]{:S(2)}) collective-permute-start(bf16[288,128]{1,0:T(8,128)(2,1)S(1)} %reduce_sum.12), channel_id=1, source_target_pairs={{0,32},{64,96},{32,0},{96,64},{1,33},{65,97},{33,1},{97,65},{2,34}... | collective-permute-start | bytes 221192 | tf_op jit(solution)/shard_map/ppermute | solution.py:354
  41.7 3.1 %collective-permute-start.6 = (bf16[128,768]{1,0:T(8,128)(2,1)}, bf16[128,768]{1,0:T(8,128)(2,1)S(1)}, u32[]{:S(2)}, u32[]{:S(2)}) collective-permute-start(bf16[128,768]{1,0:T(8,128)(2,1)} %pad_maximum_fusion.1), channel_id=1, source_target_pairs={{0,12},{4,0},{8,4},{12,8},{1,13},{5,1},{9,5},{13,9},{2,14},{6,2},{... | collective-permute-start | bytes 589832 | tf_op jit(solution)/shard_map/ppermute | solution.py:372
  44.8 1.9 %collective-permute-start.4 = (bf16[128,1152]{1,0:T(8,128)(2,1)}, bf16[128,1152]{1,0:T(8,128)(2,1)S(1)}, u32[]{:S(2)}, u32[]{:S(2)}) collective-permute-start(bf16[128,1152]{1,0:T(8,128)(2,1)} %get-tuple-element.60), channel_id=1, source_target_pairs={{0,12},{4,0},{8,4},{12,8},{1,13},{5,1},{9,5},{13,9},{2,14},{6,2},{... | collective-permute-start | bytes 884744 | tf_op jit(solution)/shard_map/ppermute | solution.py:372
  46.7 3.3 %collective-permute-start.3 = (bf16[128,1152]{1,0:T(8,128)(2,1)}, bf16[128,1152]{1,0:T(8,128)(2,1)S(1)}, u32[]{:S(2)}, u32[]{:S(2)}) collective-permute-start(bf16[128,1152]{1,0:T(8,128)(2,1)} %get-tuple-element.63), channel_id=1, source_target_pairs={{0,8},{4,12},{8,0},{12,4},{1,9},{5,13},{9,1},{13,5},{2,10},{6,14},... | collective-permute-start | bytes 884744 | tf_op jit(solution)/shard_map/ppermute | solution.py:372
  50.1 7.5 %collective-permute-start.2 = (bf16[288,128]{1,0:T(8,128)(2,1)S(1)}, bf16[288,128]{1,0:T(8,128)(2,1)S(1)}, u32[]{:S(2)}, u32[]{:S(2)}) collective-permute-start(bf16[288,128]{1,0:T(8,128)(2,1)S(1)} %add_convert_fusion.mine_ref), channel_id=1, source_target_pairs={{32,64},{96,0},{64,32},{0,96},{33,65},{97,1},{65,33},{1,97},{34,66... | collective-permute-start | bytes 221192 | tf_op jit(solution)/shard_map/ppermute | solution.py:354
  57.8 14.0 %collective-permute-done.3.refs_2_ = bf16[128,1152]{1,0:T(8,128)(2,1)S(1)} collective-permute-done((bf16[128,1152]{1,0:T(8,128)(2,1)}, bf16[128,1152]{1,0:T(8,128)(2,1)S(1)}, u32[]{:S(2)}, u32[]{:S(2)}) %collective-permute-start.3) | collective-permute-done | bytes 294944 | tf_op jit(solution)/shard_map/ppermute | solution.py:372
  73.5 5.3 %all-to-all-start.1 = ((bf16[16,288,128]{2,1,0:T(8,128)(2,1)}), bf16[16,288,128]{2,1,0:T(8,128)(2,1)S(1)}, u32[]{:S(2)}, u32[]{:S(2)}) async-start(bf16[16,288,128]{2,1,0:T(8,128)(2,1)} %outer_step.1), calls=%async_computation.1 | async-start | bytes 2359296 | tf_op jit(solution)/shard_map/all_to_all | solution.py:383
  78.8 2.7 %collective-permute-start.7 = (bf16[128,768]{1,0:T(8,128)(2,1)S(1)}, bf16[128,768]{1,0:T(8,128)(2,1)S(1)}, u32[]{:S(2)}, u32[]{:S(2)}) collective-permute-start(bf16[128,768]{1,0:T(8,128)(2,1)S(1)} %pad_maximum_fusion.3), channel_id=1, source_target_pairs={{0,8},{4,12},{8,0},{12,4},{1,9},{5,13},{9,1},{13,5},{2,10},{6,14},... | collective-permute-start | bytes 589832 | tf_op jit(solution)/shard_map/ppermute | solution.py:372
  82.3 4.2 %collective-permute-done.7.refs_2_ = bf16[128,768]{1,0:T(8,128)(2,1)S(1)} collective-permute-done((bf16[128,768]{1,0:T(8,128)(2,1)S(1)}, bf16[128,768]{1,0:T(8,128)(2,1)S(1)}, u32[]{:S(2)}, u32[]{:S(2)}) %collective-permute-start.7) | collective-permute-done | bytes 196640 | tf_op jit(solution)/shard_map/ppermute | solution.py:372
  87.1 7.5 %all-to-all-done.1.refs_5_ = bf16[16,288,128]{2,1,0:T(8,128)(2,1)S(1)} async-done(((bf16[16,288,128]{2,1,0:T(8,128)(2,1)}), bf16[16,288,128]{2,1,0:T(8,128)(2,1)S(1)}, u32[]{:S(2)}, u32[]{:S(2)}) %all-to-all-start.1) | async-done | bytes 1179680 | tf_op jit(solution)/shard_map/all_to_all | solution.py:383
  94.7 5.6 %collective-permute-start.8 = (bf16[16,288,128]{2,1,0:T(8,128)(2,1)S(1)}, bf16[16,288,128]{2,1,0:T(8,128)(2,1)S(1)}, u32[]{:S(2)}, u32[]{:S(2)}) collective-permute-start(bf16[16,288,128]{2,1,0:T(8,128)(2,1)S(1)} %all-to-all-done.1.refs_5_), channel_id=1, source_target_pairs={{0,16},{16,0},{1,17},{17,1},{2,18},{18,2},{3,19},{19,3},{4,20},{20... | collective-permute-start | bytes 3538952 | tf_op jit(solution)/shard_map/ppermute | solution.py:407
  100.3 2.5 %collective-permute-done.8.refs_6_ = bf16[16,288,128]{2,1,0:T(8,128)(2,1)S(1)} collective-permute-done((bf16[16,288,128]{2,1,0:T(8,128)(2,1)S(1)}, bf16[16,288,128]{2,1,0:T(8,128)(2,1)S(1)}, u32[]{:S(2)}, u32[]{:S(2)}) %collective-permute-start.8) | collective-permute-done | bytes 1179680 | tf_op jit(solution)/shard_map/ppermute | solution.py:407
  104.7 5.6 %project.1 = bf16[4,512,256]{2,1,0:T(8,128)(2,1)S(1)} custom-call(s32[4]{0:T(128)S(1)} %pad_add_fusion.place_ref, bf16[128,1152]{1,0:T(8,128)(2,1)S(1)} %get-tuple-element.62.refs_0_, bf16[128,1152]{1,0:T(8,128)(2,1)S(1)} %collective-permute-done.refs_1_, bf16[128,1152]{1,0:T(8,128)(2,1)S(1)} %copy-done.8, bf16[128,1152]{1,0:T(8,128)(2,1)S(1)} %copy-done.6, ...), custom_call_target="tpu_custom_call" | custom-call | tf_op jit(solution)/shard_map/project/pallas_call | solution.py:159
  111.3 10.2 %all-to-all-start.2 = ((bf16[4,512,256]{2,1,0:T(8,128)(2,1)}), bf16[4,512,256]{2,1,0:T(8,128)(2,1)}, u32[]{:S(2)}, u32[]{:S(2)}) async-start(bf16[4,512,256]{2,1,0:T(8,128)(2,1)} %copy-done.1), calls=%async_computation.2 | async-start | bytes 2097152 | tf_op jit(solution)/shard_map/all_to_all | solution.py:383
  126.4 2.2 %collective-permute-start.9 = (bf16[512,256]{1,0:T(8,128)(2,1)S(1)}, bf16[512,256]{1,0:T(8,128)(2,1)S(1)}, u32[]{:S(2)}, u32[]{:S(2)}) collective-permute-start(bf16[512,256]{1,0:T(8,128)(2,1)S(1)} %get-tuple-element.51), channel_id=1, source_target_pairs={{0,1},{1,2},{2,3},{3,0},{4,5},{5,6},{6,7},{7,4},{8,9},{9,10},{10,1... | collective-permute-start | bytes 786440 | tf_op jit(solution)/shard_map/ppermute | solution.py:379
  128.6 2.6 %collective-permute-start.10 = (bf16[512,256]{1,0:T(8,128)(2,1)S(1)}, bf16[512,256]{1,0:T(8,128)(2,1)S(1)}, u32[]{:S(2)}, u32[]{:S(2)}) collective-permute-start(bf16[512,256]{1,0:T(8,128)(2,1)S(1)} %get-tuple-element.52), channel_id=1, source_target_pairs={{0,2},{1,3},{2,0},{3,1},{4,6},{5,7},{6,4},{7,5},{8,10},{9,11},{10,... | collective-permute-start | bytes 786440 | tf_op jit(solution)/shard_map/ppermute | solution.py:379
  131.2 3.6 %collective-permute-start.11 = (bf16[512,256]{1,0:T(8,128)(2,1)S(1)}, bf16[512,256]{1,0:T(8,128)(2,1)S(1)}, u32[]{:S(2)}, u32[]{:S(2)}) collective-permute-start(bf16[512,256]{1,0:T(8,128)(2,1)S(1)} %get-tuple-element.53), channel_id=1, source_target_pairs={{0,3},{1,0},{2,1},{3,2},{4,7},{5,4},{6,5},{7,6},{8,11},{9,8},{10,9... | collective-permute-start | bytes 786440 | tf_op jit(solution)/shard_map/ppermute | solution.py:379
  136.7 5.6 %collective-permute-done.9.refs_1_ = bf16[512,256]{1,0:T(8,128)(2,1)S(1)} collective-permute-done((bf16[512,256]{1,0:T(8,128)(2,1)S(1)}, bf16[512,256]{1,0:T(8,128)(2,1)S(1)}, u32[]{:S(2)}, u32[]{:S(2)}) %collective-permute-start.9) | collective-permute-done | bytes 262176 | tf_op jit(solution)/shard_map/ppermute | solution.py:379
  148.4 11.6 %all_to_all.25.keys_any = bf16[4,512,128]{2,1,0:T(8,128)(2,1)S(1)} all-to-all(bf16[4,512,128]{2,1,0:T(8,128)(2,1)S(1)} %reduce_keys.1), channel_id=1, replica_groups=mesh['x'=4,'zh'=4,'c'=2,'zl'=4,'y'=4] {'y'}, dimensions={0} | all-to-all | bytes 1048576 | tf_op jit(solution)/shard_map/all_to_all | solution.py:383
  160.0 5.1 %attend.1 = bf16[16,128,128]{2,1,0:T(8,128)(2,1)S(1)} custom-call(s32[4]{0:T(128)S(1)} %pad_add_fusion.place_ref, bf16[4,512,128]{2,1,0:T(8,128)(2,1)S(1)} %all_to_all.25.keys_any, bf16[512,256]{1,0:T(8,128)(2,1)S(1)} %copy-done.10, bf16[512,256]{1,0:T(8,128)(2,1)S(1)} %copy-done.12, bf16[512,256]{1,0:T(8,128)(2,1)S(1)} %copy-done.14, ...), custom_call_target="tpu_custom_call" | custom-call | tf_op jit(solution)/shard_map/attend/pallas_call | solution.py:319
  165.1 17.7 %all_to_all.26.mixed_any = bf16[16,128,128]{2,1,0:T(8,128)(2,1)S(1)} all-to-all(bf16[16,128,128]{2,1,0:T(8,128)(2,1)S(1)} %attend.1), channel_id=1, replica_groups=mesh['x'=4,'zh'=4,'c'=2,'zl'=4,'y'=4] {'zl','y'}, dimensions={0} | all-to-all | bytes 1048576 | tf_op jit(solution)/shard_map/all_to_all | solution.py:383
  (81 shorter events, 28.7 us)
Async XLA Ops:
  7.2 95.6 %all-gather.2.cloned.1.call-start = ((), (), s32[]{:S(2)}) async-start(), calls=%async_computation.5 | async-start | bytes 2949120 | tf_op jit(solution)/shard_map/all_gather | solution.py:391
  10.5 23.8 %all-to-all-start = ((bf16[8,288,128]{2,1,0:T(8,128)(2,1)}), bf16[8,288,128]{2,1,0:T(8,128)(2,1)S(1)}, u32[]{:S(2)}, u32[]{:S(2)}) async-start(bf16[8,288,128]{2,1,0:T(8,128)(2,1)} %get-tuple-element.31.delta_ref), calls=%async_computation | async-start | bytes 1179648 | tf_op jit(solution)/shard_map/all_to_all | solution.py:383
  21.9 12.3 %collective-permute-start = (bf16[128,1152]{1,0:T(8,128)(2,1)}, bf16[128,1152]{1,0:T(8,128)(2,1)S(1)}, u32[]{:S(2)}, u32[]{:S(2)}) collective-permute-start(bf16[128,1152]{1,0:T(8,128)(2,1)} %get-tuple-element.61), channel_id=1, source_target_pairs={{0,4},{4,8},{8,12},{12,0},{1,5},{5,9},{9,13},{13,1},{2,6},{6,10},{... | collective-permute-start | bytes 884744 | tf_op jit(solution)/shard_map/ppermute | solution.py:372
  24.6 47.2 %copy-start = (bf16[288,1024]{1,0:T(8,128)(2,1)S(1)}, bf16[288,1024]{1,0:T(8,128)(2,1)}, u32[]{:S(2)}) copy-start(bf16[288,1024]{1,0:T(8,128)(2,1)} %base_ref.3) | copy-start | bytes 1769476
  24.6 47.2 %copy-start.4 = (bf16[288,1024]{1,0:T(8,128)(2,1)S(1)}, bf16[288,1024]{1,0:T(8,128)(2,1)}, u32[]{:S(2)}) copy-start(bf16[288,1024]{1,0:T(8,128)(2,1)} %momentum_ref.1) | copy-start | bytes 1769476
  26.2 31.5 %collective-permute-start.5 = (bf16[128,768]{1,0:T(8,128)(2,1)}, bf16[128,768]{1,0:T(8,128)(2,1)S(1)}, u32[]{:S(2)}, u32[]{:S(2)}) collective-permute-start(bf16[128,768]{1,0:T(8,128)(2,1)} %pad_maximum_fusion), channel_id=1, source_target_pairs={{0,4},{4,8},{8,12},{12,0},{1,5},{5,9},{9,13},{13,1},{2,6},{6,10},{... | collective-permute-start | bytes 589832 | tf_op jit(solution)/shard_map/ppermute | solution.py:372
  34.4 15.7 %collective-permute-start.1 = (bf16[288,128]{1,0:T(8,128)(2,1)S(1)}, bf16[288,128]{1,0:T(8,128)(2,1)S(1)}, u32[]{:S(2)}, u32[]{:S(2)}) collective-permute-start(bf16[288,128]{1,0:T(8,128)(2,1)S(1)} %reduce_sum.12), channel_id=1, source_target_pairs={{0,32},{64,96},{32,0},{96,64},{1,33},{65,97},{33,1},{97,65},{2,34}... | collective-permute-start | bytes 221192 | tf_op jit(solution)/shard_map/ppermute | solution.py:354
  41.7 16.1 %collective-permute-start.6 = (bf16[128,768]{1,0:T(8,128)(2,1)}, bf16[128,768]{1,0:T(8,128)(2,1)S(1)}, u32[]{:S(2)}, u32[]{:S(2)}) collective-permute-start(bf16[128,768]{1,0:T(8,128)(2,1)} %pad_maximum_fusion.1), channel_id=1, source_target_pairs={{0,12},{4,0},{8,4},{12,8},{1,13},{5,1},{9,5},{13,9},{2,14},{6,2},{... | collective-permute-start | bytes 589832 | tf_op jit(solution)/shard_map/ppermute | solution.py:372
  44.8 12.9 %collective-permute-start.4 = (bf16[128,1152]{1,0:T(8,128)(2,1)}, bf16[128,1152]{1,0:T(8,128)(2,1)S(1)}, u32[]{:S(2)}, u32[]{:S(2)}) collective-permute-start(bf16[128,1152]{1,0:T(8,128)(2,1)} %get-tuple-element.60), channel_id=1, source_target_pairs={{0,12},{4,0},{8,4},{12,8},{1,13},{5,1},{9,5},{13,9},{2,14},{6,2},{... | collective-permute-start | bytes 884744 | tf_op jit(solution)/shard_map/ppermute | solution.py:372
  46.7 25.0 %collective-permute-start.3 = (bf16[128,1152]{1,0:T(8,128)(2,1)}, bf16[128,1152]{1,0:T(8,128)(2,1)S(1)}, u32[]{:S(2)}, u32[]{:S(2)}) collective-permute-start(bf16[128,1152]{1,0:T(8,128)(2,1)} %get-tuple-element.63), channel_id=1, source_target_pairs={{0,8},{4,12},{8,0},{12,4},{1,9},{5,13},{9,1},{13,5},{2,10},{6,14},... | collective-permute-start | bytes 884744 | tf_op jit(solution)/shard_map/ppermute | solution.py:372
  50.1 21.6 %collective-permute-start.2 = (bf16[288,128]{1,0:T(8,128)(2,1)S(1)}, bf16[288,128]{1,0:T(8,128)(2,1)S(1)}, u32[]{:S(2)}, u32[]{:S(2)}) collective-permute-start(bf16[288,128]{1,0:T(8,128)(2,1)S(1)} %add_convert_fusion.mine_ref), channel_id=1, source_target_pairs={{32,64},{96,0},{64,32},{0,96},{33,65},{97,1},{65,33},{1,97},{34,66... | collective-permute-start | bytes 221192 | tf_op jit(solution)/shard_map/ppermute | solution.py:354
  57.7 15.8 %copy-start.17 = (bf16[128,768]{1,0:T(8,128)(2,1)}, bf16[128,768]{1,0:T(8,128)(2,1)S(1)}, u32[]{:S(2)}) copy-start(bf16[128,768]{1,0:T(8,128)(2,1)S(1)} %collective-permute-done.5.refs_1_) | copy-start | bytes 589828
  57.7 15.8 %copy-start.19 = (bf16[128,768]{1,0:T(8,128)(2,1)}, bf16[128,768]{1,0:T(8,128)(2,1)S(1)}, u32[]{:S(2)}) copy-start(bf16[128,768]{1,0:T(8,128)(2,1)S(1)} %collective-permute-done.6.refs_3_) | copy-start | bytes 589828
  57.7 15.8 %copy-start.5 = (bf16[128,1152]{1,0:T(8,128)(2,1)}, bf16[128,1152]{1,0:T(8,128)(2,1)S(1)}, u32[]{:S(2)}) copy-start(bf16[128,1152]{1,0:T(8,128)(2,1)S(1)} %collective-permute-done.4.refs_3_) | copy-start | bytes 884740
  73.5 21.1 %all-to-all-start.1 = ((bf16[16,288,128]{2,1,0:T(8,128)(2,1)}), bf16[16,288,128]{2,1,0:T(8,128)(2,1)S(1)}, u32[]{:S(2)}, u32[]{:S(2)}) async-start(bf16[16,288,128]{2,1,0:T(8,128)(2,1)} %outer_step.1), calls=%async_computation.1 | async-start | bytes 2359296 | tf_op jit(solution)/shard_map/all_to_all | solution.py:383
  78.8 7.6 %collective-permute-start.7 = (bf16[128,768]{1,0:T(8,128)(2,1)S(1)}, bf16[128,768]{1,0:T(8,128)(2,1)S(1)}, u32[]{:S(2)}, u32[]{:S(2)}) collective-permute-start(bf16[128,768]{1,0:T(8,128)(2,1)S(1)} %pad_maximum_fusion.3), channel_id=1, source_target_pairs={{0,8},{4,12},{8,0},{12,4},{1,9},{5,13},{9,1},{13,5},{2,10},{6,14},... | collective-permute-start | bytes 589832 | tf_op jit(solution)/shard_map/ppermute | solution.py:372
  94.7 8.1 %collective-permute-start.8 = (bf16[16,288,128]{2,1,0:T(8,128)(2,1)S(1)}, bf16[16,288,128]{2,1,0:T(8,128)(2,1)S(1)}, u32[]{:S(2)}, u32[]{:S(2)}) collective-permute-start(bf16[16,288,128]{2,1,0:T(8,128)(2,1)S(1)} %all-to-all-done.1.refs_5_), channel_id=1, source_target_pairs={{0,16},{16,0},{1,17},{17,1},{2,18},{18,2},{3,19},{19,3},{4,20},{20... | collective-permute-start | bytes 3538952 | tf_op jit(solution)/shard_map/ppermute | solution.py:407
  111.3 23.5 %copy-start.2 = (bf16[8,288,128]{2,1,0:T(8,128)(2,1)S(1)}, bf16[8,288,128]{2,1,0:T(8,128)(2,1)}, u32[]{:S(2)}) copy-start(bf16[8,288,128]{2,1,0:T(8,128)(2,1)} %get-tuple-element.31.delta_ref) | copy-start | bytes 1769476
  111.3 35.6 %all-to-all-start.2 = ((bf16[4,512,256]{2,1,0:T(8,128)(2,1)}), bf16[4,512,256]{2,1,0:T(8,128)(2,1)}, u32[]{:S(2)}, u32[]{:S(2)}) async-start(bf16[4,512,256]{2,1,0:T(8,128)(2,1)} %copy-done.1), calls=%async_computation.2 | async-start | bytes 2097152 | tf_op jit(solution)/shard_map/all_to_all | solution.py:383
  126.4 15.9 %collective-permute-start.9 = (bf16[512,256]{1,0:T(8,128)(2,1)S(1)}, bf16[512,256]{1,0:T(8,128)(2,1)S(1)}, u32[]{:S(2)}, u32[]{:S(2)}) collective-permute-start(bf16[512,256]{1,0:T(8,128)(2,1)S(1)} %get-tuple-element.51), channel_id=1, source_target_pairs={{0,1},{1,2},{2,3},{3,0},{4,5},{5,6},{6,7},{7,4},{8,9},{9,10},{10,1... | collective-permute-start | bytes 786440 | tf_op jit(solution)/shard_map/ppermute | solution.py:379
  128.6 14.4 %collective-permute-start.10 = (bf16[512,256]{1,0:T(8,128)(2,1)S(1)}, bf16[512,256]{1,0:T(8,128)(2,1)S(1)}, u32[]{:S(2)}, u32[]{:S(2)}) collective-permute-start(bf16[512,256]{1,0:T(8,128)(2,1)S(1)} %get-tuple-element.52), channel_id=1, source_target_pairs={{0,2},{1,3},{2,0},{3,1},{4,6},{5,7},{6,4},{7,5},{8,10},{9,11},{10,... | collective-permute-start | bytes 786440 | tf_op jit(solution)/shard_map/ppermute | solution.py:379
  131.2 13.6 %collective-permute-start.11 = (bf16[512,256]{1,0:T(8,128)(2,1)S(1)}, bf16[512,256]{1,0:T(8,128)(2,1)S(1)}, u32[]{:S(2)}, u32[]{:S(2)}) collective-permute-start(bf16[512,256]{1,0:T(8,128)(2,1)S(1)} %get-tuple-element.53), channel_id=1, source_target_pairs={{0,3},{1,0},{2,1},{3,2},{4,7},{5,4},{6,5},{7,6},{8,11},{9,8},{10,9... | collective-permute-start | bytes 786440 | tf_op jit(solution)/shard_map/ppermute | solution.py:379
  146.9 13.1 %copy-start.14 = (bf16[512,256]{1,0:T(8,128)(2,1)S(1)}, bf16[512,256]{1,0:T(8,128)(2,1)}, u32[]{:S(2)}) copy-start(bf16[512,256]{1,0:T(8,128)(2,1)} %copy-done.13) | copy-start | bytes 786436
  146.9 13.1 %copy-start.16 = (bf16[512,256]{1,0:T(8,128)(2,1)S(1)}, bf16[512,256]{1,0:T(8,128)(2,1)}, u32[]{:S(2)}) copy-start(bf16[512,256]{1,0:T(8,128)(2,1)} %copy-done.15) | copy-start | bytes 786436
  (18 other events, 64.7 us)
Sparse Core Ops, SparseCore 0:
  10.6 46.0 all-gather.1

commit v6 on v5

--- a/solution.py
+++ b/solution.py
@@ -108,71 +108,87 @@
     )(place, mine, sent, base, momentum)
 
 
-def project_kernel(place_ref, *refs):
-    hidden_any, (part_any, same_any, other_any) = refs[:4], refs[4:7]
-    out_ref, hidden, parts, outer, weight, part_sems, sems, hidden_sems = refs[7:]
-    rows = outer.shape[1]
-    c, z = place_ref[0], place_ref[1]
-    part_copies, outer_copies, hidden_copies = [], [], []
+def local_kernel(place_ref, *refs):
+    pieces, part_any, hidden_ref, out_ref, part, sems = refs[:4], *refs[4:]
+    z = place_ref[1]
+    copies = []
+    for s in range(NZL):
+        to = pl.ds(pl.multiple_of(lax.rem(z - s + NZL, NZL) * 128, 128), 128)
+        copies.append(pltpu.make_async_copy(pieces[s], hidden_ref.at[to], sems.at[s]))
     for n in range(NZL):
-        cols = pl.ds(n * 2 * BLOCK, 2 * BLOCK)
-        part_copies.append(
-            pltpu.make_async_copy(part_any.at[:, cols], parts.at[n], part_sems.at[n])
+        cols = pl.ds(n * 256, 256)
+        copies.append(pltpu.make_async_copy(part_any.at[:, cols], part.at[n], sems.at[NZL + n]))
+    start_all(copies)
+    for copy in copies[:NZL]:
+        copy.wait()
+    for n in range(NZL):
+        copies[NZL + n].wait()
+        out_ref[n] = blend_share * jnp.dot(
+            hidden_ref[...], part[n], preferred_element_type=jnp.float32
         )
+
+
+def local_product(place, hidden, part):
+    depth = part.shape[0]
+    return pl.pallas_call(
+        local_kernel,
+        out_shape=(
+            jax.ShapeDtypeStruct((512, depth), jnp.bfloat16),
+            jax.ShapeDtypeStruct((NZL, 512, 256), jnp.float32),
+        ),
+        in_specs=[SMEM] + [ANY] * 5,
+        out_specs=(VMEM, VMEM),
+        scratch_shapes=[
+            pltpu.VMEM((NZL, depth, 256), jnp.bfloat16),
+            pltpu.SemaphoreType.DMA((2 * NZL,)),
+        ],
+        compiler_params=params(),
+        name="local_product",
+    )(place, *hidden, part)
+
+
+def project_kernel(place_ref, hidden_any, local_any, same_any, other_any, out_ref, *refs):
+    hidden, local, weight, sems, local_sems, hidden_sem = refs
+    c = place_ref[0]
+    hidden_copy = pltpu.make_async_copy(hidden_any, hidden, hidden_sem)
+    copies = []
+    for n in range(NZL):
         for near, source in enumerate((same_any, other_any)):
-            half = lax.rem(c + near, NC)
-            at = pl.ds((n * NC + half) * NY, NY)
-            outer_copies.append(
+            at = pl.multiple_of(lax.rem(c + near, NC) * BLOCK, BLOCK)
+            copies.append(
                 pltpu.make_async_copy(
-                    source.at[pl.ds(n * NY, NY)], outer.at[at], sems.at[n * NC + near]
+                    source.at[n], weight.at[n, :, pl.ds(at, BLOCK)], sems.at[n, near]
                 )
             )
-    for s in range(NZL):
-        to = pl.ds(pl.multiple_of(lax.rem(z - s + NZL, NZL) * 128, 128), 128)
-        hidden_copies.append(
-            pltpu.make_async_copy(hidden_any[s], hidden.at[to], hidden_sems.at[s])
-        )
-    start_all([part_copies[0]] + outer_copies[:2] + hidden_copies)
-    for n in range(1, NZL):
-        start_all([part_copies[n]] + outer_copies[2 * n : 2 * n + 2])
+        copies.append(pltpu.make_async_copy(local_any.at[n], local.at[n], local_sems.at[n]))
+    start_all(copies[:2] + [hidden_copy] + copies[2:])
+    hidden_copy.wait()
     for n in range(NZL):
-        for copy in [part_copies[n]] + outer_copies[2 * n : 2 * n + 2]:
+        for copy in copies[3 * n : 3 * n + 3]:
             copy.wait()
-        for half in range(NC):
-            cols = slice(half * BLOCK, (half + 1) * BLOCK)
-            for y in range(NY):
-                at = slice(y * rows, (y + 1) * rows)
-                blend = blend_share * parts[n, at, cols].astype(jnp.float32)
-                piece = outer[(n * NC + half) * NY + y].astype(jnp.float32)
-                blend += (1.0 - blend_share) * piece
-                weight[n, at, cols] = blend.astype(jnp.bfloat16)
-        if n == 0:
-            for copy in hidden_copies:
-                copy.wait()
-        keys = jnp.dot(hidden[...], weight[n], preferred_element_type=jnp.float32)
-        out_ref[n] = keys.astype(jnp.bfloat16)
-
-
-def project(place, hidden, part, same, other):
-    rows = same.shape[1]
-    depth = NY * rows
+        outer = jnp.dot(hidden[...], weight[n], preferred_element_type=jnp.float32)
+        out_ref[n] = (local[n] + (1.0 - blend_share) * outer).astype(jnp.bfloat16)
+
+
+def project(place, hidden, local, same, other):
+    depth = hidden.shape[1]
+    blocks = (NZL, depth, BLOCK)
     return pl.pallas_call(
         project_kernel,
         out_shape=jax.ShapeDtypeStruct((NZL, 512, 2 * BLOCK), jnp.bfloat16),
-        in_specs=[SMEM] + [ANY] * 7,
+        in_specs=[SMEM] + [ANY] * 4,
         out_specs=VMEM,
         scratch_shapes=[
             pltpu.VMEM((512, depth), jnp.bfloat16),
+            pltpu.VMEM((NZL, 512, 256), jnp.float32),
             pltpu.VMEM((NZL, depth, 2 * BLOCK), jnp.bfloat16),
-            pltpu.VMEM((NZL * NC * NY, rows, BLOCK), jnp.bfloat16),
-            pltpu.VMEM((NZL, depth, 2 * BLOCK), jnp.bfloat16),
+            pltpu.SemaphoreType.DMA((NZL, 2)),
             pltpu.SemaphoreType.DMA((NZL,)),
-            pltpu.SemaphoreType.DMA((NZL * NC,)),
-            pltpu.SemaphoreType.DMA((NZL,)),
+            pltpu.SemaphoreType.DMA,
         ],
-        compiler_params=params(48),
+        compiler_params=params(),
         name="project",
-    )(place, *hidden, part, same, other)
+    )(place, hidden, local, same.reshape(blocks), other.reshape(blocks))
 
 
 def reduce_kernel(sums_ref, out_ref):
@@ -395,18 +411,20 @@
     sent, hidden_here[1] = lax.optimization_barrier((sent, hidden_here[1]))
     eighth = jnp.sum(sent.astype(jnp.float32), axis=0).astype(jnp.bfloat16)
     pair = add(eighth, swap(eighth, "zh", [(0, 1), (2, 3)])).astype(jnp.bfloat16)
+    pair, hidden_here[2] = lax.optimization_barrier((pair, hidden_here[2]))
     swapped = swap(pair, "zh", [(1, 2), (3, 0)])
     both = deal([queries[0], values[0]], "zl")
-    swapped, hidden_here[2], hidden_here[3], both[1], both[3] = lax.optimization_barrier(
-        (swapped, hidden_here[2], hidden_here[3], both[1], both[3])
+    swapped, hidden_here[3], both[1], both[3] = lax.optimization_barrier(
+        (swapped, hidden_here[3], both[1], both[3])
     )
     outer = outer_step(place, pair, swapped, base, momentum)
 
     same = exchange(outer, ("x", "y"))
-    same, *both = lax.optimization_barrier((same, *both))
+    ordered, local = local_product(place, hidden_here, part_all)
+    same, ordered, local, *both = lax.optimization_barrier((same, ordered, local, *both))
     other = lax.ppermute(same, "c", [(0, 1), (1, 0)])
 
-    sums = project(place, hidden_here, part_all, same, other)
+    sums = project(place, ordered, local, same, other)
     sums, *both = lax.optimization_barrier((sums, *both))
     sums = exchange(sums, "zl")
     by_head = turn(list(regroup(place, both)), "y")

time: 193 us -> 191 us (0.990)
  waiting for transfers between devices: 42.4 us -> 22.8 us
  starting transfers between devices: 68.2 us -> 79.1 us
  Pallas kernels: 21.1 us -> 30 us
    ppermute x6, waiting for transfers between devices: 24.3 us -> 9.97 us  [deal(): piece = lax.ppermute(piece, axis, [(i, (i + step) % 4) for i in range(4)])]
    ppermute x6, starting transfers between devices: 14.9 us -> 26.2 us  [deal(): piece = lax.ppermute(piece, axis, [(i, (i + step) % 4) for i in range(4)])]
    all_to_all x3, waiting for transfers between devices: 8.92 us -> 1.38 us  [exchange(): return lax.all_to_all(array, axis, 0, 0, tiled=True)]
    pallas_call x0 -> x1, Pallas kernels: none -> 6.81 us  [local_product(): pl.pallas_call(local_kernel, out_shape=(jax.ShapeDtypeStruct((512, depth)...]
    all_to_all x3, starting transfers between devices: 26 us -> 29.4 us  [exchange(): return lax.all_to_all(array, axis, 0, 0, tiled=True)]
    ppermute x1, starting transfers between devices: 5.64 us -> 2.95 us  [on_device(): other = lax.ppermute(same, 'c', [(0, 1), (1, 0)])]
    ppermute x2, waiting for transfers between devices: 0.01 us -> 2.41 us  [swap(): return lax.ppermute(array, axis, pairs + [(b, a) for a, b in pairs])]
    pallas_call x1, Pallas kernels: 5.64 us -> 7.62 us  [project(): pl.pallas_call(project_kernel, out_shape=jax.ShapeDtypeStruct((NZL, 512,...]
  transfers between devices with their start and end apart: 16 -> 16, of which waited for: 8 -> 9; matrix products, arithmetic and copies ran while one was open for 3% -> 3% of each run, Pallas kernels for 2% -> 6%
where the time goes in v6:
time: 191 us; the launch traced here: 188 us
  starting transfers between devices  79.1 us (41%)
  Pallas kernels  30 us (16%)
  blocking collectives  29.3 us (15%)
  waiting for transfers between devices  22.8 us (12%)
  between operations  14.5 us (8%)
  local copies, waits for them, and re-layouts  9.3 us (5%)
  other arithmetic  3.11 us (2%)
    all_to_all x3, starting transfers between devices, exchange(): return lax.all_to_all(array, axis, 0, 0, tiled=True)  29.4 us
    all_to_all x2, blocking collectives, exchange(): return lax.all_to_all(array, axis, 0, 0, tiled=True)  29.3 us
    ppermute x6, starting transfers between devices, deal(): piece = lax.ppermute(piece, axis, [(i, (i + step) % 4) for i in range(4)])  26.2 us
    ppermute x2, starting transfers between devices, swap(): return lax.ppermute(array, axis, pairs + [(b, a) for a, b in pairs])  12.1 us
    ppermute x6, waiting for transfers between devices, deal(): piece = lax.ppermute(piece, axis, [(i, (i + step) % 4) for i in range(4)])  9.97 us
    ppermute x3, starting transfers between devices, turn(): lax.ppermute(a, axis, shift)  8.49 us
    unnamed x62, local copies, waits for them, and re-layouts  7.64 us
    pallas_call x1, Pallas kernels, project(): pl.pallas_call(project_kernel, out_shape=jax.ShapeDtypeStruct((NZL, 512,...  7.62 us
  transfers between devices with their start and end apart: 16, of which 9 were waited for; matrix products, arithmetic and copies ran while one was open for 3% of the time, Pallas kernels for 6%

profile of v6, /device:TPU:1, one launch (start us, length us, event | category | flops | bytes accessed | tf_op | source)
XLA Modules:
  0.0 188.0 jit_solution(10342159944057301463)
XLA Ops:
  7.2 3.3 %prep.1 = (bf16[8,288,128]{2,1,0:T(8,128)(2,1)}, bf16[288,1024]{1,0:T(8,128)(2,1)}) custom-call(bf16[288,1024]{1,0:T(8,128)(2,1)} %bitcast.43, s32[8,288]{1,0:T(8,128)} %bitcast.45, bf16[288,1024]{1,0:T(8,128)(2,1)} %base_ref.3), custom_call_target="tpu_custom_call" | custom-call | tf_op jit(solution)/shard_map/prep/pallas_call | solution.py:64
  10.5 10.5 %all-to-all-start = ((bf16[8,288,128]{2,1,0:T(8,128)(2,1)}), bf16[8,288,128]{2,1,0:T(8,128)(2,1)S(1)}, u32[]{:S(2)}, u32[]{:S(2)}) async-start(bf16[8,288,128]{2,1,0:T(8,128)(2,1)} %get-tuple-element.36.delta_ref), calls=%async_computation | async-start | bytes 1179648 | tf_op jit(solution)/shard_map/all_to_all | solution.py:399
  27.3 5.4 %collective-permute-start.2 = (bf16[128,1152]{1,0:T(8,128)(2,1)}, bf16[128,1152]{1,0:T(8,128)(2,1)S(1)}, u32[]{:S(2)}, u32[]{:S(2)}) collective-permute-start(bf16[128,1152]{1,0:T(8,128)(2,1)} %get-tuple-element.71), channel_id=1, source_target_pairs={{0,8},{4,12},{8,0},{12,4},{1,9},{5,13},{9,1},{13,5},{2,10},{6,14},... | collective-permute-start | bytes 884744 | tf_op jit(solution)/shard_map/ppermute | solution.py:388
  34.4 5.8 %collective-permute-start.1 = (bf16[288,128]{1,0:T(8,128)(2,1)S(1)}, bf16[288,128]{1,0:T(8,128)(2,1)S(1)}, u32[]{:S(2)}, u32[]{:S(2)}) collective-permute-start(bf16[288,128]{1,0:T(8,128)(2,1)S(1)} %reduce_sum.12), channel_id=1, source_target_pairs={{0,32},{64,96},{32,0},{96,64},{1,33},{65,97},{33,1},{97,65},{2,34}... | collective-permute-start | bytes 221192 | tf_op jit(solution)/shard_map/ppermute | solution.py:370
  41.7 3.1 %collective-permute-start.6 = (bf16[128,768]{1,0:T(8,128)(2,1)}, bf16[128,768]{1,0:T(8,128)(2,1)S(1)}, u32[]{:S(2)}, u32[]{:S(2)}) collective-permute-start(bf16[128,768]{1,0:T(8,128)(2,1)} %pad_maximum_fusion.1), channel_id=1, source_target_pairs={{0,12},{4,0},{8,4},{12,8},{1,13},{5,1},{9,5},{13,9},{2,14},{6,2},{... | collective-permute-start | bytes 589832 | tf_op jit(solution)/shard_map/ppermute | solution.py:388
  44.8 1.9 %collective-permute-start.4 = (bf16[128,1152]{1,0:T(8,128)(2,1)S(1)}, bf16[128,1152]{1,0:T(8,128)(2,1)S(1)}, u32[]{:S(2)}, u32[]{:S(2)}) collective-permute-start(bf16[128,1152]{1,0:T(8,128)(2,1)S(1)} %get-tuple-element.73), channel_id=1, source_target_pairs={{0,12},{4,0},{8,4},{12,8},{1,13},{5,1},{9,5},{13,9},{2,14},{6,2},{... | collective-permute-start | bytes 884744 | tf_op jit(solution)/shard_map/ppermute | solution.py:388
  46.8 8.1 %collective-permute-done.2.refs_2_ = bf16[128,1152]{1,0:T(8,128)(2,1)S(1)} collective-permute-done((bf16[128,1152]{1,0:T(8,128)(2,1)}, bf16[128,1152]{1,0:T(8,128)(2,1)S(1)}, u32[]{:S(2)}, u32[]{:S(2)}) %collective-permute-start.2) | collective-permute-done | bytes 294944 | tf_op jit(solution)/shard_map/ppermute | solution.py:388
  54.9 6.3 %collective-permute-start.3 = (bf16[288,128]{1,0:T(8,128)(2,1)S(1)}, bf16[288,128]{1,0:T(8,128)(2,1)S(1)}, u32[]{:S(2)}, u32[]{:S(2)}) collective-permute-start(bf16[288,128]{1,0:T(8,128)(2,1)S(1)} %add_convert_fusion.mine_ref), channel_id=1, source_target_pairs={{32,64},{96,0},{64,32},{0,96},{33,65},{97,1},{65,33},{1,97},{34,66... | collective-permute-start | bytes 221192 | tf_op jit(solution)/shard_map/ppermute | solution.py:370
  61.6 2.4 %collective-permute-done.3.sent_ref = bf16[288,128]{1,0:T(8,128)(2,1)S(1)} collective-permute-done((bf16[288,128]{1,0:T(8,128)(2,1)S(1)}, bf16[288,128]{1,0:T(8,128)(2,1)S(1)}, u32[]{:S(2)}, u32[]{:S(2)}) %collective-permute-start.3) | collective-permute-done | bytes 73760 | tf_op jit(solution)/shard_map/ppermute | solution.py:370
  65.9 6.7 %all-to-all-start.1 = ((bf16[16,288,128]{2,1,0:T(8,128)(2,1)}), bf16[16,288,128]{2,1,0:T(8,128)(2,1)S(1)}, u32[]{:S(2)}, u32[]{:S(2)}) async-start(bf16[16,288,128]{2,1,0:T(8,128)(2,1)} %outer_step.1), calls=%async_computation.1 | async-start | bytes 2359296 | tf_op jit(solution)/shard_map/all_to_all | solution.py:399
  72.6 11.9 %collective-permute-start.7 = (bf16[128,768]{1,0:T(8,128)(2,1)S(1)}, bf16[128,768]{1,0:T(8,128)(2,1)S(1)}, u32[]{:S(2)}, u32[]{:S(2)}) collective-permute-start(bf16[128,768]{1,0:T(8,128)(2,1)S(1)} %pad_maximum_fusion.3), channel_id=1, source_target_pairs={{0,8},{4,12},{8,0},{12,4},{1,9},{5,13},{9,1},{13,5},{2,10},{6,14},... | collective-permute-start | bytes 589832 | tf_op jit(solution)/shard_map/ppermute | solution.py:388
  85.1 6.8 %local_product.1 = (bf16[512,1152]{1,0:T(8,128)(2,1)}, f32[4,512,256]{2,1,0:T(8,128)}) custom-call(s32[4]{0:T(128)} %copy-done.22, bf16[128,1152]{1,0:T(8,128)(2,1)} %get-tuple-element.70.refs_0_, bf16[128,1152]{1,0:T(8,128)(2,1)} %copy-done.26, bf16[128,1152]{1,0:T(8,128)(2,1)} %copy-done.27, bf16[128,1152]{1,0:T(8,128)(2,1)} %copy-done.28, ...), custom_call_target="tpu_custom_call" | custom-call | tf_op jit(solution)/shard_map/local_product/pallas_call | solution.py:133
  92.7 3.0 %collective-permute-start.8 = (bf16[16,288,128]{2,1,0:T(8,128)(2,1)S(1)}, bf16[16,288,128]{2,1,0:T(8,128)(2,1)S(1)}, u32[]{:S(2)}, u32[]{:S(2)}) collective-permute-start(bf16[16,288,128]{2,1,0:T(8,128)(2,1)S(1)} %all-to-all-done.1), channel_id=1, source_target_pairs={{0,16},{16,0},{1,17},{17,1},{2,18},{18,2},{3,19},{19,3},{4,20},{20... | collective-permute-start | bytes 3538952 | tf_op jit(solution)/shard_map/ppermute | solution.py:425
  95.6 2.5 %collective-permute-done.8 = bf16[16,288,128]{2,1,0:T(8,128)(2,1)S(1)} collective-permute-done((bf16[16,288,128]{2,1,0:T(8,128)(2,1)S(1)}, bf16[16,288,128]{2,1,0:T(8,128)(2,1)S(1)}, u32[]{:S(2)}, u32[]{:S(2)}) %collective-permute-start.8) | collective-permute-done | bytes 1179680 | tf_op jit(solution)/shard_map/ppermute | solution.py:425
  99.1 7.6 %project.1 = bf16[4,512,256]{2,1,0:T(8,128)(2,1)} custom-call(s32[4]{0:T(128)} %copy-done.22, bf16[512,1152]{1,0:T(8,128)(2,1)} %get-tuple-element.48.hidden_any, f32[4,512,256]{2,1,0:T(8,128)} %get-tuple-element.49.local_any, bf16[4,1152,128]{2,1,0:T(8,128)(2,1)} %bitcast.38, bf16[4,1152,128]{2,1,0:T(8,128)(2,1)} %bitcast.40), custom_call_target="tpu_custom_call" | custom-call | tf_op jit(solution)/shard_map/project/pallas_call | solution.py:176
  106.8 12.3 %all-to-all-start.2 = ((bf16[4,512,256]{2,1,0:T(8,128)(2,1)}), bf16[4,512,256]{2,1,0:T(8,128)(2,1)}, u32[]{:S(2)}, u32[]{:S(2)}) async-start(bf16[4,512,256]{2,1,0:T(8,128)(2,1)} %project.1), calls=%async_computation.2 | async-start | bytes 2097152 | tf_op jit(solution)/shard_map/all_to_all | solution.py:399
  123.9 2.3 %collective-permute-start.9 = (bf16[512,256]{1,0:T(8,128)(2,1)S(1)}, bf16[512,256]{1,0:T(8,128)(2,1)S(1)}, u32[]{:S(2)}, u32[]{:S(2)}) collective-permute-start(bf16[512,256]{1,0:T(8,128)(2,1)S(1)} %get-tuple-element.61), channel_id=1, source_target_pairs={{0,1},{1,2},{2,3},{3,0},{4,5},{5,6},{6,7},{7,4},{8,9},{9,10},{10,1... | collective-permute-start | bytes 786440 | tf_op jit(solution)/shard_map/ppermute | solution.py:395
  126.1 3.4 %collective-permute-start.10 = (bf16[512,256]{1,0:T(8,128)(2,1)S(1)}, bf16[512,256]{1,0:T(8,128)(2,1)S(1)}, u32[]{:S(2)}, u32[]{:S(2)}) collective-permute-start(bf16[512,256]{1,0:T(8,128)(2,1)S(1)} %get-tuple-element.62), channel_id=1, source_target_pairs={{0,2},{1,3},{2,0},{3,1},{4,6},{5,7},{6,4},{7,5},{8,10},{9,11},{10,... | collective-permute-start | bytes 786440 | tf_op jit(solution)/shard_map/ppermute | solution.py:395
  129.5 2.8 %collective-permute-start.11 = (bf16[512,256]{1,0:T(8,128)(2,1)S(1)}, bf16[512,256]{1,0:T(8,128)(2,1)S(1)}, u32[]{:S(2)}, u32[]{:S(2)}) collective-permute-start(bf16[512,256]{1,0:T(8,128)(2,1)S(1)} %get-tuple-element.63), channel_id=1, source_target_pairs={{0,3},{1,0},{2,1},{3,2},{4,7},{5,4},{6,5},{7,6},{8,11},{9,8},{10,9... | collective-permute-start | bytes 786440 | tf_op jit(solution)/shard_map/ppermute | solution.py:395
  135.7 3.3 %collective-permute-done.10.refs_2_ = bf16[512,256]{1,0:T(8,128)(2,1)S(1)} collective-permute-done((bf16[512,256]{1,0:T(8,128)(2,1)S(1)}, bf16[512,256]{1,0:T(8,128)(2,1)S(1)}, u32[]{:S(2)}, u32[]{:S(2)}) %collective-permute-start.10) | collective-permute-done | bytes 262176 | tf_op jit(solution)/shard_map/ppermute | solution.py:395
  139.7 2.6 %collective-permute-done.11.refs_3_ = bf16[512,256]{1,0:T(8,128)(2,1)S(1)} collective-permute-done((bf16[512,256]{1,0:T(8,128)(2,1)S(1)}, bf16[512,256]{1,0:T(8,128)(2,1)S(1)}, u32[]{:S(2)}, u32[]{:S(2)}) %collective-permute-start.11) | collective-permute-done | bytes 262176 | tf_op jit(solution)/shard_map/ppermute | solution.py:395
  145.9 11.6 %all_to_all.25.keys_any = bf16[4,512,128]{2,1,0:T(8,128)(2,1)S(1)} all-to-all(bf16[4,512,128]{2,1,0:T(8,128)(2,1)S(1)} %reduce_keys.1), channel_id=1, replica_groups=mesh['x'=4,'zh'=4,'c'=2,'zl'=4,'y'=4] {'y'}, dimensions={0} | all-to-all | bytes 1048576 | tf_op jit(solution)/shard_map/all_to_all | solution.py:399
  157.5 5.1 %attend.1 = bf16[16,128,128]{2,1,0:T(8,128)(2,1)S(1)} custom-call(s32[4]{0:T(128)S(1)} %copy-done.23, bf16[4,512,128]{2,1,0:T(8,128)(2,1)S(1)} %all_to_all.25.keys_any, bf16[512,256]{1,0:T(8,128)(2,1)S(1)} %copy-done.9, bf16[512,256]{1,0:T(8,128)(2,1)S(1)} %copy-done.11, bf16[512,256]{1,0:T(8,128)(2,1)S(1)} %copy-done.13, bf16[512,256]{1,0:T(8,128)(2,1)S(1)} %copy-done.15), custom_call_target="tpu_custom_call" | custom-call | tf_op jit(solution)/shard_map/attend/pallas_call | solution.py:335
  162.6 17.7 %all_to_all.26.mixed_any = bf16[16,128,128]{2,1,0:T(8,128)(2,1)S(1)} all-to-all(bf16[16,128,128]{2,1,0:T(8,128)(2,1)S(1)} %attend.1), channel_id=1, replica_groups=mesh['x'=4,'zh'=4,'c'=2,'zl'=4,'y'=4] {'zl','y'}, dimensions={0} | all-to-all | bytes 1048576 | tf_op jit(solution)/shard_map/all_to_all | solution.py:399
  (92 shorter events, 27.4 us)
Async XLA Ops:
  7.2 78.0 %all-gather.2.cloned.1.call-start = ((), (), s32[]{:S(2)}) async-start(), calls=%async_computation.5 | async-start | bytes 2949120 | tf_op jit(solution)/shard_map/all_gather | solution.py:407
  10.5 23.8 %all-to-all-start = ((bf16[8,288,128]{2,1,0:T(8,128)(2,1)}), bf16[8,288,128]{2,1,0:T(8,128)(2,1)S(1)}, u32[]{:S(2)}, u32[]{:S(2)}) async-start(bf16[8,288,128]{2,1,0:T(8,128)(2,1)} %get-tuple-element.36.delta_ref), calls=%async_computation | async-start | bytes 1179648 | tf_op jit(solution)/shard_map/all_to_all | solution.py:399
  21.9 12.3 %collective-permute-start = (bf16[128,1152]{1,0:T(8,128)(2,1)}, bf16[128,1152]{1,0:T(8,128)(2,1)S(1)}, u32[]{:S(2)}, u32[]{:S(2)}) collective-permute-start(bf16[128,1152]{1,0:T(8,128)(2,1)} %get-tuple-element.72), channel_id=1, source_target_pairs={{0,4},{4,8},{8,12},{12,0},{1,5},{5,9},{9,13},{13,1},{2,6},{6,10},{... | collective-permute-start | bytes 884744 | tf_op jit(solution)/shard_map/ppermute | solution.py:388
  24.6 39.4 %copy-start.2 = (bf16[288,1024]{1,0:T(8,128)(2,1)S(1)}, bf16[288,1024]{1,0:T(8,128)(2,1)}, u32[]{:S(2)}) copy-start(bf16[288,1024]{1,0:T(8,128)(2,1)} %base_ref.3) | copy-start | bytes 1769476
  24.6 39.4 %copy-start.7 = (bf16[288,1024]{1,0:T(8,128)(2,1)S(1)}, bf16[288,1024]{1,0:T(8,128)(2,1)}, u32[]{:S(2)}) copy-start(bf16[288,1024]{1,0:T(8,128)(2,1)} %momentum_ref.1) | copy-start | bytes 1769476
  25.3 36.0 %collective-permute-start.5 = (bf16[128,768]{1,0:T(8,128)(2,1)}, bf16[128,768]{1,0:T(8,128)(2,1)S(1)}, u32[]{:S(2)}, u32[]{:S(2)}) collective-permute-start(bf16[128,768]{1,0:T(8,128)(2,1)} %pad_maximum_fusion), channel_id=1, source_target_pairs={{0,4},{4,8},{8,12},{12,0},{1,5},{5,9},{9,13},{13,1},{2,6},{6,10},{... | collective-permute-start | bytes 589832 | tf_op jit(solution)/shard_map/ppermute | solution.py:388
  27.3 27.7 %collective-permute-start.2 = (bf16[128,1152]{1,0:T(8,128)(2,1)}, bf16[128,1152]{1,0:T(8,128)(2,1)S(1)}, u32[]{:S(2)}, u32[]{:S(2)}) collective-permute-start(bf16[128,1152]{1,0:T(8,128)(2,1)} %get-tuple-element.71), channel_id=1, source_target_pairs={{0,8},{4,12},{8,0},{12,4},{1,9},{5,13},{9,1},{13,5},{2,10},{6,14},... | collective-permute-start | bytes 884744 | tf_op jit(solution)/shard_map/ppermute | solution.py:388
  34.3 31.5 %copy-start.26 = (bf16[128,1152]{1,0:T(8,128)(2,1)}, bf16[128,1152]{1,0:T(8,128)(2,1)S(1)}, u32[]{:S(2)}) copy-start(bf16[128,1152]{1,0:T(8,128)(2,1)S(1)} %collective-permute-done.refs_1_) | copy-start | bytes 884740
  34.4 12.4 %collective-permute-start.1 = (bf16[288,128]{1,0:T(8,128)(2,1)S(1)}, bf16[288,128]{1,0:T(8,128)(2,1)S(1)}, u32[]{:S(2)}, u32[]{:S(2)}) collective-permute-start(bf16[288,128]{1,0:T(8,128)(2,1)S(1)} %reduce_sum.12), channel_id=1, source_target_pairs={{0,32},{64,96},{32,0},{96,64},{1,33},{65,97},{33,1},{97,65},{2,34}... | collective-permute-start | bytes 221192 | tf_op jit(solution)/shard_map/ppermute | solution.py:370
  41.7 19.7 %collective-permute-start.6 = (bf16[128,768]{1,0:T(8,128)(2,1)}, bf16[128,768]{1,0:T(8,128)(2,1)S(1)}, u32[]{:S(2)}, u32[]{:S(2)}) collective-permute-start(bf16[128,768]{1,0:T(8,128)(2,1)} %pad_maximum_fusion.1), channel_id=1, source_target_pairs={{0,12},{4,0},{8,4},{12,8},{1,13},{5,1},{9,5},{13,9},{2,14},{6,2},{... | collective-permute-start | bytes 589832 | tf_op jit(solution)/shard_map/ppermute | solution.py:388
  44.8 16.8 %collective-permute-start.4 = (bf16[128,1152]{1,0:T(8,128)(2,1)S(1)}, bf16[128,1152]{1,0:T(8,128)(2,1)S(1)}, u32[]{:S(2)}, u32[]{:S(2)}) collective-permute-start(bf16[128,1152]{1,0:T(8,128)(2,1)S(1)} %get-tuple-element.73), channel_id=1, source_target_pairs={{0,12},{4,0},{8,4},{12,8},{1,13},{5,1},{9,5},{13,9},{2,14},{6,2},{... | collective-permute-start | bytes 884744 | tf_op jit(solution)/shard_map/ppermute | solution.py:388
  54.9 9.1 %collective-permute-start.3 = (bf16[288,128]{1,0:T(8,128)(2,1)S(1)}, bf16[288,128]{1,0:T(8,128)(2,1)S(1)}, u32[]{:S(2)}, u32[]{:S(2)}) collective-permute-start(bf16[288,128]{1,0:T(8,128)(2,1)S(1)} %add_convert_fusion.mine_ref), channel_id=1, source_target_pairs={{32,64},{96,0},{64,32},{0,96},{33,65},{97,1},{65,33},{1,97},{34,66... | collective-permute-start | bytes 221192 | tf_op jit(solution)/shard_map/ppermute | solution.py:370
  65.9 26.8 %all-to-all-start.1 = ((bf16[16,288,128]{2,1,0:T(8,128)(2,1)}), bf16[16,288,128]{2,1,0:T(8,128)(2,1)S(1)}, u32[]{:S(2)}, u32[]{:S(2)}) async-start(bf16[16,288,128]{2,1,0:T(8,128)(2,1)} %outer_step.1), calls=%async_computation.1 | async-start | bytes 2359296 | tf_op jit(solution)/shard_map/all_to_all | solution.py:399
  72.6 19.4 %collective-permute-start.7 = (bf16[128,768]{1,0:T(8,128)(2,1)S(1)}, bf16[128,768]{1,0:T(8,128)(2,1)S(1)}, u32[]{:S(2)}, u32[]{:S(2)}) collective-permute-start(bf16[128,768]{1,0:T(8,128)(2,1)S(1)} %pad_maximum_fusion.3), channel_id=1, source_target_pairs={{0,8},{4,12},{8,0},{12,4},{1,9},{5,13},{9,1},{13,5},{2,10},{6,14},... | collective-permute-start | bytes 589832 | tf_op jit(solution)/shard_map/ppermute | solution.py:388
  92.7 5.4 %collective-permute-start.8 = (bf16[16,288,128]{2,1,0:T(8,128)(2,1)S(1)}, bf16[16,288,128]{2,1,0:T(8,128)(2,1)S(1)}, u32[]{:S(2)}, u32[]{:S(2)}) collective-permute-start(bf16[16,288,128]{2,1,0:T(8,128)(2,1)S(1)} %all-to-all-done.1), channel_id=1, source_target_pairs={{0,16},{16,0},{1,17},{17,1},{2,18},{18,2},{3,19},{19,3},{4,20},{20... | collective-permute-start | bytes 3538952 | tf_op jit(solution)/shard_map/ppermute | solution.py:425
  99.1 19.9 %copy-start.23 = (s32[4]{0:T(128)S(1)}, s32[4]{0:T(128)}, u32[]{:S(2)}) copy-start(s32[4]{0:T(128)} %copy-done.22) | copy-start | bytes 52
  99.1 33.3 %copy-start.5 = (bf16[8,288,128]{2,1,0:T(8,128)(2,1)S(1)}, bf16[8,288,128]{2,1,0:T(8,128)(2,1)}, u32[]{:S(2)}) copy-start(bf16[8,288,128]{2,1,0:T(8,128)(2,1)} %get-tuple-element.36.delta_ref) | copy-start | bytes 1769476
  106.7 25.7 %copy-start.1 = (bf16[16,288,128]{2,1,0:T(8,128)(2,1)S(1)}, bf16[16,288,128]{2,1,0:T(8,128)(2,1)}, u32[]{:S(2)}) copy-start(bf16[16,288,128]{2,1,0:T(8,128)(2,1)} %copy-done) | copy-start | bytes 3538948
  106.7 25.7 %copy-start.4 = (bf16[16,288,128]{2,1,0:T(8,128)(2,1)S(1)}, bf16[16,288,128]{2,1,0:T(8,128)(2,1)}, u32[]{:S(2)}) copy-start(bf16[16,288,128]{2,1,0:T(8,128)(2,1)} %copy-done.3) | copy-start | bytes 3538948
  106.8 37.6 %all-to-all-start.2 = ((bf16[4,512,256]{2,1,0:T(8,128)(2,1)}), bf16[4,512,256]{2,1,0:T(8,128)(2,1)}, u32[]{:S(2)}, u32[]{:S(2)}) async-start(bf16[4,512,256]{2,1,0:T(8,128)(2,1)} %project.1), calls=%async_computation.2 | async-start | bytes 2097152 | tf_op jit(solution)/shard_map/all_to_all | solution.py:399
  123.9 11.1 %collective-permute-start.9 = (bf16[512,256]{1,0:T(8,128)(2,1)S(1)}, bf16[512,256]{1,0:T(8,128)(2,1)S(1)}, u32[]{:S(2)}, u32[]{:S(2)}) collective-permute-start(bf16[512,256]{1,0:T(8,128)(2,1)S(1)} %get-tuple-element.61), channel_id=1, source_target_pairs={{0,1},{1,2},{2,3},{3,0},{4,5},{5,6},{6,7},{7,4},{8,9},{9,10},{10,1... | collective-permute-start | bytes 786440 | tf_op jit(solution)/shard_map/ppermute | solution.py:395
  126.1 12.9 %collective-permute-start.10 = (bf16[512,256]{1,0:T(8,128)(2,1)S(1)}, bf16[512,256]{1,0:T(8,128)(2,1)S(1)}, u32[]{:S(2)}, u32[]{:S(2)}) collective-permute-start(bf16[512,256]{1,0:T(8,128)(2,1)S(1)} %get-tuple-element.62), channel_id=1, source_target_pairs={{0,2},{1,3},{2,0},{3,1},{4,6},{5,7},{6,4},{7,5},{8,10},{9,11},{10,... | collective-permute-start | bytes 786440 | tf_op jit(solution)/shard_map/ppermute | solution.py:395
  129.5 12.8 %collective-permute-start.11 = (bf16[512,256]{1,0:T(8,128)(2,1)S(1)}, bf16[512,256]{1,0:T(8,128)(2,1)S(1)}, u32[]{:S(2)}, u32[]{:S(2)}) collective-permute-start(bf16[512,256]{1,0:T(8,128)(2,1)S(1)} %get-tuple-element.63), channel_id=1, source_target_pairs={{0,3},{1,0},{2,1},{3,2},{4,7},{5,4},{6,5},{7,6},{8,11},{9,8},{10,9... | collective-permute-start | bytes 786440 | tf_op jit(solution)/shard_map/ppermute | solution.py:395
  144.4 13.1 %copy-start.15 = (bf16[512,256]{1,0:T(8,128)(2,1)S(1)}, bf16[512,256]{1,0:T(8,128)(2,1)}, u32[]{:S(2)}) copy-start(bf16[512,256]{1,0:T(8,128)(2,1)} %copy-done.14) | copy-start | bytes 786436
  (23 other events, 114.8 us)
Sparse Core Ops, SparseCore 0:
  10.7 46.0 all-gather.1

commit v7 on v6

--- a/solution.py
+++ b/solution.py
@@ -115,16 +115,16 @@
     for s in range(NZL):
         to = pl.ds(pl.multiple_of(lax.rem(z - s + NZL, NZL) * 128, 128), 128)
         copies.append(pltpu.make_async_copy(pieces[s], hidden_ref.at[to], sems.at[s]))
-    for n in range(NZL):
-        cols = pl.ds(n * 256, 256)
-        copies.append(pltpu.make_async_copy(part_any.at[:, cols], part.at[n], sems.at[NZL + n]))
-    start_all(copies)
-    for copy in copies[:NZL]:
+    step = part.shape[0] // NY
+    for y in range(NY):
+        rows = pl.ds(y * step, step)
+        copies.append(pltpu.make_async_copy(part_any.at[rows], part.at[rows], sems.at[NZL + y]))
+    for copy in start_all(copies):
         copy.wait()
     for n in range(NZL):
-        copies[NZL + n].wait()
+        cols = slice(n * 256, (n + 1) * 256)
         out_ref[n] = blend_share * jnp.dot(
-            hidden_ref[...], part[n], preferred_element_type=jnp.float32
+            hidden_ref[...], part[:, cols], preferred_element_type=jnp.float32
         )
 
 
@@ -139,35 +139,22 @@
         in_specs=[SMEM] + [ANY] * 5,
         out_specs=(VMEM, VMEM),
         scratch_shapes=[
-            pltpu.VMEM((NZL, depth, 256), jnp.bfloat16),
+            pltpu.VMEM(part.shape, jnp.bfloat16),
             pltpu.SemaphoreType.DMA((2 * NZL,)),
         ],
-        compiler_params=params(),
+        compiler_params=params(48),
         name="local_product",
     )(place, *hidden, part)
 
 
-def project_kernel(place_ref, hidden_any, local_any, same_any, other_any, out_ref, *refs):
-    hidden, local, weight, sems, local_sems, hidden_sem = refs
+def project_kernel(place_ref, hidden_ref, local_ref, same_ref, other_ref, out_ref, weight):
     c = place_ref[0]
-    hidden_copy = pltpu.make_async_copy(hidden_any, hidden, hidden_sem)
-    copies = []
     for n in range(NZL):
-        for near, source in enumerate((same_any, other_any)):
+        for near, ref in enumerate((same_ref, other_ref)):
             at = pl.multiple_of(lax.rem(c + near, NC) * BLOCK, BLOCK)
-            copies.append(
-                pltpu.make_async_copy(
-                    source.at[n], weight.at[n, :, pl.ds(at, BLOCK)], sems.at[n, near]
-                )
-            )
-        copies.append(pltpu.make_async_copy(local_any.at[n], local.at[n], local_sems.at[n]))
-    start_all(copies[:2] + [hidden_copy] + copies[2:])
-    hidden_copy.wait()
-    for n in range(NZL):
-        for copy in copies[3 * n : 3 * n + 3]:
-            copy.wait()
-        outer = jnp.dot(hidden[...], weight[n], preferred_element_type=jnp.float32)
-        out_ref[n] = (local[n] + (1.0 - blend_share) * outer).astype(jnp.bfloat16)
+            weight[n, :, pl.ds(at, BLOCK)] = ref[n]
+        outer = jnp.dot(hidden_ref[...], weight[n], preferred_element_type=jnp.float32)
+        out_ref[n] = (local_ref[n] + (1.0 - blend_share) * outer).astype(jnp.bfloat16)
 
 
 def project(place, hidden, local, same, other):
@@ -176,17 +163,10 @@
     return pl.pallas_call(
         project_kernel,
         out_shape=jax.ShapeDtypeStruct((NZL, 512, 2 * BLOCK), jnp.bfloat16),
-        in_specs=[SMEM] + [ANY] * 4,
+        in_specs=[SMEM] + [VMEM] * 4,
         out_specs=VMEM,
-        scratch_shapes=[
-            pltpu.VMEM((512, depth), jnp.bfloat16),
-            pltpu.VMEM((NZL, 512, 256), jnp.float32),
-            pltpu.VMEM((NZL, depth, 2 * BLOCK), jnp.bfloat16),
-            pltpu.SemaphoreType.DMA((NZL, 2)),
-            pltpu.SemaphoreType.DMA((NZL,)),
-            pltpu.SemaphoreType.DMA,
-        ],
-        compiler_params=params(),
+        scratch_shapes=[pltpu.VMEM((NZL, depth, 2 * BLOCK), jnp.bfloat16)],
+        compiler_params=params(20),
         name="project",
     )(place, hidden, local, same.reshape(blocks), other.reshape(blocks))
 

time: 191 us -> 189 us (0.990)
  Pallas kernels: 30 us -> 21.9 us
  local copies, waits for them, and re-layouts: 9.3 us -> 15.1 us
    pallas_call x1, Pallas kernels: 7.62 us -> 2.44 us  [project(): pl.pallas_call(project_kernel, out_shape=jax.ShapeDtypeStruct((NZL, 512,...]
    unnamed x62 -> x56, local copies, waits for them, and re-layouts: 7.64 us -> 12.8 us
    pallas_call x1, Pallas kernels: 6.81 us -> 3.99 us  [local_product(): pl.pallas_call(local_kernel, out_shape=(jax.ShapeDtypeStruct((512, depth)...]
  transfers between devices with their start and end apart: 16 -> 16, of which waited for: 9 -> 7; matrix products, arithmetic and copies ran while one was open for 3% -> 3% of each run, Pallas kernels for 6% -> 5%
where the time goes in v7:
time: 189 us; the launch traced here: 186 us
  starting transfers between devices  80.2 us (42%)
  blocking collectives  29.2 us (15%)
  Pallas kernels  21.9 us (12%)
  waiting for transfers between devices  21.4 us (11%)
  local copies, waits for them, and re-layouts  15.1 us (8%)
  between operations  14.4 us (8%)
  other arithmetic  4 us (2%)
    all_to_all x3, starting transfers between devices, exchange(): return lax.all_to_all(array, axis, 0, 0, tiled=True)  29.8 us
    all_to_all x2, blocking collectives, exchange(): return lax.all_to_all(array, axis, 0, 0, tiled=True)  29.2 us
    ppermute x6, starting transfers between devices, deal(): piece = lax.ppermute(piece, axis, [(i, (i + step) % 4) for i in range(4)])  26.8 us
    unnamed x56, local copies, waits for them, and re-layouts  12.8 us
    ppermute x2, starting transfers between devices, swap(): return lax.ppermute(array, axis, pairs + [(b, a) for a, b in pairs])  12.1 us
    ppermute x3, starting transfers between devices, turn(): lax.ppermute(a, axis, shift)  8.41 us
    ppermute x6, waiting for transfers between devices, deal(): piece = lax.ppermute(piece, axis, [(i, (i + step) % 4) for i in range(4)])  8.16 us
    ppermute x3, waiting for transfers between devices, turn(): lax.ppermute(a, axis, shift)  6.68 us
  transfers between devices with their start and end apart: 16, of which 7 were waited for; matrix products, arithmetic and copies ran while one was open for 3% of the time, Pallas kernels for 5%

profile of v7, /device:TPU:1, one launch (start us, length us, event | category | flops | bytes accessed | tf_op | source)
XLA Modules:
  0.0 186.2 jit_solution(1852568863196177579)
XLA Ops:
  7.2 3.3 %prep.1 = (bf16[8,288,128]{2,1,0:T(8,128)(2,1)}, bf16[288,1024]{1,0:T(8,128)(2,1)}) custom-call(bf16[288,1024]{1,0:T(8,128)(2,1)} %bitcast.43, s32[8,288]{1,0:T(8,128)} %bitcast.45, bf16[288,1024]{1,0:T(8,128)(2,1)} %base_ref.3), custom_call_target="tpu_custom_call" | custom-call | tf_op jit(solution)/shard_map/prep/pallas_call | solution.py:64
  10.5 10.5 %all-to-all-start = ((bf16[8,288,128]{2,1,0:T(8,128)(2,1)}), bf16[8,288,128]{2,1,0:T(8,128)(2,1)S(1)}, u32[]{:S(2)}, u32[]{:S(2)}) async-start(bf16[8,288,128]{2,1,0:T(8,128)(2,1)} %get-tuple-element.36.delta_ref), calls=%async_computation | async-start | bytes 1179648 | tf_op jit(solution)/shard_map/all_to_all | solution.py:379
  21.9 1.9 %collective-permute-start = (bf16[128,1152]{1,0:T(8,128)(2,1)}, bf16[128,1152]{1,0:T(8,128)(2,1)S(1)}, u32[]{:S(2)}, u32[]{:S(2)}) collective-permute-start(bf16[128,1152]{1,0:T(8,128)(2,1)} %get-tuple-element.72), channel_id=1, source_target_pairs={{0,4},{4,8},{8,12},{12,0},{1,5},{5,9},{9,13},{13,1},{2,6},{6,10},{... | collective-permute-start | bytes 884744 | tf_op jit(solution)/shard_map/ppermute | solution.py:368
  28.8 5.4 %collective-permute-start.2 = (bf16[128,1152]{1,0:T(8,128)(2,1)}, bf16[128,1152]{1,0:T(8,128)(2,1)S(1)}, u32[]{:S(2)}, u32[]{:S(2)}) collective-permute-start(bf16[128,1152]{1,0:T(8,128)(2,1)} %get-tuple-element.71), channel_id=1, source_target_pairs={{0,8},{4,12},{8,0},{12,4},{1,9},{5,13},{9,1},{13,5},{2,10},{6,14},... | collective-permute-start | bytes 884744 | tf_op jit(solution)/shard_map/ppermute | solution.py:368
  34.4 5.8 %collective-permute-start.1 = (bf16[288,128]{1,0:T(8,128)(2,1)S(1)}, bf16[288,128]{1,0:T(8,128)(2,1)S(1)}, u32[]{:S(2)}, u32[]{:S(2)}) collective-permute-start(bf16[288,128]{1,0:T(8,128)(2,1)S(1)} %reduce_sum.12), channel_id=1, source_target_pairs={{0,32},{64,96},{32,0},{96,64},{1,33},{65,97},{33,1},{97,65},{2,34}... | collective-permute-start | bytes 221192 | tf_op jit(solution)/shard_map/ppermute | solution.py:350
  41.1 3.8 %collective-permute-start.6 = (bf16[128,768]{1,0:T(8,128)(2,1)S(1)}, bf16[128,768]{1,0:T(8,128)(2,1)S(1)}, u32[]{:S(2)}, u32[]{:S(2)}) collective-permute-start(bf16[128,768]{1,0:T(8,128)(2,1)S(1)} %pad_maximum_fusion.1), channel_id=1, source_target_pairs={{0,12},{4,0},{8,4},{12,8},{1,13},{5,1},{9,5},{13,9},{2,14},{6,2},{... | collective-permute-start | bytes 589832 | tf_op jit(solution)/shard_map/ppermute | solution.py:368
  44.9 1.9 %collective-permute-start.4 = (bf16[128,1152]{1,0:T(8,128)(2,1)}, bf16[128,1152]{1,0:T(8,128)(2,1)S(1)}, u32[]{:S(2)}, u32[]{:S(2)}) collective-permute-start(bf16[128,1152]{1,0:T(8,128)(2,1)} %get-tuple-element.73), channel_id=1, source_target_pairs={{0,12},{4,0},{8,4},{12,8},{1,13},{5,1},{9,5},{13,9},{2,14},{6,2},{... | collective-permute-start | bytes 884744 | tf_op jit(solution)/shard_map/ppermute | solution.py:368
  46.9 8.1 %collective-permute-done.2.refs_2_ = bf16[128,1152]{1,0:T(8,128)(2,1)S(1)} collective-permute-done((bf16[128,1152]{1,0:T(8,128)(2,1)}, bf16[128,1152]{1,0:T(8,128)(2,1)S(1)}, u32[]{:S(2)}, u32[]{:S(2)}) %collective-permute-start.2) | collective-permute-done | bytes 294944 | tf_op jit(solution)/shard_map/ppermute | solution.py:368
  54.9 6.3 %collective-permute-start.3 = (bf16[288,128]{1,0:T(8,128)(2,1)S(1)}, bf16[288,128]{1,0:T(8,128)(2,1)S(1)}, u32[]{:S(2)}, u32[]{:S(2)}) collective-permute-start(bf16[288,128]{1,0:T(8,128)(2,1)S(1)} %add_convert_fusion.mine_ref), channel_id=1, source_target_pairs={{32,64},{96,0},{64,32},{0,96},{33,65},{97,1},{65,33},{1,97},{34,66... | collective-permute-start | bytes 221192 | tf_op jit(solution)/shard_map/ppermute | solution.py:350
  61.4 2.6 %collective-permute-done.3.sent_ref = bf16[288,128]{1,0:T(8,128)(2,1)S(1)} collective-permute-done((bf16[288,128]{1,0:T(8,128)(2,1)S(1)}, bf16[288,128]{1,0:T(8,128)(2,1)S(1)}, u32[]{:S(2)}, u32[]{:S(2)}) %collective-permute-start.3) | collective-permute-done | bytes 73760 | tf_op jit(solution)/shard_map/ppermute | solution.py:350
  65.8 6.7 %all-to-all-start.1 = ((bf16[16,288,128]{2,1,0:T(8,128)(2,1)}), bf16[16,288,128]{2,1,0:T(8,128)(2,1)S(1)}, u32[]{:S(2)}, u32[]{:S(2)}) async-start(bf16[16,288,128]{2,1,0:T(8,128)(2,1)} %outer_step.1), calls=%async_computation.1 | async-start | bytes 2359296 | tf_op jit(solution)/shard_map/all_to_all | solution.py:379
  73.2 11.9 %collective-permute-start.7 = (bf16[128,768]{1,0:T(8,128)(2,1)}, bf16[128,768]{1,0:T(8,128)(2,1)S(1)}, u32[]{:S(2)}, u32[]{:S(2)}) collective-permute-start(bf16[128,768]{1,0:T(8,128)(2,1)} %pad_maximum_fusion.3), channel_id=1, source_target_pairs={{0,8},{4,12},{8,0},{12,4},{1,9},{5,13},{9,1},{13,5},{2,10},{6,14},... | collective-permute-start | bytes 589832 | tf_op jit(solution)/shard_map/ppermute | solution.py:368
  85.7 4.0 %local_product.1 = (bf16[512,1152]{1,0:T(8,128)(2,1)S(1)}, f32[4,512,256]{2,1,0:T(8,128)S(1)}) custom-call(s32[4]{0:T(128)S(1)} %pad_add_fusion.place_ref, bf16[128,1152]{1,0:T(8,128)(2,1)S(1)} %get-tuple-element.70.refs_0_, bf16[128,1152]{1,0:T(8,128)(2,1)S(1)} %collective-permute-done.refs_1_, bf16[128,1152]{1,0:T(8,128)(2,1)S(1)} %collective-permute-done.2.refs_2_, ...), custom_call_target="tpu_custom_call" | custom-call | tf_op jit(solution)/shard_map/local_product/pallas_call | solution.py:133
  92.8 3.0 %collective-permute-start.8 = (bf16[16,288,128]{2,1,0:T(8,128)(2,1)S(1)}, bf16[16,288,128]{2,1,0:T(8,128)(2,1)S(1)}, u32[]{:S(2)}, u32[]{:S(2)}) collective-permute-start(bf16[16,288,128]{2,1,0:T(8,128)(2,1)S(1)} %all-to-all-done.1), channel_id=1, source_target_pairs={{0,16},{16,0},{1,17},{17,1},{2,18},{18,2},{3,19},{19,3},{4,20},{20... | collective-permute-start | bytes 3538952 | tf_op jit(solution)/shard_map/ppermute | solution.py:405
  95.8 2.5 %collective-permute-done.8 = bf16[16,288,128]{2,1,0:T(8,128)(2,1)S(1)} collective-permute-done((bf16[16,288,128]{2,1,0:T(8,128)(2,1)S(1)}, bf16[16,288,128]{2,1,0:T(8,128)(2,1)S(1)}, u32[]{:S(2)}, u32[]{:S(2)}) %collective-permute-start.8) | collective-permute-done | bytes 1179680 | tf_op jit(solution)/shard_map/ppermute | solution.py:405
  101.1 2.4 %project.1 = bf16[4,512,256]{2,1,0:T(8,128)(2,1)S(1)} custom-call(s32[4]{0:T(128)S(1)} %pad_add_fusion.place_ref, bf16[512,1152]{1,0:T(8,128)(2,1)S(1)} %copy-done.6, f32[4,512,256]{2,1,0:T(8,128)S(1)} %copy-done.4, bf16[4,1152,128]{2,1,0:T(8,128)(2,1)S(1)} %bitcast.38, bf16[4,1152,128]{2,1,0:T(8,128)(2,1)S(1)} %bitcast.40), custom_call_target="tpu_custom_call" | custom-call | tf_op jit(solution)/shard_map/project/pallas_call | solution.py:163
  104.5 12.7 %all-to-all-start.2 = ((bf16[4,512,256]{2,1,0:T(8,128)(2,1)}), bf16[4,512,256]{2,1,0:T(8,128)(2,1)}, u32[]{:S(2)}, u32[]{:S(2)}) async-start(bf16[4,512,256]{2,1,0:T(8,128)(2,1)} %copy-done.1), calls=%async_computation.2 | async-start | bytes 2097152 | tf_op jit(solution)/shard_map/all_to_all | solution.py:379
  122.1 2.2 %collective-permute-start.9 = (bf16[512,256]{1,0:T(8,128)(2,1)S(1)}, bf16[512,256]{1,0:T(8,128)(2,1)S(1)}, u32[]{:S(2)}, u32[]{:S(2)}) collective-permute-start(bf16[512,256]{1,0:T(8,128)(2,1)S(1)} %get-tuple-element.61), channel_id=1, source_target_pairs={{0,1},{1,2},{2,3},{3,0},{4,5},{5,6},{6,7},{7,4},{8,9},{9,10},{10,1... | collective-permute-start | bytes 786440 | tf_op jit(solution)/shard_map/ppermute | solution.py:375
  124.3 2.9 %collective-permute-start.10 = (bf16[512,256]{1,0:T(8,128)(2,1)S(1)}, bf16[512,256]{1,0:T(8,128)(2,1)S(1)}, u32[]{:S(2)}, u32[]{:S(2)}) collective-permute-start(bf16[512,256]{1,0:T(8,128)(2,1)S(1)} %get-tuple-element.62), channel_id=1, source_target_pairs={{0,2},{1,3},{2,0},{3,1},{4,6},{5,7},{6,4},{7,5},{8,10},{9,11},{10,... | collective-permute-start | bytes 786440 | tf_op jit(solution)/shard_map/ppermute | solution.py:375
  127.2 3.3 %collective-permute-start.11 = (bf16[512,256]{1,0:T(8,128)(2,1)S(1)}, bf16[512,256]{1,0:T(8,128)(2,1)S(1)}, u32[]{:S(2)}, u32[]{:S(2)}) collective-permute-start(bf16[512,256]{1,0:T(8,128)(2,1)S(1)} %get-tuple-element.63), channel_id=1, source_target_pairs={{0,3},{1,0},{2,1},{3,2},{4,7},{5,4},{6,5},{7,6},{8,11},{9,8},{10,9... | collective-permute-start | bytes 786440 | tf_op jit(solution)/shard_map/ppermute | solution.py:375
  132.4 5.6 %collective-permute-done.9.refs_1_ = bf16[512,256]{1,0:T(8,128)(2,1)S(1)} collective-permute-done((bf16[512,256]{1,0:T(8,128)(2,1)S(1)}, bf16[512,256]{1,0:T(8,128)(2,1)S(1)}, u32[]{:S(2)}, u32[]{:S(2)}) %collective-permute-start.9) | collective-permute-done | bytes 262176 | tf_op jit(solution)/shard_map/ppermute | solution.py:375
  144.1 11.6 %all_to_all.25.keys_any = bf16[4,512,128]{2,1,0:T(8,128)(2,1)S(1)} all-to-all(bf16[4,512,128]{2,1,0:T(8,128)(2,1)S(1)} %reduce_keys.1), channel_id=1, replica_groups=mesh['x'=4,'zh'=4,'c'=2,'zl'=4,'y'=4] {'y'}, dimensions={0} | all-to-all | bytes 1048576 | tf_op jit(solution)/shard_map/all_to_all | solution.py:379
  155.7 5.1 %attend.1 = bf16[16,128,128]{2,1,0:T(8,128)(2,1)S(1)} custom-call(s32[4]{0:T(128)S(1)} %pad_add_fusion.place_ref, bf16[4,512,128]{2,1,0:T(8,128)(2,1)S(1)} %all_to_all.25.keys_any, bf16[512,256]{1,0:T(8,128)(2,1)S(1)} %copy-done.10, bf16[512,256]{1,0:T(8,128)(2,1)S(1)} %copy-done.12, bf16[512,256]{1,0:T(8,128)(2,1)S(1)} %copy-done.14, ...), custom_call_target="tpu_custom_call" | custom-call | tf_op jit(solution)/shard_map/attend/pallas_call | solution.py:315
  160.8 17.7 %all_to_all.26.mixed_any = bf16[16,128,128]{2,1,0:T(8,128)(2,1)S(1)} all-to-all(bf16[16,128,128]{2,1,0:T(8,128)(2,1)S(1)} %attend.1), channel_id=1, replica_groups=mesh['x'=4,'zh'=4,'c'=2,'zl'=4,'y'=4] {'zl','y'}, dimensions={0} | all-to-all | bytes 1048576 | tf_op jit(solution)/shard_map/all_to_all | solution.py:379
  (86 shorter events, 30.8 us)
Async XLA Ops:
  7.2 78.6 %all-gather.2.cloned.1.call-start = ((), (), s32[]{:S(2)}) async-start(), calls=%async_computation.5 | async-start | bytes 2949120 | tf_op jit(solution)/shard_map/all_gather | solution.py:387
  10.5 23.8 %all-to-all-start = ((bf16[8,288,128]{2,1,0:T(8,128)(2,1)}), bf16[8,288,128]{2,1,0:T(8,128)(2,1)S(1)}, u32[]{:S(2)}, u32[]{:S(2)}) async-start(bf16[8,288,128]{2,1,0:T(8,128)(2,1)} %get-tuple-element.36.delta_ref), calls=%async_computation | async-start | bytes 1179648 | tf_op jit(solution)/shard_map/all_to_all | solution.py:379
  21.9 12.3 %collective-permute-start = (bf16[128,1152]{1,0:T(8,128)(2,1)}, bf16[128,1152]{1,0:T(8,128)(2,1)S(1)}, u32[]{:S(2)}, u32[]{:S(2)}) collective-permute-start(bf16[128,1152]{1,0:T(8,128)(2,1)} %get-tuple-element.72), channel_id=1, source_target_pairs={{0,4},{4,8},{8,12},{12,0},{1,5},{5,9},{9,13},{13,1},{2,6},{6,10},{... | collective-permute-start | bytes 884744 | tf_op jit(solution)/shard_map/ppermute | solution.py:368
  24.6 39.4 %copy-start = (bf16[288,1024]{1,0:T(8,128)(2,1)S(1)}, bf16[288,1024]{1,0:T(8,128)(2,1)}, u32[]{:S(2)}) copy-start(bf16[288,1024]{1,0:T(8,128)(2,1)} %base_ref.3) | copy-start | bytes 1769476
  24.6 39.4 %copy-start.8 = (bf16[288,1024]{1,0:T(8,128)(2,1)S(1)}, bf16[288,1024]{1,0:T(8,128)(2,1)}, u32[]{:S(2)}) copy-start(bf16[288,1024]{1,0:T(8,128)(2,1)} %momentum_ref.1) | copy-start | bytes 1769476
  26.8 34.5 %collective-permute-start.5 = (bf16[128,768]{1,0:T(8,128)(2,1)}, bf16[128,768]{1,0:T(8,128)(2,1)S(1)}, u32[]{:S(2)}, u32[]{:S(2)}) collective-permute-start(bf16[128,768]{1,0:T(8,128)(2,1)} %pad_maximum_fusion), channel_id=1, source_target_pairs={{0,4},{4,8},{8,12},{12,0},{1,5},{5,9},{9,13},{13,1},{2,6},{6,10},{... | collective-permute-start | bytes 589832 | tf_op jit(solution)/shard_map/ppermute | solution.py:368
  28.8 26.2 %collective-permute-start.2 = (bf16[128,1152]{1,0:T(8,128)(2,1)}, bf16[128,1152]{1,0:T(8,128)(2,1)S(1)}, u32[]{:S(2)}, u32[]{:S(2)}) collective-permute-start(bf16[128,1152]{1,0:T(8,128)(2,1)} %get-tuple-element.71), channel_id=1, source_target_pairs={{0,8},{4,12},{8,0},{12,4},{1,9},{5,13},{9,1},{13,5},{2,10},{6,14},... | collective-permute-start | bytes 884744 | tf_op jit(solution)/shard_map/ppermute | solution.py:368
  34.4 12.5 %collective-permute-start.1 = (bf16[288,128]{1,0:T(8,128)(2,1)S(1)}, bf16[288,128]{1,0:T(8,128)(2,1)S(1)}, u32[]{:S(2)}, u32[]{:S(2)}) collective-permute-start(bf16[288,128]{1,0:T(8,128)(2,1)S(1)} %reduce_sum.12), channel_id=1, source_target_pairs={{0,32},{64,96},{32,0},{96,64},{1,33},{65,97},{33,1},{97,65},{2,34}... | collective-permute-start | bytes 221192 | tf_op jit(solution)/shard_map/ppermute | solution.py:350
  41.1 20.3 %collective-permute-start.6 = (bf16[128,768]{1,0:T(8,128)(2,1)S(1)}, bf16[128,768]{1,0:T(8,128)(2,1)S(1)}, u32[]{:S(2)}, u32[]{:S(2)}) collective-permute-start(bf16[128,768]{1,0:T(8,128)(2,1)S(1)} %pad_maximum_fusion.1), channel_id=1, source_target_pairs={{0,12},{4,0},{8,4},{12,8},{1,13},{5,1},{9,5},{13,9},{2,14},{6,2},{... | collective-permute-start | bytes 589832 | tf_op jit(solution)/shard_map/ppermute | solution.py:368
  44.9 16.5 %collective-permute-start.4 = (bf16[128,1152]{1,0:T(8,128)(2,1)}, bf16[128,1152]{1,0:T(8,128)(2,1)S(1)}, u32[]{:S(2)}, u32[]{:S(2)}) collective-permute-start(bf16[128,1152]{1,0:T(8,128)(2,1)} %get-tuple-element.73), channel_id=1, source_target_pairs={{0,12},{4,0},{8,4},{12,8},{1,13},{5,1},{9,5},{13,9},{2,14},{6,2},{... | collective-permute-start | bytes 884744 | tf_op jit(solution)/shard_map/ppermute | solution.py:368
  54.9 9.1 %collective-permute-start.3 = (bf16[288,128]{1,0:T(8,128)(2,1)S(1)}, bf16[288,128]{1,0:T(8,128)(2,1)S(1)}, u32[]{:S(2)}, u32[]{:S(2)}) collective-permute-start(bf16[288,128]{1,0:T(8,128)(2,1)S(1)} %add_convert_fusion.mine_ref), channel_id=1, source_target_pairs={{32,64},{96,0},{64,32},{0,96},{33,65},{97,1},{65,33},{1,97},{34,66... | collective-permute-start | bytes 221192 | tf_op jit(solution)/shard_map/ppermute | solution.py:350
  65.8 19.2 %copy-start.26 = (bf16[128,256]{1,0:T(8,128)(2,1)S(1)}, bf16[128,256]{1,0:T(8,128)(2,1)}, u32[]{:S(2)}) copy-start(bf16[128,256]{1,0:T(8,128)(2,1)} %get-tuple-element.81) | copy-start | bytes 196612
  65.8 27.0 %all-to-all-start.1 = ((bf16[16,288,128]{2,1,0:T(8,128)(2,1)}), bf16[16,288,128]{2,1,0:T(8,128)(2,1)S(1)}, u32[]{:S(2)}, u32[]{:S(2)}) async-start(bf16[16,288,128]{2,1,0:T(8,128)(2,1)} %outer_step.1), calls=%async_computation.1 | async-start | bytes 2359296 | tf_op jit(solution)/shard_map/all_to_all | solution.py:379
  73.2 18.9 %collective-permute-start.7 = (bf16[128,768]{1,0:T(8,128)(2,1)}, bf16[128,768]{1,0:T(8,128)(2,1)S(1)}, u32[]{:S(2)}, u32[]{:S(2)}) collective-permute-start(bf16[128,768]{1,0:T(8,128)(2,1)} %pad_maximum_fusion.3), channel_id=1, source_target_pairs={{0,8},{4,12},{8,0},{12,4},{1,9},{5,13},{9,1},{13,5},{2,10},{6,14},... | collective-permute-start | bytes 589832 | tf_op jit(solution)/shard_map/ppermute | solution.py:368
  92.8 5.4 %collective-permute-start.8 = (bf16[16,288,128]{2,1,0:T(8,128)(2,1)S(1)}, bf16[16,288,128]{2,1,0:T(8,128)(2,1)S(1)}, u32[]{:S(2)}, u32[]{:S(2)}) collective-permute-start(bf16[16,288,128]{2,1,0:T(8,128)(2,1)S(1)} %all-to-all-done.1), channel_id=1, source_target_pairs={{0,16},{16,0},{1,17},{17,1},{2,18},{18,2},{3,19},{19,3},{4,20},{20... | collective-permute-start | bytes 3538952 | tf_op jit(solution)/shard_map/ppermute | solution.py:405
  104.5 26.0 %copy-start.2 = (bf16[8,288,128]{2,1,0:T(8,128)(2,1)S(1)}, bf16[8,288,128]{2,1,0:T(8,128)(2,1)}, u32[]{:S(2)}) copy-start(bf16[8,288,128]{2,1,0:T(8,128)(2,1)} %get-tuple-element.36.delta_ref) | copy-start | bytes 1769476
  104.5 38.1 %all-to-all-start.2 = ((bf16[4,512,256]{2,1,0:T(8,128)(2,1)}), bf16[4,512,256]{2,1,0:T(8,128)(2,1)}, u32[]{:S(2)}, u32[]{:S(2)}) async-start(bf16[4,512,256]{2,1,0:T(8,128)(2,1)} %copy-done.1), calls=%async_computation.2 | async-start | bytes 2097152 | tf_op jit(solution)/shard_map/all_to_all | solution.py:379
  122.1 15.9 %collective-permute-start.9 = (bf16[512,256]{1,0:T(8,128)(2,1)S(1)}, bf16[512,256]{1,0:T(8,128)(2,1)S(1)}, u32[]{:S(2)}, u32[]{:S(2)}) collective-permute-start(bf16[512,256]{1,0:T(8,128)(2,1)S(1)} %get-tuple-element.61), channel_id=1, source_target_pairs={{0,1},{1,2},{2,3},{3,0},{4,5},{5,6},{6,7},{7,4},{8,9},{9,10},{10,1... | collective-permute-start | bytes 786440 | tf_op jit(solution)/shard_map/ppermute | solution.py:375
  124.3 14.4 %collective-permute-start.10 = (bf16[512,256]{1,0:T(8,128)(2,1)S(1)}, bf16[512,256]{1,0:T(8,128)(2,1)S(1)}, u32[]{:S(2)}, u32[]{:S(2)}) collective-permute-start(bf16[512,256]{1,0:T(8,128)(2,1)S(1)} %get-tuple-element.62), channel_id=1, source_target_pairs={{0,2},{1,3},{2,0},{3,1},{4,6},{5,7},{6,4},{7,5},{8,10},{9,11},{10,... | collective-permute-start | bytes 786440 | tf_op jit(solution)/shard_map/ppermute | solution.py:375
  127.2 13.3 %collective-permute-start.11 = (bf16[512,256]{1,0:T(8,128)(2,1)S(1)}, bf16[512,256]{1,0:T(8,128)(2,1)S(1)}, u32[]{:S(2)}, u32[]{:S(2)}) collective-permute-start(bf16[512,256]{1,0:T(8,128)(2,1)S(1)} %get-tuple-element.63), channel_id=1, source_target_pairs={{0,3},{1,0},{2,1},{3,2},{4,7},{5,4},{6,5},{7,6},{8,11},{9,8},{10,9... | collective-permute-start | bytes 786440 | tf_op jit(solution)/shard_map/ppermute | solution.py:375
  142.6 13.1 %copy-start.10 = (bf16[512,256]{1,0:T(8,128)(2,1)S(1)}, bf16[512,256]{1,0:T(8,128)(2,1)}, u32[]{:S(2)}) copy-start(bf16[512,256]{1,0:T(8,128)(2,1)} %copy-done.9) | copy-start | bytes 786436
  142.6 13.1 %copy-start.12 = (bf16[512,256]{1,0:T(8,128)(2,1)S(1)}, bf16[512,256]{1,0:T(8,128)(2,1)}, u32[]{:S(2)}) copy-start(bf16[512,256]{1,0:T(8,128)(2,1)} %copy-done.11) | copy-start | bytes 786436
  142.6 13.1 %copy-start.14 = (bf16[512,256]{1,0:T(8,128)(2,1)S(1)}, bf16[512,256]{1,0:T(8,128)(2,1)}, u32[]{:S(2)}) copy-start(bf16[512,256]{1,0:T(8,128)(2,1)} %copy-done.13) | copy-start | bytes 786436
  142.6 13.1 %copy-start.16 = (bf16[512,256]{1,0:T(8,128)(2,1)S(1)}, bf16[512,256]{1,0:T(8,128)(2,1)}, u32[]{:S(2)}) copy-start(bf16[512,256]{1,0:T(8,128)(2,1)} %copy-done.15) | copy-start | bytes 786436
  (20 other events, 55.6 us)
Sparse Core Ops, SparseCore 0:
  10.7 46.0 all-gather.1

commit v8 on v7

--- a/solution.py
+++ b/solution.py
@@ -391,11 +391,10 @@
     sent, hidden_here[1] = lax.optimization_barrier((sent, hidden_here[1]))
     eighth = jnp.sum(sent.astype(jnp.float32), axis=0).astype(jnp.bfloat16)
     pair = add(eighth, swap(eighth, "zh", [(0, 1), (2, 3)])).astype(jnp.bfloat16)
-    pair, hidden_here[2] = lax.optimization_barrier((pair, hidden_here[2]))
     swapped = swap(pair, "zh", [(1, 2), (3, 0)])
     both = deal([queries[0], values[0]], "zl")
-    swapped, hidden_here[3], both[1], both[3] = lax.optimization_barrier(
-        (swapped, hidden_here[3], both[1], both[3])
+    swapped, hidden_here[2], hidden_here[3], both[1] = lax.optimization_barrier(
+        (swapped, hidden_here[2], hidden_here[3], both[1])
     )
     outer = outer_step(place, pair, swapped, base, momentum)
 

time: 189 us -> 190 us (level)
  the two profiles are of different devices: /device:TPU:1 before, /device:TPU:128 now
where the time goes in v8:
time: 190 us; the launch traced here: 189 us
  starting transfers between devices  74.7 us (39%)
  blocking collectives  31.1 us (16%)
  waiting for transfers between devices  27.7 us (15%)
  Pallas kernels  21.9 us (12%)
  local copies, waits for them, and re-layouts  15.8 us (8%)
  between operations  14.4 us (8%)
  other arithmetic  3.2 us (2%)
    ppermute x6, starting transfers between devices, deal(): piece = lax.ppermute(piece, axis, [(i, (i + step) % 4) for i in range(4)])  34.5 us
    all_to_all x2, blocking collectives, exchange(): return lax.all_to_all(array, axis, 0, 0, tiled=True)  31.1 us
    all_to_all x3, starting transfers between devices, exchange(): return lax.all_to_all(array, axis, 0, 0, tiled=True)  17 us
    ppermute x6, waiting for transfers between devices, deal(): piece = lax.ppermute(piece, axis, [(i, (i + step) % 4) for i in range(4)])  16 us
    unnamed x58, local copies, waits for them, and re-layouts  13.4 us
    ppermute x2, starting transfers between devices, swap(): return lax.ppermute(array, axis, pairs + [(b, a) for a, b in pairs])  12.3 us
    ppermute x3, starting transfers between devices, turn(): lax.ppermute(a, axis, shift)  9.03 us
    ppermute x3, waiting for transfers between devices, turn(): lax.ppermute(a, axis, shift)  6.98 us
  transfers between devices with their start and end apart: 16, of which 7 were waited for; matrix products, arithmetic and copies ran while one was open for 3% of the time, Pallas kernels for 5%

profile of v8, /device:TPU:128, one launch (start us, length us, event | category | flops | bytes accessed | tf_op | source)
XLA Modules:
  0.0 188.8 jit_solution(18368267208703745056)
XLA Ops:
  7.2 3.3 %prep.1 = (bf16[8,288,128]{2,1,0:T(8,128)(2,1)}, bf16[288,1024]{1,0:T(8,128)(2,1)}) custom-call(bf16[288,1024]{1,0:T(8,128)(2,1)} %bitcast.43, s32[8,288]{1,0:T(8,128)} %bitcast.45, bf16[288,1024]{1,0:T(8,128)(2,1)} %base_ref.3), custom_call_target="tpu_custom_call" | custom-call | tf_op jit(solution)/shard_map/prep/pallas_call | solution.py:64
  10.5 4.4 %all-to-all-start = ((bf16[8,288,128]{2,1,0:T(8,128)(2,1)}), bf16[8,288,128]{2,1,0:T(8,128)(2,1)S(1)}, u32[]{:S(2)}, u32[]{:S(2)}) async-start(bf16[8,288,128]{2,1,0:T(8,128)(2,1)} %get-tuple-element.34.delta_ref), calls=%async_computation | async-start | bytes 1179648 | tf_op jit(solution)/shard_map/all_to_all | solution.py:379
  15.9 3.8 %collective-permute-start = (bf16[128,1152]{1,0:T(8,128)(2,1)}, bf16[128,1152]{1,0:T(8,128)(2,1)S(1)}, u32[]{:S(2)}, u32[]{:S(2)}) collective-permute-start(bf16[128,1152]{1,0:T(8,128)(2,1)} %get-tuple-element.68), channel_id=1, source_target_pairs={{0,4},{4,8},{8,12},{12,0},{1,5},{5,9},{9,13},{13,1},{2,6},{6,10},{... | collective-permute-start | bytes 884744 | tf_op jit(solution)/shard_map/ppermute | solution.py:368
  21.2 9.1 %collective-permute-done.refs_1_ = bf16[128,1152]{1,0:T(8,128)(2,1)S(1)} collective-permute-done((bf16[128,1152]{1,0:T(8,128)(2,1)}, bf16[128,1152]{1,0:T(8,128)(2,1)S(1)}, u32[]{:S(2)}, u32[]{:S(2)}) %collective-permute-start) | collective-permute-done | bytes 294944 | tf_op jit(solution)/shard_map/ppermute | solution.py:368
  30.4 4.1 %collective-permute-start.1 = (bf16[288,128]{1,0:T(8,128)(2,1)S(1)}, bf16[288,128]{1,0:T(8,128)(2,1)S(1)}, u32[]{:S(2)}, u32[]{:S(2)}) collective-permute-start(bf16[288,128]{1,0:T(8,128)(2,1)S(1)} %reduce_sum.12), channel_id=1, source_target_pairs={{0,32},{64,96},{32,0},{96,64},{1,33},{65,97},{33,1},{97,65},{2,34}... | collective-permute-start | bytes 221192 | tf_op jit(solution)/shard_map/ppermute | solution.py:350
  35.4 1.9 %collective-permute-start.5 = (bf16[128,768]{1,0:T(8,128)(2,1)S(1)}, bf16[128,768]{1,0:T(8,128)(2,1)S(1)}, u32[]{:S(2)}, u32[]{:S(2)}) collective-permute-start(bf16[128,768]{1,0:T(8,128)(2,1)S(1)} %pad_maximum_fusion), channel_id=1, source_target_pairs={{0,4},{4,8},{8,12},{12,0},{1,5},{5,9},{9,13},{13,1},{2,6},{6,10},{... | collective-permute-start | bytes 589832 | tf_op jit(solution)/shard_map/ppermute | solution.py:368
  37.4 2.1 %collective-permute-start.3 = (bf16[128,1152]{1,0:T(8,128)(2,1)}, bf16[128,1152]{1,0:T(8,128)(2,1)S(1)}, u32[]{:S(2)}, u32[]{:S(2)}) collective-permute-start(bf16[128,1152]{1,0:T(8,128)(2,1)} %get-tuple-element.67), channel_id=1, source_target_pairs={{0,8},{4,12},{8,0},{12,4},{1,9},{5,13},{9,1},{13,5},{2,10},{6,14},... | collective-permute-start | bytes 884744 | tf_op jit(solution)/shard_map/ppermute | solution.py:368
  39.5 5.5 %collective-permute-start.4 = (bf16[128,1152]{1,0:T(8,128)(2,1)}, bf16[128,1152]{1,0:T(8,128)(2,1)S(1)}, u32[]{:S(2)}, u32[]{:S(2)}) collective-permute-start(bf16[128,1152]{1,0:T(8,128)(2,1)} %get-tuple-element.69), channel_id=1, source_target_pairs={{0,12},{4,0},{8,4},{12,8},{1,13},{5,1},{9,5},{13,9},{2,14},{6,2},{... | collective-permute-start | bytes 884744 | tf_op jit(solution)/shard_map/ppermute | solution.py:368
  45.1 8.2 %collective-permute-start.2 = (bf16[288,128]{1,0:T(8,128)(2,1)S(1)}, bf16[288,128]{1,0:T(8,128)(2,1)S(1)}, u32[]{:S(2)}, u32[]{:S(2)}) collective-permute-start(bf16[288,128]{1,0:T(8,128)(2,1)S(1)} %add_convert_fusion.mine_ref), channel_id=1, source_target_pairs={{32,64},{96,0},{64,32},{0,96},{33,65},{97,1},{65,33},{1,97},{34,66... | collective-permute-start | bytes 221192 | tf_op jit(solution)/shard_map/ppermute | solution.py:350
  53.4 6.1 %collective-permute-done.3.refs_2_ = bf16[128,1152]{1,0:T(8,128)(2,1)S(1)} collective-permute-done((bf16[128,1152]{1,0:T(8,128)(2,1)}, bf16[128,1152]{1,0:T(8,128)(2,1)S(1)}, u32[]{:S(2)}, u32[]{:S(2)}) %collective-permute-start.3) | collective-permute-done | bytes 294944 | tf_op jit(solution)/shard_map/ppermute | solution.py:368
  62.1 5.3 %all-to-all-start.1 = ((bf16[16,288,128]{2,1,0:T(8,128)(2,1)}), bf16[16,288,128]{2,1,0:T(8,128)(2,1)S(1)}, u32[]{:S(2)}, u32[]{:S(2)}) async-start(bf16[16,288,128]{2,1,0:T(8,128)(2,1)} %outer_step.1), calls=%async_computation.1 | async-start | bytes 2359296 | tf_op jit(solution)/shard_map/all_to_all | solution.py:379
  68.1 19.2 %collective-permute-start.6 = (bf16[128,768]{1,0:T(8,128)(2,1)}, bf16[128,768]{1,0:T(8,128)(2,1)S(1)}, u32[]{:S(2)}, u32[]{:S(2)}) collective-permute-start(bf16[128,768]{1,0:T(8,128)(2,1)} %pad_maximum_fusion.2), channel_id=1, source_target_pairs={{0,8},{4,12},{8,0},{12,4},{1,9},{5,13},{9,1},{13,5},{2,10},{6,14},... | collective-permute-start | bytes 589832 | tf_op jit(solution)/shard_map/ppermute | solution.py:368
  90.6 4.0 %local_product.1 = (bf16[512,1152]{1,0:T(8,128)(2,1)S(1)}, f32[4,512,256]{2,1,0:T(8,128)S(1)}) custom-call(s32[4]{0:T(128)S(1)} %pad_add_fusion.place_ref, bf16[128,1152]{1,0:T(8,128)(2,1)S(1)} %get-tuple-element.66.refs_0_, bf16[128,1152]{1,0:T(8,128)(2,1)S(1)} %collective-permute-done.refs_1_, bf16[128,1152]{1,0:T(8,128)(2,1)S(1)} %collective-permute-done.3.refs_2_, ...), custom_call_target="tpu_custom_call" | custom-call | tf_op jit(solution)/shard_map/local_product/pallas_call | solution.py:133
  98.4 1.9 %collective-permute-start.8 = (bf16[16,288,128]{2,1,0:T(8,128)(2,1)S(1)}, bf16[16,288,128]{2,1,0:T(8,128)(2,1)S(1)}, u32[]{:S(2)}, u32[]{:S(2)}) collective-permute-start(bf16[16,288,128]{2,1,0:T(8,128)(2,1)S(1)} %all-to-all-done.1), channel_id=1, source_target_pairs={{0,16},{16,0},{1,17},{17,1},{2,18},{18,2},{3,19},{19,3},{4,20},{20... | collective-permute-start | bytes 3538952 | tf_op jit(solution)/shard_map/ppermute | solution.py:404
  100.3 2.8 %collective-permute-done.8 = bf16[16,288,128]{2,1,0:T(8,128)(2,1)S(1)} collective-permute-done((bf16[16,288,128]{2,1,0:T(8,128)(2,1)S(1)}, bf16[16,288,128]{2,1,0:T(8,128)(2,1)S(1)}, u32[]{:S(2)}, u32[]{:S(2)}) %collective-permute-start.8) | collective-permute-done | bytes 1179680 | tf_op jit(solution)/shard_map/ppermute | solution.py:404
  106.0 2.4 %project.1 = bf16[4,512,256]{2,1,0:T(8,128)(2,1)S(1)} custom-call(s32[4]{0:T(128)S(1)} %pad_add_fusion.place_ref, bf16[512,1152]{1,0:T(8,128)(2,1)S(1)} %copy-done.6, f32[4,512,256]{2,1,0:T(8,128)S(1)} %copy-done.4, bf16[4,1152,128]{2,1,0:T(8,128)(2,1)S(1)} %bitcast.38, bf16[4,1152,128]{2,1,0:T(8,128)(2,1)S(1)} %bitcast.40), custom_call_target="tpu_custom_call" | custom-call | tf_op jit(solution)/shard_map/project/pallas_call | solution.py:163
  109.4 7.2 %all-to-all-start.2 = ((bf16[4,512,256]{2,1,0:T(8,128)(2,1)}), bf16[4,512,256]{2,1,0:T(8,128)(2,1)}, u32[]{:S(2)}, u32[]{:S(2)}) async-start(bf16[4,512,256]{2,1,0:T(8,128)(2,1)} %copy-done.1), calls=%async_computation.2 | async-start | bytes 2097152 | tf_op jit(solution)/shard_map/all_to_all | solution.py:379
  121.5 2.5 %collective-permute-start.9 = (bf16[512,256]{1,0:T(8,128)(2,1)S(1)}, bf16[512,256]{1,0:T(8,128)(2,1)S(1)}, u32[]{:S(2)}, u32[]{:S(2)}) collective-permute-start(bf16[512,256]{1,0:T(8,128)(2,1)S(1)} %get-tuple-element.57), channel_id=1, source_target_pairs={{0,1},{1,2},{2,3},{3,0},{4,5},{5,6},{6,7},{7,4},{8,9},{9,10},{10,1... | collective-permute-start | bytes 786440 | tf_op jit(solution)/shard_map/ppermute | solution.py:375
  124.0 3.1 %collective-permute-start.10 = (bf16[512,256]{1,0:T(8,128)(2,1)S(1)}, bf16[512,256]{1,0:T(8,128)(2,1)S(1)}, u32[]{:S(2)}, u32[]{:S(2)}) collective-permute-start(bf16[512,256]{1,0:T(8,128)(2,1)S(1)} %get-tuple-element.58), channel_id=1, source_target_pairs={{0,2},{1,3},{2,0},{3,1},{4,6},{5,7},{6,4},{7,5},{8,10},{9,11},{10,... | collective-permute-start | bytes 786440 | tf_op jit(solution)/shard_map/ppermute | solution.py:375
  127.1 3.4 %collective-permute-start.11 = (bf16[512,256]{1,0:T(8,128)(2,1)S(1)}, bf16[512,256]{1,0:T(8,128)(2,1)S(1)}, u32[]{:S(2)}, u32[]{:S(2)}) collective-permute-start(bf16[512,256]{1,0:T(8,128)(2,1)S(1)} %get-tuple-element.59), channel_id=1, source_target_pairs={{0,3},{1,0},{2,1},{3,2},{4,7},{5,4},{6,5},{7,6},{8,11},{9,8},{10,9... | collective-permute-start | bytes 786440 | tf_op jit(solution)/shard_map/ppermute | solution.py:375
  132.4 5.8 %collective-permute-done.9.refs_1_ = bf16[512,256]{1,0:T(8,128)(2,1)S(1)} collective-permute-done((bf16[512,256]{1,0:T(8,128)(2,1)S(1)}, bf16[512,256]{1,0:T(8,128)(2,1)S(1)}, u32[]{:S(2)}, u32[]{:S(2)}) %collective-permute-start.9) | collective-permute-done | bytes 262176 | tf_op jit(solution)/shard_map/ppermute | solution.py:375
  144.8 12.1 %all_to_all.25.keys_any = bf16[4,512,128]{2,1,0:T(8,128)(2,1)S(1)} all-to-all(bf16[4,512,128]{2,1,0:T(8,128)(2,1)S(1)} %reduce_keys.1), channel_id=1, replica_groups=mesh['x'=4,'zh'=4,'c'=2,'zl'=4,'y'=4] {'y'}, dimensions={0} | all-to-all | bytes 1048576 | tf_op jit(solution)/shard_map/all_to_all | solution.py:379
  156.9 5.1 %attend.1 = bf16[16,128,128]{2,1,0:T(8,128)(2,1)S(1)} custom-call(s32[4]{0:T(128)S(1)} %pad_add_fusion.place_ref, bf16[4,512,128]{2,1,0:T(8,128)(2,1)S(1)} %all_to_all.25.keys_any, bf16[512,256]{1,0:T(8,128)(2,1)S(1)} %copy-done.10, bf16[512,256]{1,0:T(8,128)(2,1)S(1)} %copy-done.12, bf16[512,256]{1,0:T(8,128)(2,1)S(1)} %copy-done.14, ...), custom_call_target="tpu_custom_call" | custom-call | tf_op jit(solution)/shard_map/attend/pallas_call | solution.py:315
  162.0 19.0 %all_to_all.26.mixed_any = bf16[16,128,128]{2,1,0:T(8,128)(2,1)S(1)} all-to-all(bf16[16,128,128]{2,1,0:T(8,128)(2,1)S(1)} %attend.1), channel_id=1, replica_groups=mesh['x'=4,'zh'=4,'c'=2,'zl'=4,'y'=4] {'zl','y'}, dimensions={0} | all-to-all | bytes 1048576 | tf_op jit(solution)/shard_map/all_to_all | solution.py:379
  (88 shorter events, 31.8 us)
Async XLA Ops:
  7.2 83.5 %all-gather.2.cloned.1.call-start = ((), (), s32[]{:S(2)}) async-start(), calls=%async_computation.5 | async-start | bytes 2949120 | tf_op jit(solution)/shard_map/all_gather | solution.py:387
  10.5 19.8 %all-to-all-start = ((bf16[8,288,128]{2,1,0:T(8,128)(2,1)}), bf16[8,288,128]{2,1,0:T(8,128)(2,1)S(1)}, u32[]{:S(2)}, u32[]{:S(2)}) async-start(bf16[8,288,128]{2,1,0:T(8,128)(2,1)} %get-tuple-element.34.delta_ref), calls=%async_computation | async-start | bytes 1179648 | tf_op jit(solution)/shard_map/all_to_all | solution.py:379
  15.9 14.4 %collective-permute-start = (bf16[128,1152]{1,0:T(8,128)(2,1)}, bf16[128,1152]{1,0:T(8,128)(2,1)S(1)}, u32[]{:S(2)}, u32[]{:S(2)}) collective-permute-start(bf16[128,1152]{1,0:T(8,128)(2,1)} %get-tuple-element.68), channel_id=1, source_target_pairs={{0,4},{4,8},{8,12},{12,0},{1,5},{5,9},{9,13},{13,1},{2,6},{6,10},{... | collective-permute-start | bytes 884744 | tf_op jit(solution)/shard_map/ppermute | solution.py:368
  20.5 14.0 %copy-start.28 = (bf16[128,256]{1,0:T(8,128)(2,1)S(1)}, bf16[128,256]{1,0:T(8,128)(2,1)}, u32[]{:S(2)}) copy-start(bf16[128,256]{1,0:T(8,128)(2,1)} %get-tuple-element.76) | copy-start | bytes 196612
  20.5 39.8 %copy-start = (bf16[288,1024]{1,0:T(8,128)(2,1)S(1)}, bf16[288,1024]{1,0:T(8,128)(2,1)}, u32[]{:S(2)}) copy-start(bf16[288,1024]{1,0:T(8,128)(2,1)} %base_ref.3) | copy-start | bytes 1769476
  20.5 39.8 %copy-start.8 = (bf16[288,1024]{1,0:T(8,128)(2,1)S(1)}, bf16[288,1024]{1,0:T(8,128)(2,1)}, u32[]{:S(2)}) copy-start(bf16[288,1024]{1,0:T(8,128)(2,1)} %momentum_ref.1) | copy-start | bytes 1769476
  30.4 14.6 %collective-permute-start.1 = (bf16[288,128]{1,0:T(8,128)(2,1)S(1)}, bf16[288,128]{1,0:T(8,128)(2,1)S(1)}, u32[]{:S(2)}, u32[]{:S(2)}) collective-permute-start(bf16[288,128]{1,0:T(8,128)(2,1)S(1)} %reduce_sum.12), channel_id=1, source_target_pairs={{0,32},{64,96},{32,0},{96,64},{1,33},{65,97},{33,1},{97,65},{2,34}... | collective-permute-start | bytes 221192 | tf_op jit(solution)/shard_map/ppermute | solution.py:350
  35.4 17.9 %collective-permute-start.5 = (bf16[128,768]{1,0:T(8,128)(2,1)S(1)}, bf16[128,768]{1,0:T(8,128)(2,1)S(1)}, u32[]{:S(2)}, u32[]{:S(2)}) collective-permute-start(bf16[128,768]{1,0:T(8,128)(2,1)S(1)} %pad_maximum_fusion), channel_id=1, source_target_pairs={{0,4},{4,8},{8,12},{12,0},{1,5},{5,9},{9,13},{13,1},{2,6},{6,10},{... | collective-permute-start | bytes 589832 | tf_op jit(solution)/shard_map/ppermute | solution.py:368
  37.4 22.2 %collective-permute-start.3 = (bf16[128,1152]{1,0:T(8,128)(2,1)}, bf16[128,1152]{1,0:T(8,128)(2,1)S(1)}, u32[]{:S(2)}, u32[]{:S(2)}) collective-permute-start(bf16[128,1152]{1,0:T(8,128)(2,1)} %get-tuple-element.67), channel_id=1, source_target_pairs={{0,8},{4,12},{8,0},{12,4},{1,9},{5,13},{9,1},{13,5},{2,10},{6,14},... | collective-permute-start | bytes 884744 | tf_op jit(solution)/shard_map/ppermute | solution.py:368
  39.5 20.8 %collective-permute-start.4 = (bf16[128,1152]{1,0:T(8,128)(2,1)}, bf16[128,1152]{1,0:T(8,128)(2,1)S(1)}, u32[]{:S(2)}, u32[]{:S(2)}) collective-permute-start(bf16[128,1152]{1,0:T(8,128)(2,1)} %get-tuple-element.69), channel_id=1, source_target_pairs={{0,12},{4,0},{8,4},{12,8},{1,13},{5,1},{9,5},{13,9},{2,14},{6,2},{... | collective-permute-start | bytes 884744 | tf_op jit(solution)/shard_map/ppermute | solution.py:368
  45.1 15.3 %collective-permute-start.2 = (bf16[288,128]{1,0:T(8,128)(2,1)S(1)}, bf16[288,128]{1,0:T(8,128)(2,1)S(1)}, u32[]{:S(2)}, u32[]{:S(2)}) collective-permute-start(bf16[288,128]{1,0:T(8,128)(2,1)S(1)} %add_convert_fusion.mine_ref), channel_id=1, source_target_pairs={{32,64},{96,0},{64,32},{0,96},{33,65},{97,1},{65,33},{1,97},{34,66... | collective-permute-start | bytes 221192 | tf_op jit(solution)/shard_map/ppermute | solution.py:350
  62.1 27.9 %copy-start.26 = (bf16[128,256]{1,0:T(8,128)(2,1)S(1)}, bf16[128,256]{1,0:T(8,128)(2,1)}, u32[]{:S(2)}) copy-start(bf16[128,256]{1,0:T(8,128)(2,1)} %get-tuple-element.75) | copy-start | bytes 196612
  62.1 36.3 %all-to-all-start.1 = ((bf16[16,288,128]{2,1,0:T(8,128)(2,1)}), bf16[16,288,128]{2,1,0:T(8,128)(2,1)S(1)}, u32[]{:S(2)}, u32[]{:S(2)}) async-start(bf16[16,288,128]{2,1,0:T(8,128)(2,1)} %outer_step.1), calls=%async_computation.1 | async-start | bytes 2359296 | tf_op jit(solution)/shard_map/all_to_all | solution.py:379
  68.1 28.8 %collective-permute-start.6 = (bf16[128,768]{1,0:T(8,128)(2,1)}, bf16[128,768]{1,0:T(8,128)(2,1)S(1)}, u32[]{:S(2)}, u32[]{:S(2)}) collective-permute-start(bf16[128,768]{1,0:T(8,128)(2,1)} %pad_maximum_fusion.2), channel_id=1, source_target_pairs={{0,8},{4,12},{8,0},{12,4},{1,9},{5,13},{9,1},{13,5},{2,10},{6,14},... | collective-permute-start | bytes 589832 | tf_op jit(solution)/shard_map/ppermute | solution.py:368
  88.0 9.7 %collective-permute-start.7 = (bf16[128,768]{1,0:T(8,128)(2,1)}, bf16[128,768]{1,0:T(8,128)(2,1)S(1)}, u32[]{:S(2)}, u32[]{:S(2)}) collective-permute-start(bf16[128,768]{1,0:T(8,128)(2,1)} %pad_maximum_fusion.3), channel_id=1, source_target_pairs={{0,12},{4,0},{8,4},{12,8},{1,13},{5,1},{9,5},{13,9},{2,14},{6,2},{... | collective-permute-start | bytes 589832 | tf_op jit(solution)/shard_map/ppermute | solution.py:368
  98.4 4.7 %collective-permute-start.8 = (bf16[16,288,128]{2,1,0:T(8,128)(2,1)S(1)}, bf16[16,288,128]{2,1,0:T(8,128)(2,1)S(1)}, u32[]{:S(2)}, u32[]{:S(2)}) collective-permute-start(bf16[16,288,128]{2,1,0:T(8,128)(2,1)S(1)} %all-to-all-done.1), channel_id=1, source_target_pairs={{0,16},{16,0},{1,17},{17,1},{2,18},{18,2},{3,19},{19,3},{4,20},{20... | collective-permute-start | bytes 3538952 | tf_op jit(solution)/shard_map/ppermute | solution.py:404
  109.4 21.1 %copy-start.2 = (bf16[8,288,128]{2,1,0:T(8,128)(2,1)S(1)}, bf16[8,288,128]{2,1,0:T(8,128)(2,1)}, u32[]{:S(2)}) copy-start(bf16[8,288,128]{2,1,0:T(8,128)(2,1)} %get-tuple-element.34.delta_ref) | copy-start | bytes 1769476
  109.4 33.9 %all-to-all-start.2 = ((bf16[4,512,256]{2,1,0:T(8,128)(2,1)}), bf16[4,512,256]{2,1,0:T(8,128)(2,1)}, u32[]{:S(2)}, u32[]{:S(2)}) async-start(bf16[4,512,256]{2,1,0:T(8,128)(2,1)} %copy-done.1), calls=%async_computation.2 | async-start | bytes 2097152 | tf_op jit(solution)/shard_map/all_to_all | solution.py:379
  121.5 16.8 %collective-permute-start.9 = (bf16[512,256]{1,0:T(8,128)(2,1)S(1)}, bf16[512,256]{1,0:T(8,128)(2,1)S(1)}, u32[]{:S(2)}, u32[]{:S(2)}) collective-permute-start(bf16[512,256]{1,0:T(8,128)(2,1)S(1)} %get-tuple-element.57), channel_id=1, source_target_pairs={{0,1},{1,2},{2,3},{3,0},{4,5},{5,6},{6,7},{7,4},{8,9},{9,10},{10,1... | collective-permute-start | bytes 786440 | tf_op jit(solution)/shard_map/ppermute | solution.py:375
  124.0 15.0 %collective-permute-start.10 = (bf16[512,256]{1,0:T(8,128)(2,1)S(1)}, bf16[512,256]{1,0:T(8,128)(2,1)S(1)}, u32[]{:S(2)}, u32[]{:S(2)}) collective-permute-start(bf16[512,256]{1,0:T(8,128)(2,1)S(1)} %get-tuple-element.58), channel_id=1, source_target_pairs={{0,2},{1,3},{2,0},{3,1},{4,6},{5,7},{6,4},{7,5},{8,10},{9,11},{10,... | collective-permute-start | bytes 786440 | tf_op jit(solution)/shard_map/ppermute | solution.py:375
  127.1 13.7 %collective-permute-start.11 = (bf16[512,256]{1,0:T(8,128)(2,1)S(1)}, bf16[512,256]{1,0:T(8,128)(2,1)S(1)}, u32[]{:S(2)}, u32[]{:S(2)}) collective-permute-start(bf16[512,256]{1,0:T(8,128)(2,1)S(1)} %get-tuple-element.59), channel_id=1, source_target_pairs={{0,3},{1,0},{2,1},{3,2},{4,7},{5,4},{6,5},{7,6},{8,11},{9,8},{10,9... | collective-permute-start | bytes 786440 | tf_op jit(solution)/shard_map/ppermute | solution.py:375
  143.3 13.6 %copy-start.12 = (bf16[512,256]{1,0:T(8,128)(2,1)S(1)}, bf16[512,256]{1,0:T(8,128)(2,1)}, u32[]{:S(2)}) copy-start(bf16[512,256]{1,0:T(8,128)(2,1)} %copy-done.11) | copy-start | bytes 786436
  143.3 13.6 %copy-start.14 = (bf16[512,256]{1,0:T(8,128)(2,1)S(1)}, bf16[512,256]{1,0:T(8,128)(2,1)}, u32[]{:S(2)}) copy-start(bf16[512,256]{1,0:T(8,128)(2,1)} %copy-done.13) | copy-start | bytes 786436
  143.3 13.6 %copy-start.16 = (bf16[512,256]{1,0:T(8,128)(2,1)S(1)}, bf16[512,256]{1,0:T(8,128)(2,1)}, u32[]{:S(2)}) copy-start(bf16[512,256]{1,0:T(8,128)(2,1)} %copy-done.15) | copy-start | bytes 786436
  (21 other events, 66.8 us)
Sparse Core Ops, SparseCore 0:
  10.6 43.7 all-gather.1

commit v9 on v7

--- a/solution.py
+++ b/solution.py
@@ -142,19 +142,33 @@
             pltpu.VMEM(part.shape, jnp.bfloat16),
             pltpu.SemaphoreType.DMA((2 * NZL,)),
         ],
-        compiler_params=params(48),
+        compiler_params=params(),
         name="local_product",
     )(place, *hidden, part)
 
 
-def project_kernel(place_ref, hidden_ref, local_ref, same_ref, other_ref, out_ref, weight):
+def project_kernel(place_ref, hidden_any, local_any, same_any, other_any, out_ref, *refs):
+    hidden, local, pieces, weight, sems, local_sems, hidden_sem = refs
     c = place_ref[0]
+    hidden_copy = pltpu.make_async_copy(hidden_any, hidden, hidden_sem)
+    copies = []
     for n in range(NZL):
-        for near, ref in enumerate((same_ref, other_ref)):
+        for near, source in enumerate((same_any, other_any)):
+            copies.append(
+                pltpu.make_async_copy(source.at[n], pieces.at[near, n], sems.at[near, n])
+            )
+        copies.append(pltpu.make_async_copy(local_any.at[n], local.at[n], local_sems.at[n]))
+    start_all(copies[:2] + [hidden_copy] + copies[2:])
+    for n in range(NZL):
+        for near in range(NC):
+            copies[3 * n + near].wait()
             at = pl.multiple_of(lax.rem(c + near, NC) * BLOCK, BLOCK)
-            weight[n, :, pl.ds(at, BLOCK)] = ref[n]
-        outer = jnp.dot(hidden_ref[...], weight[n], preferred_element_type=jnp.float32)
-        out_ref[n] = (local_ref[n] + (1.0 - blend_share) * outer).astype(jnp.bfloat16)
+            weight[n, :, pl.ds(at, BLOCK)] = pieces[near, n]
+        if n == 0:
+            hidden_copy.wait()
+        outer = jnp.dot(hidden[...], weight[n], preferred_element_type=jnp.float32)
+        copies[3 * n + 2].wait()
+        out_ref[n] = (local[n] + (1.0 - blend_share) * outer).astype(jnp.bfloat16)
 
 
 def project(place, hidden, local, same, other):
@@ -163,10 +177,18 @@
     return pl.pallas_call(
         project_kernel,
         out_shape=jax.ShapeDtypeStruct((NZL, 512, 2 * BLOCK), jnp.bfloat16),
-        in_specs=[SMEM] + [VMEM] * 4,
+        in_specs=[SMEM] + [ANY] * 4,
         out_specs=VMEM,
-        scratch_shapes=[pltpu.VMEM((NZL, depth, 2 * BLOCK), jnp.bfloat16)],
-        compiler_params=params(20),
+        scratch_shapes=[
+            pltpu.VMEM(hidden.shape, jnp.bfloat16),
+            pltpu.VMEM(local.shape, jnp.float32),
+            pltpu.VMEM((NC,) + blocks, jnp.bfloat16),
+            pltpu.VMEM((NZL, depth, 2 * BLOCK), jnp.bfloat16),
+            pltpu.SemaphoreType.DMA((NC, NZL)),
+            pltpu.SemaphoreType.DMA((NZL,)),
+            pltpu.SemaphoreType.DMA,
+        ],
+        compiler_params=params(),
         name="project",
     )(place, hidden, local, same.reshape(blocks), other.reshape(blocks))
 

time: 189 us -> 191 us (1.011)
  Pallas kernels: 21.9 us -> 29.1 us
  local copies, waits for them, and re-layouts: 15.1 us -> 9.3 us
    pallas_call x1, Pallas kernels: 2.44 us -> 8 us  [project(): pl.pallas_call(project_kernel, out_shape=jax.ShapeDtypeStruct((NZL, 512,...]
    unnamed x56 -> x62, local copies, waits for them, and re-layouts: 12.8 us -> 7.64 us
  transfers between devices with their start and end apart: 16 -> 16, of which waited for: 7 -> 9; matrix products, arithmetic and copies ran while one was open for 3% -> 3% of each run, Pallas kernels for 5% -> 5%
where the time goes in v9:
time: 191 us; the launch traced here: 188 us
  starting transfers between devices  80.4 us (42%)
  blocking collectives  29.3 us (15%)
  Pallas kernels  29.1 us (15%)
  waiting for transfers between devices  22.8 us (12%)
  between operations  14.5 us (8%)
  local copies, waits for them, and re-layouts  9.3 us (5%)
  other arithmetic  3.11 us (2%)
    all_to_all x3, starting transfers between devices, exchange(): return lax.all_to_all(array, axis, 0, 0, tiled=True)  30 us
    all_to_all x2, blocking collectives, exchange(): return lax.all_to_all(array, axis, 0, 0, tiled=True)  29.3 us
    ppermute x6, starting transfers between devices, deal(): piece = lax.ppermute(piece, axis, [(i, (i + step) % 4) for i in range(4)])  26.2 us
    ppermute x2, starting transfers between devices, swap(): return lax.ppermute(array, axis, pairs + [(b, a) for a, b in pairs])  12.1 us
    ppermute x6, waiting for transfers between devices, deal(): piece = lax.ppermute(piece, axis, [(i, (i + step) % 4) for i in range(4)])  9.97 us
    ppermute x3, starting transfers between devices, turn(): lax.ppermute(a, axis, shift)  8.49 us
    pallas_call x1, Pallas kernels, project(): pl.pallas_call(project_kernel, out_shape=jax.ShapeDtypeStruct((NZL, 512,...  8 us
    unnamed x62, local copies, waits for them, and re-layouts  7.64 us
  transfers between devices with their start and end apart: 16, of which 9 were waited for; matrix products, arithmetic and copies ran while one was open for 3% of the time, Pallas kernels for 5%

profile of v9, /device:TPU:1, one launch (start us, length us, event | category | flops | bytes accessed | tf_op | source)
XLA Modules:
  0.0 188.4 jit_solution(16873192405634313434)
XLA Ops:
  7.2 3.3 %prep.1 = (bf16[8,288,128]{2,1,0:T(8,128)(2,1)}, bf16[288,1024]{1,0:T(8,128)(2,1)}) custom-call(bf16[288,1024]{1,0:T(8,128)(2,1)} %bitcast.43, s32[8,288]{1,0:T(8,128)} %bitcast.45, bf16[288,1024]{1,0:T(8,128)(2,1)} %base_ref.3), custom_call_target="tpu_custom_call" | custom-call | tf_op jit(solution)/shard_map/prep/pallas_call | solution.py:64
  10.5 10.5 %all-to-all-start = ((bf16[8,288,128]{2,1,0:T(8,128)(2,1)}), bf16[8,288,128]{2,1,0:T(8,128)(2,1)S(1)}, u32[]{:S(2)}, u32[]{:S(2)}) async-start(bf16[8,288,128]{2,1,0:T(8,128)(2,1)} %get-tuple-element.36.delta_ref), calls=%async_computation | async-start | bytes 1179648 | tf_op jit(solution)/shard_map/all_to_all | solution.py:401
  27.3 5.4 %collective-permute-start.2 = (bf16[128,1152]{1,0:T(8,128)(2,1)}, bf16[128,1152]{1,0:T(8,128)(2,1)S(1)}, u32[]{:S(2)}, u32[]{:S(2)}) collective-permute-start(bf16[128,1152]{1,0:T(8,128)(2,1)} %get-tuple-element.71), channel_id=1, source_target_pairs={{0,8},{4,12},{8,0},{12,4},{1,9},{5,13},{9,1},{13,5},{2,10},{6,14},... | collective-permute-start | bytes 884744 | tf_op jit(solution)/shard_map/ppermute | solution.py:390
  34.4 5.8 %collective-permute-start.1 = (bf16[288,128]{1,0:T(8,128)(2,1)S(1)}, bf16[288,128]{1,0:T(8,128)(2,1)S(1)}, u32[]{:S(2)}, u32[]{:S(2)}) collective-permute-start(bf16[288,128]{1,0:T(8,128)(2,1)S(1)} %reduce_sum.12), channel_id=1, source_target_pairs={{0,32},{64,96},{32,0},{96,64},{1,33},{65,97},{33,1},{97,65},{2,34}... | collective-permute-start | bytes 221192 | tf_op jit(solution)/shard_map/ppermute | solution.py:372
  41.7 3.1 %collective-permute-start.6 = (bf16[128,768]{1,0:T(8,128)(2,1)}, bf16[128,768]{1,0:T(8,128)(2,1)S(1)}, u32[]{:S(2)}, u32[]{:S(2)}) collective-permute-start(bf16[128,768]{1,0:T(8,128)(2,1)} %pad_maximum_fusion.1), channel_id=1, source_target_pairs={{0,12},{4,0},{8,4},{12,8},{1,13},{5,1},{9,5},{13,9},{2,14},{6,2},{... | collective-permute-start | bytes 589832 | tf_op jit(solution)/shard_map/ppermute | solution.py:390
  44.8 1.9 %collective-permute-start.4 = (bf16[128,1152]{1,0:T(8,128)(2,1)S(1)}, bf16[128,1152]{1,0:T(8,128)(2,1)S(1)}, u32[]{:S(2)}, u32[]{:S(2)}) collective-permute-start(bf16[128,1152]{1,0:T(8,128)(2,1)S(1)} %get-tuple-element.73), channel_id=1, source_target_pairs={{0,12},{4,0},{8,4},{12,8},{1,13},{5,1},{9,5},{13,9},{2,14},{6,2},{... | collective-permute-start | bytes 884744 | tf_op jit(solution)/shard_map/ppermute | solution.py:390
  46.8 8.1 %collective-permute-done.2.refs_2_ = bf16[128,1152]{1,0:T(8,128)(2,1)S(1)} collective-permute-done((bf16[128,1152]{1,0:T(8,128)(2,1)}, bf16[128,1152]{1,0:T(8,128)(2,1)S(1)}, u32[]{:S(2)}, u32[]{:S(2)}) %collective-permute-start.2) | collective-permute-done | bytes 294944 | tf_op jit(solution)/shard_map/ppermute | solution.py:390
  54.9 6.3 %collective-permute-start.3 = (bf16[288,128]{1,0:T(8,128)(2,1)S(1)}, bf16[288,128]{1,0:T(8,128)(2,1)S(1)}, u32[]{:S(2)}, u32[]{:S(2)}) collective-permute-start(bf16[288,128]{1,0:T(8,128)(2,1)S(1)} %add_convert_fusion.mine_ref), channel_id=1, source_target_pairs={{32,64},{96,0},{64,32},{0,96},{33,65},{97,1},{65,33},{1,97},{34,66... | collective-permute-start | bytes 221192 | tf_op jit(solution)/shard_map/ppermute | solution.py:372
  61.6 2.4 %collective-permute-done.3.sent_ref = bf16[288,128]{1,0:T(8,128)(2,1)S(1)} collective-permute-done((bf16[288,128]{1,0:T(8,128)(2,1)S(1)}, bf16[288,128]{1,0:T(8,128)(2,1)S(1)}, u32[]{:S(2)}, u32[]{:S(2)}) %collective-permute-start.3) | collective-permute-done | bytes 73760 | tf_op jit(solution)/shard_map/ppermute | solution.py:372
  65.9 6.7 %all-to-all-start.1 = ((bf16[16,288,128]{2,1,0:T(8,128)(2,1)}), bf16[16,288,128]{2,1,0:T(8,128)(2,1)S(1)}, u32[]{:S(2)}, u32[]{:S(2)}) async-start(bf16[16,288,128]{2,1,0:T(8,128)(2,1)} %outer_step.1), calls=%async_computation.1 | async-start | bytes 2359296 | tf_op jit(solution)/shard_map/all_to_all | solution.py:401
  72.6 11.9 %collective-permute-start.7 = (bf16[128,768]{1,0:T(8,128)(2,1)S(1)}, bf16[128,768]{1,0:T(8,128)(2,1)S(1)}, u32[]{:S(2)}, u32[]{:S(2)}) collective-permute-start(bf16[128,768]{1,0:T(8,128)(2,1)S(1)} %pad_maximum_fusion.3), channel_id=1, source_target_pairs={{0,8},{4,12},{8,0},{12,4},{1,9},{5,13},{9,1},{13,5},{2,10},{6,14},... | collective-permute-start | bytes 589832 | tf_op jit(solution)/shard_map/ppermute | solution.py:390
  85.1 5.6 %local_product.1 = (bf16[512,1152]{1,0:T(8,128)(2,1)}, f32[4,512,256]{2,1,0:T(8,128)}) custom-call(s32[4]{0:T(128)} %copy-done.22, bf16[128,1152]{1,0:T(8,128)(2,1)} %get-tuple-element.70.refs_0_, bf16[128,1152]{1,0:T(8,128)(2,1)} %copy-done.26, bf16[128,1152]{1,0:T(8,128)(2,1)} %copy-done.27, bf16[128,1152]{1,0:T(8,128)(2,1)} %copy-done.28, ...), custom_call_target="tpu_custom_call" | custom-call | tf_op jit(solution)/shard_map/local_product/pallas_call | solution.py:133
  91.4 3.6 %collective-permute-start.8 = (bf16[16,288,128]{2,1,0:T(8,128)(2,1)S(1)}, bf16[16,288,128]{2,1,0:T(8,128)(2,1)S(1)}, u32[]{:S(2)}, u32[]{:S(2)}) collective-permute-start(bf16[16,288,128]{2,1,0:T(8,128)(2,1)S(1)} %all-to-all-done.1), channel_id=1, source_target_pairs={{0,16},{16,0},{1,17},{17,1},{2,18},{18,2},{3,19},{19,3},{4,20},{20... | collective-permute-start | bytes 3538952 | tf_op jit(solution)/shard_map/ppermute | solution.py:427
  95.0 2.5 %collective-permute-done.8 = bf16[16,288,128]{2,1,0:T(8,128)(2,1)S(1)} collective-permute-done((bf16[16,288,128]{2,1,0:T(8,128)(2,1)S(1)}, bf16[16,288,128]{2,1,0:T(8,128)(2,1)S(1)}, u32[]{:S(2)}, u32[]{:S(2)}) %collective-permute-start.8) | collective-permute-done | bytes 1179680 | tf_op jit(solution)/shard_map/ppermute | solution.py:427
  98.5 8.0 %project.1 = bf16[4,512,256]{2,1,0:T(8,128)(2,1)} custom-call(s32[4]{0:T(128)} %copy-done.22, bf16[512,1152]{1,0:T(8,128)(2,1)} %get-tuple-element.48.hidden_any, f32[4,512,256]{2,1,0:T(8,128)} %get-tuple-element.49.local_any, bf16[4,1152,128]{2,1,0:T(8,128)(2,1)} %bitcast.38, bf16[4,1152,128]{2,1,0:T(8,128)(2,1)} %bitcast.40), custom_call_target="tpu_custom_call" | custom-call | tf_op jit(solution)/shard_map/project/pallas_call | solution.py:177
  106.5 12.9 %all-to-all-start.2 = ((bf16[4,512,256]{2,1,0:T(8,128)(2,1)}), bf16[4,512,256]{2,1,0:T(8,128)(2,1)}, u32[]{:S(2)}, u32[]{:S(2)}) async-start(bf16[4,512,256]{2,1,0:T(8,128)(2,1)} %project.1), calls=%async_computation.2 | async-start | bytes 2097152 | tf_op jit(solution)/shard_map/all_to_all | solution.py:401
  124.3 2.3 %collective-permute-start.9 = (bf16[512,256]{1,0:T(8,128)(2,1)S(1)}, bf16[512,256]{1,0:T(8,128)(2,1)S(1)}, u32[]{:S(2)}, u32[]{:S(2)}) collective-permute-start(bf16[512,256]{1,0:T(8,128)(2,1)S(1)} %get-tuple-element.61), channel_id=1, source_target_pairs={{0,1},{1,2},{2,3},{3,0},{4,5},{5,6},{6,7},{7,4},{8,9},{9,10},{10,1... | collective-permute-start | bytes 786440 | tf_op jit(solution)/shard_map/ppermute | solution.py:397
  126.5 3.4 %collective-permute-start.10 = (bf16[512,256]{1,0:T(8,128)(2,1)S(1)}, bf16[512,256]{1,0:T(8,128)(2,1)S(1)}, u32[]{:S(2)}, u32[]{:S(2)}) collective-permute-start(bf16[512,256]{1,0:T(8,128)(2,1)S(1)} %get-tuple-element.62), channel_id=1, source_target_pairs={{0,2},{1,3},{2,0},{3,1},{4,6},{5,7},{6,4},{7,5},{8,10},{9,11},{10,... | collective-permute-start | bytes 786440 | tf_op jit(solution)/shard_map/ppermute | solution.py:397
  129.9 2.8 %collective-permute-start.11 = (bf16[512,256]{1,0:T(8,128)(2,1)S(1)}, bf16[512,256]{1,0:T(8,128)(2,1)S(1)}, u32[]{:S(2)}, u32[]{:S(2)}) collective-permute-start(bf16[512,256]{1,0:T(8,128)(2,1)S(1)} %get-tuple-element.63), channel_id=1, source_target_pairs={{0,3},{1,0},{2,1},{3,2},{4,7},{5,4},{6,5},{7,6},{8,11},{9,8},{10,9... | collective-permute-start | bytes 786440 | tf_op jit(solution)/shard_map/ppermute | solution.py:397
  136.1 3.3 %collective-permute-done.10.refs_2_ = bf16[512,256]{1,0:T(8,128)(2,1)S(1)} collective-permute-done((bf16[512,256]{1,0:T(8,128)(2,1)S(1)}, bf16[512,256]{1,0:T(8,128)(2,1)S(1)}, u32[]{:S(2)}, u32[]{:S(2)}) %collective-permute-start.10) | collective-permute-done | bytes 262176 | tf_op jit(solution)/shard_map/ppermute | solution.py:397
  140.1 2.6 %collective-permute-done.11.refs_3_ = bf16[512,256]{1,0:T(8,128)(2,1)S(1)} collective-permute-done((bf16[512,256]{1,0:T(8,128)(2,1)S(1)}, bf16[512,256]{1,0:T(8,128)(2,1)S(1)}, u32[]{:S(2)}, u32[]{:S(2)}) %collective-permute-start.11) | collective-permute-done | bytes 262176 | tf_op jit(solution)/shard_map/ppermute | solution.py:397
  146.3 11.6 %all_to_all.25.keys_any = bf16[4,512,128]{2,1,0:T(8,128)(2,1)S(1)} all-to-all(bf16[4,512,128]{2,1,0:T(8,128)(2,1)S(1)} %reduce_keys.1), channel_id=1, replica_groups=mesh['x'=4,'zh'=4,'c'=2,'zl'=4,'y'=4] {'y'}, dimensions={0} | all-to-all | bytes 1048576 | tf_op jit(solution)/shard_map/all_to_all | solution.py:401
  157.9 5.1 %attend.1 = bf16[16,128,128]{2,1,0:T(8,128)(2,1)S(1)} custom-call(s32[4]{0:T(128)S(1)} %copy-done.23, bf16[4,512,128]{2,1,0:T(8,128)(2,1)S(1)} %all_to_all.25.keys_any, bf16[512,256]{1,0:T(8,128)(2,1)S(1)} %copy-done.9, bf16[512,256]{1,0:T(8,128)(2,1)S(1)} %copy-done.11, bf16[512,256]{1,0:T(8,128)(2,1)S(1)} %copy-done.13, bf16[512,256]{1,0:T(8,128)(2,1)S(1)} %copy-done.15), custom_call_target="tpu_custom_call" | custom-call | tf_op jit(solution)/shard_map/attend/pallas_call | solution.py:337
  163.0 17.7 %all_to_all.26.mixed_any = bf16[16,128,128]{2,1,0:T(8,128)(2,1)S(1)} all-to-all(bf16[16,128,128]{2,1,0:T(8,128)(2,1)S(1)} %attend.1), channel_id=1, replica_groups=mesh['x'=4,'zh'=4,'c'=2,'zl'=4,'y'=4] {'zl','y'}, dimensions={0} | all-to-all | bytes 1048576 | tf_op jit(solution)/shard_map/all_to_all | solution.py:401
  (92 shorter events, 27.3 us)
Async XLA Ops:
  7.2 78.0 %all-gather.2.cloned.1.call-start = ((), (), s32[]{:S(2)}) async-start(), calls=%async_computation.5 | async-start | bytes 2949120 | tf_op jit(solution)/shard_map/all_gather | solution.py:409
  10.5 23.8 %all-to-all-start = ((bf16[8,288,128]{2,1,0:T(8,128)(2,1)}), bf16[8,288,128]{2,1,0:T(8,128)(2,1)S(1)}, u32[]{:S(2)}, u32[]{:S(2)}) async-start(bf16[8,288,128]{2,1,0:T(8,128)(2,1)} %get-tuple-element.36.delta_ref), calls=%async_computation | async-start | bytes 1179648 | tf_op jit(solution)/shard_map/all_to_all | solution.py:401
  21.9 12.3 %collective-permute-start = (bf16[128,1152]{1,0:T(8,128)(2,1)}, bf16[128,1152]{1,0:T(8,128)(2,1)S(1)}, u32[]{:S(2)}, u32[]{:S(2)}) collective-permute-start(bf16[128,1152]{1,0:T(8,128)(2,1)} %get-tuple-element.72), channel_id=1, source_target_pairs={{0,4},{4,8},{8,12},{12,0},{1,5},{5,9},{9,13},{13,1},{2,6},{6,10},{... | collective-permute-start | bytes 884744 | tf_op jit(solution)/shard_map/ppermute | solution.py:390
  24.6 39.4 %copy-start.2 = (bf16[288,1024]{1,0:T(8,128)(2,1)S(1)}, bf16[288,1024]{1,0:T(8,128)(2,1)}, u32[]{:S(2)}) copy-start(bf16[288,1024]{1,0:T(8,128)(2,1)} %base_ref.3) | copy-start | bytes 1769476
  24.6 39.4 %copy-start.7 = (bf16[288,1024]{1,0:T(8,128)(2,1)S(1)}, bf16[288,1024]{1,0:T(8,128)(2,1)}, u32[]{:S(2)}) copy-start(bf16[288,1024]{1,0:T(8,128)(2,1)} %momentum_ref.1) | copy-start | bytes 1769476
  25.3 36.0 %collective-permute-start.5 = (bf16[128,768]{1,0:T(8,128)(2,1)}, bf16[128,768]{1,0:T(8,128)(2,1)S(1)}, u32[]{:S(2)}, u32[]{:S(2)}) collective-permute-start(bf16[128,768]{1,0:T(8,128)(2,1)} %pad_maximum_fusion), channel_id=1, source_target_pairs={{0,4},{4,8},{8,12},{12,0},{1,5},{5,9},{9,13},{13,1},{2,6},{6,10},{... | collective-permute-start | bytes 589832 | tf_op jit(solution)/shard_map/ppermute | solution.py:390
  27.3 27.7 %collective-permute-start.2 = (bf16[128,1152]{1,0:T(8,128)(2,1)}, bf16[128,1152]{1,0:T(8,128)(2,1)S(1)}, u32[]{:S(2)}, u32[]{:S(2)}) collective-permute-start(bf16[128,1152]{1,0:T(8,128)(2,1)} %get-tuple-element.71), channel_id=1, source_target_pairs={{0,8},{4,12},{8,0},{12,4},{1,9},{5,13},{9,1},{13,5},{2,10},{6,14},... | collective-permute-start | bytes 884744 | tf_op jit(solution)/shard_map/ppermute | solution.py:390
  34.3 31.5 %copy-start.26 = (bf16[128,1152]{1,0:T(8,128)(2,1)}, bf16[128,1152]{1,0:T(8,128)(2,1)S(1)}, u32[]{:S(2)}) copy-start(bf16[128,1152]{1,0:T(8,128)(2,1)S(1)} %collective-permute-done.refs_1_) | copy-start | bytes 884740
  34.4 12.4 %collective-permute-start.1 = (bf16[288,128]{1,0:T(8,128)(2,1)S(1)}, bf16[288,128]{1,0:T(8,128)(2,1)S(1)}, u32[]{:S(2)}, u32[]{:S(2)}) collective-permute-start(bf16[288,128]{1,0:T(8,128)(2,1)S(1)} %reduce_sum.12), channel_id=1, source_target_pairs={{0,32},{64,96},{32,0},{96,64},{1,33},{65,97},{33,1},{97,65},{2,34}... | collective-permute-start | bytes 221192 | tf_op jit(solution)/shard_map/ppermute | solution.py:372
  41.7 19.7 %collective-permute-start.6 = (bf16[128,768]{1,0:T(8,128)(2,1)}, bf16[128,768]{1,0:T(8,128)(2,1)S(1)}, u32[]{:S(2)}, u32[]{:S(2)}) collective-permute-start(bf16[128,768]{1,0:T(8,128)(2,1)} %pad_maximum_fusion.1), channel_id=1, source_target_pairs={{0,12},{4,0},{8,4},{12,8},{1,13},{5,1},{9,5},{13,9},{2,14},{6,2},{... | collective-permute-start | bytes 589832 | tf_op jit(solution)/shard_map/ppermute | solution.py:390
  44.8 16.8 %collective-permute-start.4 = (bf16[128,1152]{1,0:T(8,128)(2,1)S(1)}, bf16[128,1152]{1,0:T(8,128)(2,1)S(1)}, u32[]{:S(2)}, u32[]{:S(2)}) collective-permute-start(bf16[128,1152]{1,0:T(8,128)(2,1)S(1)} %get-tuple-element.73), channel_id=1, source_target_pairs={{0,12},{4,0},{8,4},{12,8},{1,13},{5,1},{9,5},{13,9},{2,14},{6,2},{... | collective-permute-start | bytes 884744 | tf_op jit(solution)/shard_map/ppermute | solution.py:390
  54.9 9.1 %collective-permute-start.3 = (bf16[288,128]{1,0:T(8,128)(2,1)S(1)}, bf16[288,128]{1,0:T(8,128)(2,1)S(1)}, u32[]{:S(2)}, u32[]{:S(2)}) collective-permute-start(bf16[288,128]{1,0:T(8,128)(2,1)S(1)} %add_convert_fusion.mine_ref), channel_id=1, source_target_pairs={{32,64},{96,0},{64,32},{0,96},{33,65},{97,1},{65,33},{1,97},{34,66... | collective-permute-start | bytes 221192 | tf_op jit(solution)/shard_map/ppermute | solution.py:372
  65.9 25.5 %all-to-all-start.1 = ((bf16[16,288,128]{2,1,0:T(8,128)(2,1)}), bf16[16,288,128]{2,1,0:T(8,128)(2,1)S(1)}, u32[]{:S(2)}, u32[]{:S(2)}) async-start(bf16[16,288,128]{2,1,0:T(8,128)(2,1)} %outer_step.1), calls=%async_computation.1 | async-start | bytes 2359296 | tf_op jit(solution)/shard_map/all_to_all | solution.py:401
  72.6 18.2 %collective-permute-start.7 = (bf16[128,768]{1,0:T(8,128)(2,1)S(1)}, bf16[128,768]{1,0:T(8,128)(2,1)S(1)}, u32[]{:S(2)}, u32[]{:S(2)}) collective-permute-start(bf16[128,768]{1,0:T(8,128)(2,1)S(1)} %pad_maximum_fusion.3), channel_id=1, source_target_pairs={{0,8},{4,12},{8,0},{12,4},{1,9},{5,13},{9,1},{13,5},{2,10},{6,14},... | collective-permute-start | bytes 589832 | tf_op jit(solution)/shard_map/ppermute | solution.py:390
  91.4 6.0 %collective-permute-start.8 = (bf16[16,288,128]{2,1,0:T(8,128)(2,1)S(1)}, bf16[16,288,128]{2,1,0:T(8,128)(2,1)S(1)}, u32[]{:S(2)}, u32[]{:S(2)}) collective-permute-start(bf16[16,288,128]{2,1,0:T(8,128)(2,1)S(1)} %all-to-all-done.1), channel_id=1, source_target_pairs={{0,16},{16,0},{1,17},{17,1},{2,18},{18,2},{3,19},{19,3},{4,20},{20... | collective-permute-start | bytes 3538952 | tf_op jit(solution)/shard_map/ppermute | solution.py:427
  98.5 20.9 %copy-start.23 = (s32[4]{0:T(128)S(1)}, s32[4]{0:T(128)}, u32[]{:S(2)}) copy-start(s32[4]{0:T(128)} %copy-done.22) | copy-start | bytes 52
  98.5 34.3 %copy-start.5 = (bf16[8,288,128]{2,1,0:T(8,128)(2,1)S(1)}, bf16[8,288,128]{2,1,0:T(8,128)(2,1)}, u32[]{:S(2)}) copy-start(bf16[8,288,128]{2,1,0:T(8,128)(2,1)} %get-tuple-element.36.delta_ref) | copy-start | bytes 1769476
  106.5 26.3 %copy-start.1 = (bf16[16,288,128]{2,1,0:T(8,128)(2,1)S(1)}, bf16[16,288,128]{2,1,0:T(8,128)(2,1)}, u32[]{:S(2)}) copy-start(bf16[16,288,128]{2,1,0:T(8,128)(2,1)} %copy-done) | copy-start | bytes 3538948
  106.5 26.3 %copy-start.4 = (bf16[16,288,128]{2,1,0:T(8,128)(2,1)S(1)}, bf16[16,288,128]{2,1,0:T(8,128)(2,1)}, u32[]{:S(2)}) copy-start(bf16[16,288,128]{2,1,0:T(8,128)(2,1)} %copy-done.3) | copy-start | bytes 3538948
  106.5 38.3 %all-to-all-start.2 = ((bf16[4,512,256]{2,1,0:T(8,128)(2,1)}), bf16[4,512,256]{2,1,0:T(8,128)(2,1)}, u32[]{:S(2)}, u32[]{:S(2)}) async-start(bf16[4,512,256]{2,1,0:T(8,128)(2,1)} %project.1), calls=%async_computation.2 | async-start | bytes 2097152 | tf_op jit(solution)/shard_map/all_to_all | solution.py:401
  124.3 11.1 %collective-permute-start.9 = (bf16[512,256]{1,0:T(8,128)(2,1)S(1)}, bf16[512,256]{1,0:T(8,128)(2,1)S(1)}, u32[]{:S(2)}, u32[]{:S(2)}) collective-permute-start(bf16[512,256]{1,0:T(8,128)(2,1)S(1)} %get-tuple-element.61), channel_id=1, source_target_pairs={{0,1},{1,2},{2,3},{3,0},{4,5},{5,6},{6,7},{7,4},{8,9},{9,10},{10,1... | collective-permute-start | bytes 786440 | tf_op jit(solution)/shard_map/ppermute | solution.py:397
  126.5 12.8 %collective-permute-start.10 = (bf16[512,256]{1,0:T(8,128)(2,1)S(1)}, bf16[512,256]{1,0:T(8,128)(2,1)S(1)}, u32[]{:S(2)}, u32[]{:S(2)}) collective-permute-start(bf16[512,256]{1,0:T(8,128)(2,1)S(1)} %get-tuple-element.62), channel_id=1, source_target_pairs={{0,2},{1,3},{2,0},{3,1},{4,6},{5,7},{6,4},{7,5},{8,10},{9,11},{10,... | collective-permute-start | bytes 786440 | tf_op jit(solution)/shard_map/ppermute | solution.py:397
  129.9 12.8 %collective-permute-start.11 = (bf16[512,256]{1,0:T(8,128)(2,1)S(1)}, bf16[512,256]{1,0:T(8,128)(2,1)S(1)}, u32[]{:S(2)}, u32[]{:S(2)}) collective-permute-start(bf16[512,256]{1,0:T(8,128)(2,1)S(1)} %get-tuple-element.63), channel_id=1, source_target_pairs={{0,3},{1,0},{2,1},{3,2},{4,7},{5,4},{6,5},{7,6},{8,11},{9,8},{10,9... | collective-permute-start | bytes 786440 | tf_op jit(solution)/shard_map/ppermute | solution.py:397
  144.8 13.1 %copy-start.15 = (bf16[512,256]{1,0:T(8,128)(2,1)S(1)}, bf16[512,256]{1,0:T(8,128)(2,1)}, u32[]{:S(2)}) copy-start(bf16[512,256]{1,0:T(8,128)(2,1)} %copy-done.14) | copy-start | bytes 786436
  (23 other events, 115.4 us)
Sparse Core Ops, SparseCore 0:
  10.7 46.0 all-gather.1
